TPU v7x, 512 devices: a whole 4x4x16 slice. The times are simulated.
512 devices in a mesh: lon: 64 (over x_hi, z, core), lat: 8 (over y, x_lo).
Axes of the slice: x: 4 (x_hi: 2, x_lo: 2; x = x_hi * 2 + x_lo), y: 4, z: 16, core: 2. Of those that a mesh axis runs over, the one named last changes fastest.
Arguments:
- tokens: bfloat16 [128, 512, 1024], P('lat', 'lon'), may hold values from -6 to 6
- labels: int32 [128, 512], P('lat', 'lon'), may hold values from 0 to 3
- w_qkv: bfloat16 [1024, 1536], replicated, may hold values from -0.1875 to 0.1875
- w_proj: bfloat16 [512, 1024], replicated, may hold values from -0.25 to 0.25
- logit_scale: float32 [16], replicated, may hold values from 0 to 2
- bias_table: float32 [16, 225], replicated, may hold values from -6 to 6
- norm_gain: float32 [1024], replicated, may hold values from 0.1 to 1.9
- norm_shift: float32 [1024], replicated, may hold values from -3 to 3
- merge_gain: float32 [4096], replicated, may hold values from 0.1 to 1.9
- cotangent: bfloat16 [64, 256, 4096], P('lat', 'lon'), may hold values from -6 to 6
Outputs:
- d_tokens: bfloat16 [128, 512, 1024], P('lat', 'lon')
All inputs are finite; a program needn't handle non-finite values.
Results may differ from a plain program's by a relative error of at most 0.0065.
Values may be sent and summed in bfloat16 or wider, within the bound.
No kernel may reach another device: no remote copies, remote signals or barrier semaphores. Data moves between devices by JAX's collectives and lax.ppermute only.
A program may use at most 64 MiB of HBM per device.

v0:
```python
import math

import jax
import jax.numpy as jnp
from jax import lax
from jax.sharding import PartitionSpec as P

WIN = 8


norm_eps = 1e-05
unit_eps = 1e-06
highest = lax.Precision.HIGHEST


def passed_along(block, axis, distance):
    devices = range(lax.axis_size(axis))
    route = [((i - distance) % len(devices), i) for i in devices]
    return lax.ppermute(block, axis, route)


def to_windows(array):
    row_count, col_count, feature = array.shape
    blocks = array.reshape(row_count // WIN, WIN, col_count // WIN, WIN, feature)
    return blocks.transpose(0, 2, 1, 3, 4).reshape(-1, WIN * WIN, feature)


def from_windows(array, row_count, col_count):
    feature = array.shape[-1]
    blocks = array.reshape(row_count // WIN, col_count // WIN, WIN, WIN, feature)
    return blocks.transpose(0, 2, 1, 3, 4).reshape(row_count, col_count, feature)


def relative_bias(bias_table):
    spread = 2 * WIN - 1
    cell_ids = jnp.arange(WIN * WIN, dtype=jnp.int32)
    row_in = cell_ids // WIN
    col_in = cell_ids % WIN
    offset = (row_in[:, None] - row_in[None, :] + WIN - 1) * spread + (
        col_in[:, None] - col_in[None, :] + WIN - 1
    )
    onehot = (offset[:, :, None] == jnp.arange(spread * spread, dtype=jnp.int32)).astype(
        jnp.float32
    )
    raw_bias = jnp.einsum("ijr,hr->hij", onehot, bias_table, precision=highest)
    return 16.0 * jax.nn.sigmoid(raw_bias)


def window_mask(labels, wrapped):
    label_win = to_windows(labels[:, :, None])[:, :, 0]
    wrap_win = to_windows(wrapped[:, :, None])[:, :, 0]
    same_label = label_win[:, :, None] == label_win[:, None, :]
    same_side = wrap_win[:, :, None] == wrap_win[:, None, :]
    return same_label & same_side


def attend_forward(packed, allowed, temper, rel_bias):
    win_count = packed.shape[0]
    head_count = rel_bias.shape[0]
    att_width = packed.shape[-1] // 3
    split_heads = packed.reshape(win_count, WIN * WIN, 3, head_count, att_width // head_count)
    queries = split_heads[:, :, 0].astype(jnp.float32)
    key_heads = split_heads[:, :, 1].astype(jnp.float32)
    val_heads = split_heads[:, :, 2]
    query_inv = lax.rsqrt(jnp.sum(queries * queries, -1, keepdims=True) + unit_eps)
    key_inv = lax.rsqrt(jnp.sum(key_heads * key_heads, -1, keepdims=True) + unit_eps)
    query_unit = queries * query_inv
    key_unit = key_heads * key_inv
    cosine = jnp.einsum("nihd,njhd->nhij", query_unit, key_unit, precision=highest)
    scores = cosine * temper[None, :, None, None] + rel_bias[None]
    mask_gate = allowed[:, None]
    row_max = jnp.max(jnp.where(mask_gate, scores, -jnp.inf), -1, keepdims=True)
    exponent = jnp.where(mask_gate, jnp.exp(scores - row_max), 0.0)
    attn_prob = exponent / jnp.sum(exponent, -1, keepdims=True)
    weights = attn_prob.astype(jnp.bfloat16)
    attended = jnp.einsum("nhij,njhd->nihd", weights, val_heads, preferred_element_type=jnp.float32)
    attended = attended.reshape(win_count, WIN * WIN, att_width).astype(jnp.bfloat16)
    return (attended, (query_unit, key_unit, query_inv, key_inv, attn_prob, weights, val_heads))


def attend_backward(grad_out, stored, temper):
    query_unit, key_unit, query_inv, key_inv, attn_prob, weights, val_heads = stored
    win_count, cell_count, head_count, head_width = query_unit.shape
    grad_heads = grad_out.reshape(win_count, cell_count, head_count, head_width)
    grad_prob = jnp.einsum(
        "nihd,njhd->nhij", grad_heads, val_heads, preferred_element_type=jnp.float32
    )
    grad_val = jnp.einsum(
        "nhij,nihd->njhd", weights, grad_heads, preferred_element_type=jnp.float32
    )
    grad_score = attn_prob * (grad_prob - jnp.sum(attn_prob * grad_prob, -1, keepdims=True))
    grad_cos = grad_score * temper[None, :, None, None]
    grad_qunit = jnp.einsum("nhij,njhd->nihd", grad_cos, key_unit, precision=highest)
    grad_kunit = jnp.einsum("nhij,nihd->njhd", grad_cos, query_unit, precision=highest)
    grad_query = query_inv * (
        grad_qunit - query_unit * jnp.sum(query_unit * grad_qunit, -1, keepdims=True)
    )
    grad_key = key_inv * (grad_kunit - key_unit * jnp.sum(key_unit * grad_kunit, -1, keepdims=True))
    stacked = jnp.stack([grad_query, grad_key, grad_val], 2)
    return stacked.reshape(win_count, cell_count, -1).astype(jnp.bfloat16)


def merge_tokens(mixed):
    row_count, col_count, width_d = mixed.shape
    grouped = mixed.reshape(row_count // 2, 2, col_count // 2, 2, width_d)
    return grouped.transpose(0, 2, 3, 1, 4).reshape(row_count // 2, col_count // 2, 4 * width_d)


def split_tokens(merged, width_d):
    row_half, col_half, fourfold = merged.shape
    grouped = merged.reshape(row_half, col_half, 2, 2, width_d)
    return grouped.transpose(0, 3, 1, 2, 4).reshape(row_half * 2, col_half * 2, width_d)


def token_backward(attended, rolled, cot, w_proj, norm_gain, norm_shift, merge_gain):
    row_count, col_count, att_width = attended.shape
    width_d = w_proj.shape[1]
    projected = jnp.dot(attended.reshape(-1, att_width), w_proj, preferred_element_type=jnp.float32)
    centered = projected - jnp.mean(projected, -1, keepdims=True)
    inv_std = lax.rsqrt(jnp.mean(centered * centered, -1, keepdims=True) + norm_eps)
    normed = centered * inv_std
    mixed = rolled.reshape(-1, width_d).astype(jnp.float32) + normed * norm_gain + norm_shift
    merged = merge_tokens(mixed.reshape(row_count, col_count, width_d))
    merge_cent = merged - jnp.mean(merged, -1, keepdims=True)
    merge_inv = lax.rsqrt(jnp.mean(merge_cent * merge_cent, -1, keepdims=True) + norm_eps)
    merge_hat = merge_cent * merge_inv
    grad_hat = cot.astype(jnp.float32) * merge_gain
    grad_merged = merge_inv * (
        grad_hat
        - jnp.mean(grad_hat, -1, keepdims=True)
        - merge_hat * jnp.mean(grad_hat * merge_hat, -1, keepdims=True)
    )
    grad_mixed = split_tokens(grad_merged, width_d).reshape(-1, width_d)
    grad_norm = grad_mixed * norm_gain
    grad_proj = inv_std * (
        grad_norm
        - jnp.mean(grad_norm, -1, keepdims=True)
        - normed * jnp.mean(grad_norm * normed, -1, keepdims=True)
    )
    grad_proj = grad_proj.astype(jnp.bfloat16)
    grad_att = lax.dot_general(
        grad_proj, w_proj, (((1,), (1,)), ((), ())), preferred_element_type=jnp.float32
    )
    grad_att = grad_att.astype(jnp.bfloat16)
    return (
        grad_att.reshape(row_count, col_count, att_width),
        grad_mixed.reshape(row_count, col_count, width_d),
    )


def finish_grad(grad_mixed, grad_packed, w_qkv):
    row_count, col_count, width_d = grad_mixed.shape
    flat_packed = grad_packed.reshape(row_count * col_count, -1)
    through = lax.dot_general(
        flat_packed, w_qkv, (((1,), (1,)), ((), ())), preferred_element_type=jnp.float32
    )
    total = grad_mixed.reshape(-1, width_d) + through
    return total.astype(jnp.bfloat16).reshape(row_count, col_count, width_d)


def move_pair(values, labels, strip_width):
    arrived = passed_along((values[:, :strip_width], labels[:, :strip_width]), "lon", -1)
    values = jnp.concatenate([values[:, strip_width:], arrived[0]], axis=1)
    labels = jnp.concatenate([labels[:, strip_width:], arrived[1]], axis=1)
    below = passed_along((values[:strip_width], labels[:strip_width]), "lat", -1)
    values = jnp.concatenate([values[strip_width:], below[0]], axis=0)
    labels = jnp.concatenate([labels[strip_width:], below[1]], axis=0)
    return (values, labels)


def move_one(values, strip_width, direction):
    row_count = values.shape[0]
    col_count = values.shape[1]
    col_strip = values[:, :strip_width] if direction < 0 else values[:, col_count - strip_width :]
    arrived = passed_along(col_strip, "lon", direction)
    if direction < 0:
        values = jnp.concatenate([values[:, strip_width:], arrived], axis=1)
    else:
        values = jnp.concatenate([arrived, values[:, : col_count - strip_width]], axis=1)
    row_strip = values[:strip_width] if direction < 0 else values[row_count - strip_width :]
    below = passed_along(row_strip, "lat", direction)
    if direction < 0:
        values = jnp.concatenate([values[strip_width:], below], axis=0)
    else:
        values = jnp.concatenate([below, values[: row_count - strip_width]], axis=0)
    return values


def shards(
    tokens,
    labels,
    w_qkv,
    w_proj,
    logit_scale,
    bias_table,
    norm_gain,
    norm_shift,
    merge_gain,
    cotangent,
):
    half_win = WIN // 2
    row_count, col_count, width_d = tokens.shape
    temper = jnp.exp(jnp.minimum(logit_scale, math.log(100.0)))
    rel_bias = relative_bias(bias_table)
    last_lat = lax.axis_index("lat") == lax.axis_size("lat") - 1
    row_ids = lax.broadcasted_iota(jnp.int32, (row_count, col_count), 0)
    wrapped = (last_lat & (row_ids >= row_count - half_win)).astype(jnp.int32)
    packed = jnp.dot(tokens.reshape(-1, width_d), w_qkv, preferred_element_type=jnp.float32)
    packed = packed.astype(jnp.bfloat16).reshape(row_count, col_count, -1)
    packed_region, labels_region = move_pair(packed, labels, half_win)
    allowed = window_mask(labels_region, wrapped)
    attended, stored = attend_forward(to_windows(packed_region), allowed, temper, rel_bias)
    attended_tile = move_one(from_windows(attended, row_count, col_count), half_win, 1)
    grad_att, grad_mixed = token_backward(
        attended_tile, tokens, cotangent, w_proj, norm_gain, norm_shift, merge_gain
    )
    grad_region = move_one(grad_att, half_win, -1)
    grad_packed = from_windows(
        attend_backward(to_windows(grad_region), stored, temper), row_count, col_count
    )
    grad_tile = move_one(grad_packed, half_win, 1)
    return finish_grad(grad_mixed, grad_tile, w_qkv)


def solution(mesh):
    placed = (
        P("lat", "lon", None),
        P("lat", "lon"),
        P(),
        P(),
        P(),
        P(),
        P(),
        P(),
        P(),
        P("lat", "lon", None),
    )
    return jax.shard_map(
        shards, mesh=mesh, in_specs=placed, out_specs=P("lat", "lon", None), check_vma=False
    )
```

profile of v0, /device:TPU:4, one launch (start us, length us, event | category | flops | bytes accessed | tf_op | source)
XLA Modules:
  0.0 159.2 jit_solution(14619628437761644565)
XLA Ops:
  0.0 1.9 %copy-done = bf16[1024,1536]{1,0:T(8,128)(2,1)S(1)} copy-done((bf16[1024,1536]{1,0:T(8,128)(2,1)S(1)}, bf16[1024,1536]{1,0:T(8,128)(2,1)}, u32[]{:S(2)}) %copy-start) | copy-done | bytes 3145752
  1.9 1.5 fusion.4
  3.4 0.8 fusion.89
  4.2 10.8 %collective-permute-start = (bf16[16,4,1536]{2,1,0:T(4,128)(2,1)}, bf16[16,4,1536]{2,1,0:T(4,128)(2,1)S(1)}, u32[]{:S(2)}, u32[]{:S(2)}) collective-permute-start(bf16[16,4,1536]{2,1,0:T(4,128)(2,1)} %get-tuple-element.13), channel_id=1, source_target_pairs={{8,0},{16,8},{24,16},{32,24},{40,32},{48,40},{56,48},{64,56},{72,6... | collective-permute-start | bytes 589832 | tf_op jit(solution)/shard_map/ppermute | solution.py:19
  15.0 0.6 fusion.92
  15.6 2.6 %collective-permute-start.2 = (s32[16,4]{0,1:T(4,128)}, s32[16,4]{0,1:T(4,128)S(1)}, u32[]{:S(2)}, u32[]{:S(2)}) collective-permute-start(s32[16,4]{0,1:T(4,128)} %get-tuple-element.19), channel_id=1, source_target_pairs={{8,0},{16,8},{24,16},{32,24},{40,32},{48,40},{56,48},{64,56},{72,6... | collective-permute-start | bytes 776 | tf_op jit(solution)/shard_map/ppermute | solution.py:19
  18.8 4.7 %fusion.20 = f32[16,64,64]{2,0,1:T(8,128)} fusion(s32[64,64]{1,0:T(8,128)S(1)} %add_add_fusion.1, f32[16,225]{1,0:T(8,128)} %param.15), kind=kOutput, calls=%fused_computation.23 | convolution fusion | flops 178130944 | bytes 292928 | tf_op jit(solution)/shard_map/ijr,hr->hij/dot_general | solution.py:45
  23.5 0.6 and_convert_fusion
  24.1 2.1 %copy.23 = f32[16,64,64]{1,2,0:T(8,128)} copy(f32[16,64,64]{2,0,1:T(8,128)} %fusion.20) | data formatting | bytes 524288 | tf_op jit(solution)/shard_map/mul | solution.py:46
  26.2 6.5 %collective-permute-start.3 = (s32[4,8]{0,1:T(8,128)S(1)}, s32[4,8]{0,1:T(8,128)S(1)}, u32[]{:S(2)}, u32[]{:S(2)}) collective-permute-start(s32[4,8]{0,1:T(8,128)S(1)} %bitcast.97), channel_id=1, source_target_pairs={{1,0},{2,1},{3,2},{4,3},{5,4},{6,5},{7,6},{0,7},{9,8},{10,9},{11,1... | collective-permute-start | bytes 392 | tf_op jit(solution)/shard_map/ppermute | solution.py:19
  32.7 0.7 iota.37
  33.4 0.7 convert_element_type.67
  34.3 0.7 eq.54
  34.9 0.9 compare_and_fusion
  35.9 6.1 %collective-permute-start.1 = (bf16[4,8,1536]{2,1,0:T(8,128)(2,1)S(1)}, bf16[4,8,1536]{2,1,0:T(8,128)(2,1)S(1)}, u32[]{:S(2)}, u32[]{:S(2)}) collective-permute-start(bf16[4,8,1536]{2,1,0:T(8,128)(2,1)S(1)} %pad_maximum_fusion.6), channel_id=1, source_target_pairs={{1,0},{2,1},{3,2},{4,3},{5,4},{6,5},{7,6},{0,7},{9,8},{10,9},{11,1... | collective-permute-start | bytes 294920 | tf_op jit(solution)/shard_map/ppermute | solution.py:19
  42.2 2.0 %collective-permute-done.1 = bf16[4,8,1536]{2,1,0:T(8,128)(2,1)S(1)} collective-permute-done((bf16[4,8,1536]{2,1,0:T(8,128)(2,1)S(1)}, bf16[4,8,1536]{2,1,0:T(8,128)(2,1)S(1)}, u32[]{:S(2)}, u32[]{:S(2)}) %collective-permute-start.1) | collective-permute-done | bytes 98336 | tf_op jit(solution)/shard_map/ppermute | solution.py:19
  44.2 2.2 %reshape_reshape_transpose_reshape.6 = bf16[2,64,3,16,32]{4,3,2,1,0:T(8,128)(2,1)} reshape(bf16[16,8,1536]{2,1,0:T(8,128)(2,1)S(1)} %pad_maximum_fusion.2) | data formatting | bytes 786432 | tf_op jit(solution)/shard_map/reshape;reshape;transpose;reshape | solution.py:61
  46.4 2.6 %fusion.87 = (bf16[2,64,1,16,32]{4,3,2,1,0:T(8,128)(2,1)}, bf16[2,64,1,16,32]{4,3,2,1,0:T(8,128)(2,1)}, bf16[2,64,1,16,32]{4,3,2,1,0:T(8,128)(2,1)}) fusion(bf16[2,64,3,16,32]{4,3,2,1,0:T(8,128)(2,1)} %reshape_reshape_transpose_reshape.6), kind=kLoop, calls=%fused_computation.143 | loop fusion | bytes 786432 | tf_op jit(solution)/shard_map/slice | solution.py:62
  49.0 1.5 copy.39
  50.6 0.6 copy-done.2
  51.2 1.5 copy.40
  52.7 2.2 %copy.38 = bf16[2,64,1,16,32]{1,4,3,0,2:T(8,128)(2,1)} copy(bf16[2,64,1,16,32]{4,3,2,1,0:T(8,128)(2,1)} %get-tuple-element.8) | data formatting | bytes 262144
  54.9 3.0 %fusion.14 = f32[2,16,64,64]{2,3,1,0:T(8,128)S(1)} fusion(f32[16,64,64]{1,2,0:T(8,128)} %copy.23, f32[16]{0:T(128)S(1)} %copy-done.14, bf16[2,64,1,16,32]{1,4,3,0,2:T(8,128)(2,1)S(1)} %copy.40, bf16[2,64,1,16,32]{1,4,3,0,2:T(8,128)(2,1)} %copy-done.2, f32[2,64,16]{1,2,0:T(8,128)S(1)} %get-tuple-element.28, f32[2,64,16]{1,2,0:T(8,128)S(1)} %get-tuple-element.29), kind=kOutput, calls=%fused_computation.14 | convolution fusion | flops 50855936 | bytes 1065024 | tf_op jit(solution)/shard_map/nihd,njhd->nhij/dot_general | solution.py:69
  58.4 1.0 copy-done.17
  59.4 1.0 fusion.30
  60.3 2.2 %copy.25 = bf16[2,64,16,32]{3,2,1,0:T(8,128)(2,1)} copy(bf16[2,64,16,32]{1,3,2,0:T(8,128)(2,1)} %fusion.30) | data formatting | bytes 262144 | tf_op jit(solution)/shard_map/convert_element_type | solution.py:77
  62.5 1.5 convert_element_type.75
  64.1 1.9 %collective-permute-start.4 = (bf16[16,4,512]{2,1,0:T(4,128)(2,1)S(1)}, bf16[16,4,512]{2,1,0:T(4,128)(2,1)S(1)}, u32[]{:S(2)}, u32[]{:S(2)}) collective-permute-start(bf16[16,4,512]{2,1,0:T(4,128)(2,1)S(1)} %get-tuple-element.16), channel_id=1, source_target_pairs={{504,0},{0,8},{8,16},{16,24},{24,32},{32,40},{40,48},{48,56},{56,6... | collective-permute-start | bytes 196616 | tf_op jit(solution)/shard_map/ppermute | solution.py:19
  66.0 7.3 %collective-permute-done.4 = bf16[16,4,512]{2,1,0:T(4,128)(2,1)S(1)} collective-permute-done((bf16[16,4,512]{2,1,0:T(4,128)(2,1)S(1)}, bf16[16,4,512]{2,1,0:T(4,128)(2,1)S(1)}, u32[]{:S(2)}, u32[]{:S(2)}) %collective-permute-start.4) | collective-permute-done | bytes 65568 | tf_op jit(solution)/shard_map/ppermute | solution.py:19
  73.3 2.1 %collective-permute-start.5 = (bf16[4,8,512]{2,1,0:T(8,128)(2,1)S(1)}, bf16[4,8,512]{2,1,0:T(8,128)(2,1)S(1)}, u32[]{:S(2)}, u32[]{:S(2)}) collective-permute-start(bf16[4,8,512]{2,1,0:T(8,128)(2,1)S(1)} %pad_maximum_fusion.8), channel_id=1, source_target_pairs={{7,0},{0,1},{1,2},{2,3},{3,4},{4,5},{5,6},{6,7},{15,8},{8,9},{9,10... | collective-permute-start | bytes 98312 | tf_op jit(solution)/shard_map/ppermute | solution.py:19
  75.4 6.2 %collective-permute-done.5 = bf16[4,8,512]{2,1,0:T(8,128)(2,1)S(1)} collective-permute-done((bf16[4,8,512]{2,1,0:T(8,128)(2,1)S(1)}, bf16[4,8,512]{2,1,0:T(8,128)(2,1)S(1)}, u32[]{:S(2)}, u32[]{:S(2)}) %collective-permute-start.5) | collective-permute-done | bytes 32800 | tf_op jit(solution)/shard_map/ppermute | solution.py:19
  81.6 1.6 %fusion.94 = (f32[128]{0:T(128)S(1)}, f32[128,1024]{1,0:T(8,128)S(1)}) fusion(bf16[512,1024]{1,0:T(8,128)(2,1)} %param.13, bf16[16,4,512]{2,1,0:T(4,128)(2,1)S(1)} %get-tuple-element.17, bf16[16,4,512]{2,1,0:T(4,128)(2,1)S(1)} %collective-permute-done.4, bf16[4,8,512]{2,1,0:T(8,128)(2,1)S(1)} %collective-permute-done.5), kind=kOutput, calls=%fused_computation.150 | convolution fusion | flops 134741888 | bytes 1737216 | tf_op jit(solution)/shard_map/dot_general | solution.py:118
  83.4 0.6 copy-done.1
  84.0 1.9 %add_add_fusion = f32[128,1024]{1,0:T(8,128)} fusion(f32[128,1024]{1,0:T(8,128)S(1)} %get-tuple-element.23, bf16[16,8,1024]{2,1,0:T(8,128)(2,1)} %param.10, f32[1024]{0:T(1024)S(1)} %copy-done.12, f32[1024]{0:T(1024)S(1)} %copy-done.6, f32[128]{0:T(128)S(1)} %add_rsqrt_fusion.3, f32[128]{0:T(128)S(1)} %broadcast_multiply_fusion.5), kind=kLoop, calls=%fused_computation.65 | loop fusion | flops 786432 | bytes 1319936 | tf_op jit(solution)/shard_map/add | solution.py:122
  86.0 2.2 %reshape_reshape.4 = f32[8,2,4,2,1024]{4,3,2,1,0:T(2,128)} reshape(f32[128,1024]{1,0:T(8,128)} %add_add_fusion) | data formatting | bytes 1048576 | tf_op jit(solution)/shard_map/reshape;reshape | solution.py:105
  88.1 1.3 bitcast_reduce_fusion
  89.4 1.5 multiply_reduce_fusion.4
  90.9 2.3 %copy.26 = f32[8,4,2,2,1024]{4,3,2,1,0:T(2,128)} copy(f32[8,4,2,2,1024]{4,2,1,3,0:T(2,128)} %bitcast.95) | data formatting | bytes 1048576 | tf_op jit(solution)/shard_map/transpose | solution.py:106
  93.2 2.4 %reshape.240 = f32[8,4,4096]{2,1,0:T(4,128)} reshape(f32[8,4,2,2,1024]{4,3,2,1,0:T(2,128)} %copy.26) | data formatting | bytes 1048576 | tf_op jit(solution)/shard_map/reshape | solution.py:106
  95.6 1.5 fusion.44
  97.1 2.3 %subtract_multiply_fusion = f32[8,4,4096]{2,1,0:T(4,128)} fusion(bf16[8,4,4096]{2,1,0:T(4,128)(2,1)} %param.19, f32[8,4,4096]{2,1,0:T(4,128)} %reshape.240, f32[8,4]{1,0:T(8,128)S(1)} %broadcast_multiply_fusion.1, f32[8,4]{1,0:T(8,128)S(1)} %broadcast_multiply_fusion.3, f32[8,4]{1,0:T(8,128)S(1)} %broadcast_multiply_fusion.2, f32[4096]{0:T(1024)S(1)} %copy-done.7, ...), kind=kLoop, calls=%fused_computation.59 | loop fusion | flops 1048576 | bytes 1327616 | tf_op jit(solution)/shard_map/mul | solution.py:128
  99.4 2.4 %reshape.241 = f32[8,4,2,2,1024]{4,3,2,1,0:T(2,128)} reshape(f32[8,4,4096]{2,1,0:T(4,128)} %subtract_multiply_fusion) | data formatting | bytes 1048576 | tf_op jit(solution)/shard_map/reshape | solution.py:111
  101.8 2.2 %copy.44 = f32[8,4,2,2,1024]{4,2,1,3,0:T(2,128)} copy(f32[8,4,2,2,1024]{4,3,2,1,0:T(2,128)} %reshape.241) | data formatting | bytes 1048576 | tf_op jit(solution)/shard_map/reshape | solution.py:111
  103.9 1.4 multiply_reduce_fusion.2
  105.3 2.2 %reshape_reshape_reshape_reshape.3 = f32[128,1024]{1,0:T(8,128)} reshape(f32[8,2,4,2,1024]{4,3,2,1,0:T(2,128)} %bitcast.96) | data formatting | bytes 1048576 | tf_op jit(solution)/shard_map/reshape;reshape;reshape;reshape | solution.py:157
  107.5 1.4 multiply_reduce_fusion.1
  109.1 2.0 %fusion.35 = bf16[16,8,512]{2,1,0:T(8,128)(2,1)S(1)} fusion(bf16[512,1024]{1,0:T(8,128)(2,1)} %param.13, f32[128,1024]{1,0:T(8,128)} %reshape_reshape_reshape_reshape.3, f32[128,1024]{1,0:T(8,128)} %copy-done.1, f32[128]{0:T(128)S(1)} %broadcast_multiply_fusion.4, f32[128]{0:T(128)S(1)} %div.61, f32[1024]{0:T(1024)S(1)} %copy-done.6, ...), kind=kOutput, calls=%fused_computation.41 | convolution fusion | flops 135331840 | bytes 2234368 | tf_op jit(solution)/shard_map/dot_general | solution.py:141
  111.2 1.9 %collective-permute-start.6 = (bf16[16,4,512]{2,1,0:T(4,128)(2,1)S(1)}, bf16[16,4,512]{2,1,0:T(4,128)(2,1)S(1)}, u32[]{:S(2)}, u32[]{:S(2)}) collective-permute-start(bf16[16,4,512]{2,1,0:T(4,128)(2,1)S(1)} %get-tuple-element.15), channel_id=1, source_target_pairs={{8,0},{16,8},{24,16},{32,24},{40,32},{48,40},{56,48},{64,56},{72,6... | collective-permute-start | bytes 196616 | tf_op jit(solution)/shard_map/ppermute | solution.py:19
  113.1 1.9 %collective-permute-done.6 = bf16[16,4,512]{2,1,0:T(4,128)(2,1)S(1)} collective-permute-done((bf16[16,4,512]{2,1,0:T(4,128)(2,1)S(1)}, bf16[16,4,512]{2,1,0:T(4,128)(2,1)S(1)}, u32[]{:S(2)}, u32[]{:S(2)}) %collective-permute-start.6) | collective-permute-done | bytes 65568 | tf_op jit(solution)/shard_map/ppermute | solution.py:19
  115.0 4.1 %collective-permute-start.7 = (bf16[4,8,512]{2,1,0:T(8,128)(2,1)S(1)}, bf16[4,8,512]{2,1,0:T(8,128)(2,1)S(1)}, u32[]{:S(2)}, u32[]{:S(2)}) collective-permute-start(bf16[4,8,512]{2,1,0:T(8,128)(2,1)S(1)} %pad_maximum_fusion.7), channel_id=1, source_target_pairs={{1,0},{2,1},{3,2},{4,3},{5,4},{6,5},{7,6},{0,7},{9,8},{10,9},{11,1... | collective-permute-start | bytes 98312 | tf_op jit(solution)/shard_map/ppermute | solution.py:19
  119.2 1.6 %collective-permute-done.7 = bf16[4,8,512]{2,1,0:T(8,128)(2,1)S(1)} collective-permute-done((bf16[4,8,512]{2,1,0:T(8,128)(2,1)S(1)}, bf16[4,8,512]{2,1,0:T(8,128)(2,1)S(1)}, u32[]{:S(2)}, u32[]{:S(2)}) %collective-permute-start.7) | collective-permute-done | bytes 32800 | tf_op jit(solution)/shard_map/ppermute | solution.py:19
  120.9 1.1 reshape_reshape_transpose_reshape.7
  122.0 2.2 %copy.28 = bf16[2,64,16,32]{1,3,2,0:T(8,128)(2,1)} copy(bf16[2,64,16,32]{3,2,1,0:T(8,128)(2,1)} %reshape_reshape_transpose_reshape.7) | data formatting | bytes 262144 | tf_op jit(solution)/shard_map/reshape;reshape;transpose;reshape | solution.py:84
  124.2 1.8 %multiply_reduce_fusion = (f32[2,16,64]{2,1,0:T(8,128)S(1)}, f32[2,16,64,64]{2,3,1,0:T(8,128)S(1)}) fusion(f32[2,16,64,64]{2,3,1,0:T(8,128)} %copy-done.17, f32[2,16,64]{2,1,0:T(8,128)} %copy-done.19, bf16[2,64,16,32]{1,3,2,0:T(8,128)(2,1)} %copy.28, bf16[2,64,1,16,32]{1,4,3,0,2:T(8,128)(2,1)} %copy.38), kind=kOutput, calls=%fused_computation.43 | convolution fusion | flops 8779776 | bytes 1327104 | tf_op jit(solution)/shard_map/nihd,njhd->nhij/dot_general | solution.py:85
  126.1 1.2 convolution_bitcast_fusion.1
  127.3 1.9 %convolution_bitcast_fusion = f32[2,64,16,32]{1,3,2,0:T(8,128)S(1)} fusion(bf16[2,64,1,16,32]{1,4,3,0,2:T(8,128)(2,1)S(1)} %copy-done.3, f32[2,64,16]{1,2,0:T(8,128)S(1)} %copy-done.11, f32[2,16,64,64]{2,3,1,0:T(8,128)S(1)} %get-tuple-element.25, f32[2,16,64]{2,1,0:T(8,128)S(1)} %get-tuple-element.24, f32[16]{0:T(128)S(1)} %copy-done.15, ...), kind=kOutput, calls=%fused_computation.20 | convolution fusion | flops 50987008 | bytes 1466432 | tf_op jit(solution)/shard_map/nhij,nihd->njhd/dot_general | solution.py:94
  129.9 1.1 pad_maximum_fusion
  131.0 3.0 %copy.33 = bf16[2,64,3,16,32]{4,3,2,1,0:T(8,128)(2,1)} copy(bf16[2,64,3,16,32]{1,4,3,0,2:T(8,128)(2,1)} %pad_maximum_fusion) | data formatting | bytes 786432 | tf_op jit(solution)/shard_map/stack | solution.py:99
  134.1 2.7 %convert_element_type.79 = bf16[16,8,1536]{2,1,0:T(8,128)(2,1)S(1)} reshape(bf16[2,64,3,16,32]{4,3,2,1,0:T(8,128)(2,1)} %copy.33) | data formatting | bytes 786432 | tf_op jit(solution)/shard_map/convert_element_type | solution.py:100
  136.9 1.9 %collective-permute-start.8 = (bf16[16,4,1536]{2,1,0:T(4,128)(2,1)S(1)}, bf16[16,4,1536]{2,1,0:T(4,128)(2,1)S(1)}, u32[]{:S(2)}, u32[]{:S(2)}) collective-permute-start(bf16[16,4,1536]{2,1,0:T(4,128)(2,1)S(1)} %get-tuple-element.10), channel_id=1, source_target_pairs={{504,0},{0,8},{8,16},{16,24},{24,32},{32,40},{40,48},{48,56},{56,6... | collective-permute-start | bytes 589832 | tf_op jit(solution)/shard_map/ppermute | solution.py:19
  138.9 8.8 %collective-permute-done.8 = bf16[16,4,1536]{2,1,0:T(4,128)(2,1)S(1)} collective-permute-done((bf16[16,4,1536]{2,1,0:T(4,128)(2,1)S(1)}, bf16[16,4,1536]{2,1,0:T(4,128)(2,1)S(1)}, u32[]{:S(2)}, u32[]{:S(2)}) %collective-permute-start.8) | collective-permute-done | bytes 196640 | tf_op jit(solution)/shard_map/ppermute | solution.py:19
  147.7 1.9 %collective-permute-start.9 = (bf16[4,8,1536]{2,1,0:T(8,128)(2,1)S(1)}, bf16[4,8,1536]{2,1,0:T(8,128)(2,1)S(1)}, u32[]{:S(2)}, u32[]{:S(2)}) collective-permute-start(bf16[4,8,1536]{2,1,0:T(8,128)(2,1)S(1)} %pad_maximum_fusion.5), channel_id=1, source_target_pairs={{7,0},{0,1},{1,2},{2,3},{3,4},{4,5},{5,6},{6,7},{15,8},{8,9},{9,10... | collective-permute-start | bytes 294920 | tf_op jit(solution)/shard_map/ppermute | solution.py:19
  149.6 6.7 %collective-permute-done.9 = bf16[4,8,1536]{2,1,0:T(8,128)(2,1)S(1)} collective-permute-done((bf16[4,8,1536]{2,1,0:T(8,128)(2,1)S(1)}, bf16[4,8,1536]{2,1,0:T(8,128)(2,1)S(1)}, u32[]{:S(2)}, u32[]{:S(2)}) %collective-permute-start.9) | collective-permute-done | bytes 98336 | tf_op jit(solution)/shard_map/ppermute | solution.py:19
  156.3 2.9 %fusion.32 = bf16[16,8,1024]{2,1,0:T(8,128)(2,1)} fusion(f32[128,1024]{1,0:T(8,128)} %reshape_reshape_reshape_reshape.3, bf16[1024,1536]{1,0:T(8,128)(2,1)S(1)} %copy-done, bf16[16,4,1536]{2,1,0:T(4,128)(2,1)S(1)} %get-tuple-element.11, bf16[16,4,1536]{2,1,0:T(4,128)(2,1)S(1)} %collective-permute-done.8, bf16[4,8,1536]{2,1,0:T(8,128)(2,1)S(1)} %collective-permute-done.9), kind=kOutput, calls=%fused_computation.37 | convolution fusion | flops 404094976 | bytes 4423680 | tf_op jit(solution)/shard_map/dot_general | solution.py:154
  (76 shorter events, 3.3 us)
Async XLA Ops:
  0.0 1.9 %copy-start = (bf16[1024,1536]{1,0:T(8,128)(2,1)S(1)}, bf16[1024,1536]{1,0:T(8,128)(2,1)}, u32[]{:S(2)}) copy-start(bf16[1024,1536]{1,0:T(8,128)(2,1)} %param.12) | copy-start | bytes 9437188
  0.0 15.0 %copy-start.13 = (s32[16,8]{0,1:T(8,128)S(1)}, s32[16,8]{0,1:T(8,128)}, u32[]{:S(2)}) copy-start(s32[16,8]{0,1:T(8,128)} %param.11) | copy-start | bytes 1540
  0.0 18.2 %copy-start.16 = (f32[16]{0:T(128)S(1)}, f32[16]{0:T(128)}, u32[]{:S(2)}) copy-start(f32[16]{0:T(128)} %param.14) | copy-start | bytes 196
  4.2 31.5 %collective-permute-start = (bf16[16,4,1536]{2,1,0:T(4,128)(2,1)}, bf16[16,4,1536]{2,1,0:T(4,128)(2,1)S(1)}, u32[]{:S(2)}, u32[]{:S(2)}) collective-permute-start(bf16[16,4,1536]{2,1,0:T(4,128)(2,1)} %get-tuple-element.13), channel_id=1, source_target_pairs={{8,0},{16,8},{24,16},{32,24},{40,32},{48,40},{56,48},{64,56},{72,6... | collective-permute-start | bytes 589832 | tf_op jit(solution)/shard_map/ppermute | solution.py:19
  15.6 10.6 %collective-permute-start.2 = (s32[16,4]{0,1:T(4,128)}, s32[16,4]{0,1:T(4,128)S(1)}, u32[]{:S(2)}, u32[]{:S(2)}) collective-permute-start(s32[16,4]{0,1:T(4,128)} %get-tuple-element.19), channel_id=1, source_target_pairs={{8,0},{16,8},{24,16},{32,24},{40,32},{48,40},{56,48},{64,56},{72,6... | collective-permute-start | bytes 776 | tf_op jit(solution)/shard_map/ppermute | solution.py:19
  26.2 7.9 %collective-permute-start.3 = (s32[4,8]{0,1:T(8,128)S(1)}, s32[4,8]{0,1:T(8,128)S(1)}, u32[]{:S(2)}, u32[]{:S(2)}) collective-permute-start(s32[4,8]{0,1:T(8,128)S(1)} %bitcast.97), channel_id=1, source_target_pairs={{1,0},{2,1},{3,2},{4,3},{5,4},{6,5},{7,6},{0,7},{9,8},{10,9},{11,1... | collective-permute-start | bytes 392 | tf_op jit(solution)/shard_map/ppermute | solution.py:19
  35.9 8.3 %collective-permute-start.1 = (bf16[4,8,1536]{2,1,0:T(8,128)(2,1)S(1)}, bf16[4,8,1536]{2,1,0:T(8,128)(2,1)S(1)}, u32[]{:S(2)}, u32[]{:S(2)}) collective-permute-start(bf16[4,8,1536]{2,1,0:T(8,128)(2,1)S(1)} %pad_maximum_fusion.6), channel_id=1, source_target_pairs={{1,0},{2,1},{3,2},{4,3},{5,4},{6,5},{7,6},{0,7},{9,8},{10,9},{11,1... | collective-permute-start | bytes 294920 | tf_op jit(solution)/shard_map/ppermute | solution.py:19
  46.4 8.5 %copy-start.14 = (f32[16]{0:T(128)S(1)}, f32[16]{0:T(128)}, u32[]{:S(2)}) copy-start(f32[16]{0:T(128)} %minimum_exponential_fusion) | copy-start | bytes 196
  50.5 0.7 copy-start.2
  54.9 4.5 %copy-start.4 = (bf16[2,64,1,16,32]{1,4,3,0,2:T(8,128)(2,1)S(1)}, bf16[2,64,1,16,32]{1,4,3,0,2:T(8,128)(2,1)}, u32[]{:S(2)}) copy-start(bf16[2,64,1,16,32]{1,4,3,0,2:T(8,128)(2,1)} %copy.38) | copy-start | bytes 393220
  54.9 3.5 %copy-start.8 = (f32[2,64,16]{1,2,0:T(8,128)}, f32[2,64,16]{1,2,0:T(8,128)S(1)}, u32[]{:S(2)}) copy-start(f32[2,64,16]{1,2,0:T(8,128)S(1)} %get-tuple-element.28) | copy-start | bytes 24580
  54.9 3.5 %copy-start.10 = (f32[2,64,16]{1,2,0:T(8,128)}, f32[2,64,16]{1,2,0:T(8,128)S(1)}, u32[]{:S(2)}) copy-start(f32[2,64,16]{1,2,0:T(8,128)S(1)} %get-tuple-element.29) | copy-start | bytes 24580
  58.4 1.0 copy-start.17
  58.4 2.0 %copy-start.19 = (f32[2,16,64]{2,1,0:T(8,128)}, f32[2,16,64]{2,1,0:T(8,128)S(1)}, u32[]{:S(2)}) copy-start(f32[2,16,64]{2,1,0:T(8,128)S(1)} %get-tuple-element.20) | copy-start | bytes 24580
  59.4 24.7 %copy-start.6 = (f32[1024]{0:T(1024)S(1)}, f32[1024]{0:T(1024)}, u32[]{:S(2)}) copy-start(f32[1024]{0:T(1024)} %param.16) | copy-start | bytes 12292
  59.4 24.7 %copy-start.12 = (f32[1024]{0:T(1024)S(1)}, f32[1024]{0:T(1024)}, u32[]{:S(2)}) copy-start(f32[1024]{0:T(1024)} %param.17) | copy-start | bytes 12292
  64.1 9.2 %collective-permute-start.4 = (bf16[16,4,512]{2,1,0:T(4,128)(2,1)S(1)}, bf16[16,4,512]{2,1,0:T(4,128)(2,1)S(1)}, u32[]{:S(2)}, u32[]{:S(2)}) collective-permute-start(bf16[16,4,512]{2,1,0:T(4,128)(2,1)S(1)} %get-tuple-element.16), channel_id=1, source_target_pairs={{504,0},{0,8},{8,16},{16,24},{24,32},{32,40},{40,48},{48,56},{56,6... | collective-permute-start | bytes 196616 | tf_op jit(solution)/shard_map/ppermute | solution.py:19
  73.3 8.3 %collective-permute-start.5 = (bf16[4,8,512]{2,1,0:T(8,128)(2,1)S(1)}, bf16[4,8,512]{2,1,0:T(8,128)(2,1)S(1)}, u32[]{:S(2)}, u32[]{:S(2)}) collective-permute-start(bf16[4,8,512]{2,1,0:T(8,128)(2,1)S(1)} %pad_maximum_fusion.8), channel_id=1, source_target_pairs={{7,0},{0,1},{1,2},{2,3},{3,4},{4,5},{5,6},{6,7},{15,8},{8,9},{9,10... | collective-permute-start | bytes 98312 | tf_op jit(solution)/shard_map/ppermute | solution.py:19
  83.2 0.8 copy-start.1
  83.2 12.4 %copy-start.7 = (f32[4096]{0:T(1024)S(1)}, f32[4096]{0:T(1024)}, u32[]{:S(2)}) copy-start(f32[4096]{0:T(1024)} %param.18) | copy-start | bytes 49156
  111.2 3.8 %collective-permute-start.6 = (bf16[16,4,512]{2,1,0:T(4,128)(2,1)S(1)}, bf16[16,4,512]{2,1,0:T(4,128)(2,1)S(1)}, u32[]{:S(2)}, u32[]{:S(2)}) collective-permute-start(bf16[16,4,512]{2,1,0:T(4,128)(2,1)S(1)} %get-tuple-element.15), channel_id=1, source_target_pairs={{8,0},{16,8},{24,16},{32,24},{40,32},{48,40},{56,48},{64,56},{72,6... | collective-permute-start | bytes 196616 | tf_op jit(solution)/shard_map/ppermute | solution.py:19
  115.0 11.0 %copy-start.9 = (f32[2,64,16]{1,2,0:T(8,128)S(1)}, f32[2,64,16]{1,2,0:T(8,128)}, u32[]{:S(2)}) copy-start(f32[2,64,16]{1,2,0:T(8,128)} %copy-done.8) | copy-start | bytes 24580
  115.0 5.8 %collective-permute-start.7 = (bf16[4,8,512]{2,1,0:T(8,128)(2,1)S(1)}, bf16[4,8,512]{2,1,0:T(8,128)(2,1)S(1)}, u32[]{:S(2)}, u32[]{:S(2)}) collective-permute-start(bf16[4,8,512]{2,1,0:T(8,128)(2,1)S(1)} %pad_maximum_fusion.7), channel_id=1, source_target_pairs={{1,0},{2,1},{3,2},{4,3},{5,4},{6,5},{7,6},{0,7},{9,8},{10,9},{11,1... | collective-permute-start | bytes 98312 | tf_op jit(solution)/shard_map/ppermute | solution.py:19
  122.0 4.1 %copy-start.15 = (f32[16]{0:T(128)S(1)}, f32[16]{0:T(128)}, u32[]{:S(2)}) copy-start(f32[16]{0:T(128)} %minimum_exponential_fusion) | copy-start | bytes 196
  122.0 4.1 %copy-start.20 = (f32[2,16,64]{2,1,0:T(8,128)S(1)}, f32[2,16,64]{2,1,0:T(8,128)}, u32[]{:S(2)}) copy-start(f32[2,16,64]{2,1,0:T(8,128)} %copy-done.19) | copy-start | bytes 24580
  124.2 1.9 %copy-start.18 = (f32[2,16,64,64]{2,3,1,0:T(8,128)S(1)}, f32[2,16,64,64]{2,3,1,0:T(8,128)}, u32[]{:S(2)}) copy-start(f32[2,16,64,64]{2,3,1,0:T(8,128)} %copy-done.17) | copy-start | bytes 1572868
  126.0 1.3 copy-start.3
  126.0 1.3 copy-start.11
  127.3 1.9 %copy-start.5 = (bf16[2,64,16,32]{1,3,2,0:T(8,128)(2,1)S(1)}, bf16[2,64,16,32]{1,3,2,0:T(8,128)(2,1)}, u32[]{:S(2)}) copy-start(bf16[2,64,16,32]{1,3,2,0:T(8,128)(2,1)} %copy.28) | copy-start | bytes 393220
  136.9 10.7 %collective-permute-start.8 = (bf16[16,4,1536]{2,1,0:T(4,128)(2,1)S(1)}, bf16[16,4,1536]{2,1,0:T(4,128)(2,1)S(1)}, u32[]{:S(2)}, u32[]{:S(2)}) collective-permute-start(bf16[16,4,1536]{2,1,0:T(4,128)(2,1)S(1)} %get-tuple-element.10), channel_id=1, source_target_pairs={{504,0},{0,8},{8,16},{16,24},{24,32},{32,40},{40,48},{48,56},{56,6... | collective-permute-start | bytes 589832 | tf_op jit(solution)/shard_map/ppermute | solution.py:19
  147.7 8.6 %collective-permute-start.9 = (bf16[4,8,1536]{2,1,0:T(8,128)(2,1)S(1)}, bf16[4,8,1536]{2,1,0:T(8,128)(2,1)S(1)}, u32[]{:S(2)}, u32[]{:S(2)}) collective-permute-start(bf16[4,8,1536]{2,1,0:T(8,128)(2,1)S(1)} %pad_maximum_fusion.5), channel_id=1, source_target_pairs={{7,0},{0,1},{1,2},{2,3},{3,4},{4,5},{5,6},{6,7},{15,8},{8,9},{9,10... | collective-permute-start | bytes 294920 | tf_op jit(solution)/shard_map/ppermute | solution.py:19
where the time goes:
time: 161 us; the launch traced here: 159 us
  local copies, waits for them, and re-layouts  46.3 us (29%)
  starting transfers between devices  39.9 us (25%)
  waiting for transfers between devices  34.5 us (21%)
  matrix products  22.1 us (14%)
  other arithmetic  16 us (10%)
    ppermute x10, starting transfers between devices, passed_along(): return lax.ppermute(block, axis, route)  39.9 us
    ppermute x10, waiting for transfers between devices, passed_along(): return lax.ppermute(block, axis, route)  34.5 us
    unnamed x45, local copies, waits for them, and re-layouts  9.16 us
    dot_general x1, matrix products, relative_bias(): raw_bias = jnp.einsum('ijr,hr->hij', onehot, bias_table, precision=highest)  4.69 us
    reshape x2, local copies, waits for them, and re-layouts, split_tokens(): grouped = merged.reshape(row_half, col_half, 2, 2, width_d)  4.57 us
    convert_element_type x2, local copies, waits for them, and re-layouts, attend_forward(): attended.reshape(win_count, WIN * WIN, att_width).astype(jnp.bfloat16)  3.66 us
    another operation x2, local copies, waits for them, and re-layouts, attend_backward(): grad_heads = grad_out.reshape(win_count, cell_count, head_count, head_width)  3.28 us
  transfers between devices with their start and end apart: 10, of which 7 were waited for; matrix products, arithmetic and copies ran while one was open for 7% of the time, Pallas kernels for 0%

commit v1 on v0

v1 whole, which is shorter than its diff:
```python
import math

import numpy as np
import jax
import jax.numpy as jnp
from jax import lax
from jax.experimental import pallas as pl
from jax.experimental.pallas import tpu as pltpu
from jax.sharding import PartitionSpec as P

WIN = 8
D = 1024
HEADS = 16
ATT = 512
QUAD = 16
CELLS = 64
BLOCKS = 4
WIDE = 2 * D + 128

norm_eps = 1e-05
unit_eps = 1e-06
f32 = jnp.float32
bf16 = jnp.bfloat16
MIB = 1024 * 1024


def quad_cells():
    cells = [None] * QUAD
    for r in range(4):
        for c in range(4):
            s = (r % 2) + 2 * (c % 2)
            g = (r // 2) * 2 + c // 2
            cells[s * 4 + g] = (r, c)
    return cells


def sorted_cells():
    corners = [(4, 4), (8, 4), (12, 4), (4, 0), (8, 0), (12, 0), (0, 4), (0, 0)]
    return [(r0 + r, c0 + c) for r0, c0 in corners for r, c in quad_cells()]


def window_cells():
    corners = [(0, 0), (0, 4), (4, 0), (4, 4)]
    return [(r0 + r, c0 + c) for r0, c0 in corners for r, c in quad_cells()]


def constants():
    cells = sorted_cells()
    token_sort = np.zeros((128, 128), np.float32)
    cot_sort = np.zeros((128, 128), np.float32)
    label_row = np.zeros((128, 16), np.float32)
    label_col = np.zeros((128, 8), np.float32)
    for n, (r, c) in enumerate(cells):
        token_sort[n, r * 8 + c] = 1
        s = (r % 2) + 2 * (c % 2)
        cot_sort[n, s * 32 + (r // 2) * 4 + c // 2] = 1
        label_row[n, r] = 1
        label_col[n, c] = 1
    table_spread = np.zeros((225, 256), np.float32)
    for m in range(15):
        for c in range(15):
            table_spread[224 - (15 * m + c), 16 * m + c] = 1
    order = window_cells()
    toeplitz = np.zeros((256, 512), np.float32)
    row_order = np.zeros((64, 64), np.float32)
    for n, (ra, rb) in enumerate(order):
        row_order[n, ra * 8 + rb] = 1
        for a in range(8):
            toeplitz[16 * (ra - a + 7) + rb, a * 64 + n] = 1
    return (token_sort, cot_sort, label_row, label_col, table_spread, toeplitz, row_order)


def halves(value):
    high = value.astype(bf16)
    low = (value - high.astype(f32)).astype(bf16)
    return high, low


def mm(a, b):
    return jnp.dot(a, b, preferred_element_type=f32)


def mm_nt(a, b):
    return lax.dot_general(a, b, (((1,), (1,)), ((), ())), preferred_element_type=f32)


def mm_tn(a, b):
    return lax.dot_general(a, b, (((0,), (0,)), ((), ())), preferred_element_type=f32)


def pack_kernel(
    tokens, labels, cot, token_sort, cot_sort, label_row, label_col, own, lon, lat, dia, cot_rows
):
    outs = ((own, 0, 48), (lon, 48, 96), (lat, 96, 112), (dia, 112, 128))
    flat = tokens[...].reshape(128, D)
    moved = mm(token_sort[...], flat).astype(bf16)
    for ref, lo, hi in outs:
        ref[:, 0:D] = moved[lo:hi]
    for r in range(8):
        cot_rows[4 * r : 4 * r + 4, :] = cot[r].astype(f32)
    stacked = jnp.concatenate(
        [cot_rows[:, s * D : (s + 1) * D].astype(bf16) for s in range(4)], axis=0
    )
    moved_cot = mm(cot_sort[...], stacked).astype(bf16)
    for ref, lo, hi in outs:
        ref[:, D : 2 * D] = moved_cot[lo:hi]
    first = lax.axis_index("lat") == 0
    rows = lax.broadcasted_iota(jnp.int32, (16, 8), 0)
    code = labels[...] + jnp.where(rows < 4, jnp.where(first, 4, 0), 0)
    spread = mm(label_row[...], code.astype(f32).astype(bf16)) * label_col[...]
    column = jnp.sum(spread, axis=1, keepdims=True)
    wide = jnp.broadcast_to(column, (128, 128)).astype(bf16)
    for ref, lo, hi in outs:
        ref[:, 2 * D :] = wide[lo:hi]


def pack(tokens, labels, cot, consts):
    token_sort, cot_sort, label_row, label_col = consts
    shapes = [jax.ShapeDtypeStruct((n, WIDE), bf16) for n in (48, 48, 16, 16)]
    return pl.pallas_call(
        pack_kernel,
        out_shape=shapes,
        scratch_shapes=[pltpu.VMEM((32, 4 * D), f32)],
        compiler_params=pltpu.CompilerParams(vmem_limit_bytes=16 * MIB),
        name="pack",
    )(
        tokens,
        labels,
        cot,
        jnp.asarray(token_sort, bf16),
        jnp.asarray(cot_sort, bf16),
        jnp.asarray(label_row, bf16),
        jnp.asarray(label_col, f32),
    )


def prep_kernel(table, scale, table_spread, toeplitz, row_order, ebias, temper, natural):
    gate = 16.0 / (1.0 + jnp.exp(-table[...]))
    high, low = halves(gate)
    spread = mm(high, table_spread[...]) + mm(low, table_spread[...])
    pieces = []
    for h in range(HEADS):
        row = jnp.broadcast_to(spread[h : h + 1, :], (8, 256))
        pieces.append(pltpu.roll(row, 249, 1, stride=1, stride_axis=0))
    shifted = jnp.concatenate(pieces, axis=0)
    high, low = halves(shifted)
    blocks = mm(high, toeplitz[...]) + mm(low, toeplitz[...])
    left = lax.broadcasted_iota(jnp.int32, (8, 128), 1) < 64
    for q in range(8):
        for p in range(4):
            even = blocks[16 * q : 16 * q + 8, 128 * p : 128 * p + 128]
            odd = blocks[16 * q + 8 : 16 * q + 16, 128 * p : 128 * p + 128]
            lanes = slice(128 * q, 128 * q + 128)
            natural[16 * p : 16 * p + 8, lanes] = jnp.where(left, even, pltpu.roll(odd, 64, 1))
            natural[16 * p + 8 : 16 * p + 16, lanes] = jnp.where(
                left, pltpu.roll(even, 64, 1), odd
            )
    high, low = halves(natural[...])
    ordered = mm(row_order[...], high) + mm(row_order[...], low)
    ebias[...] = jnp.exp(ordered)
    per_head = jnp.exp(jnp.minimum(scale[...], math.log(100.0)))
    head_of = lax.broadcasted_iota(jnp.int32, (1, ATT), 1) // 32
    row = jnp.zeros((1, ATT), f32)
    for h in range(HEADS):
        row = jnp.where(head_of == h, per_head[0:1, h : h + 1], row)
    temper[...] = row


def prep(table, scale, consts):
    table_spread, toeplitz, row_order = consts
    return pl.pallas_call(
        prep_kernel,
        out_shape=[
            jax.ShapeDtypeStruct((CELLS, HEADS * CELLS), f32),
            jax.ShapeDtypeStruct((1, ATT), f32),
        ],
        scratch_shapes=[pltpu.VMEM((CELLS, HEADS * CELLS), f32)],
        compiler_params=pltpu.CompilerParams(vmem_limit_bytes=16 * MIB),
        cost_estimate=pl.CostEstimate(flops=100_000_000, bytes_accessed=700_000, transcendentals=80_000),
        name="prep",
    )(
        table,
        scale,
        jnp.asarray(table_spread, bf16),
        jnp.asarray(toeplitz, bf16),
        jnp.asarray(row_order, bf16),
    )


def group_total(column):
    pair = column[0:8] + column[8:16]
    pair = pair + pltpu.roll(pair, 4, 0)
    return jnp.concatenate([pair, pair], axis=0)


def row_total(value):
    return jnp.sum(value, axis=1, keepdims=True)


def main_kernel(
    own,
    lon,
    lat,
    dia,
    ebias,
    temper,
    w_qkv,
    w_proj,
    gain,
    shift,
    merge_gain,
    out_own,
    out_lon,
    out_lat,
    out_dia,
    x_s,
    qkv_s,
    unit_s,
    inv_s,
    qk_s,
    prob_s,
    att_s,
    att16_s,
    proj_s,
    mixed_s,
    gproj_s,
    ga_s,
    gpack_s,
):
    quads = (
        (own, out_own, 0),
        (lon, out_lon, 0),
        (own, out_own, 16),
        (lon, out_lon, 16),
        (own, out_own, 32),
        (lon, out_lon, 32),
        (lat, out_lat, 0),
        (dia, out_dia, 0),
    )
    for n, (ref, _, lo) in enumerate(quads):
        x_s[16 * n : 16 * n + 16, :] = ref[lo : lo + 16, 0:D]
    for n in range(6):
        cols = slice(256 * n, 256 * n + 256)
        qkv_s[:, cols] = mm(x_s[...], w_qkv[:, cols]).astype(bf16)

    lane = lax.broadcasted_iota(jnp.int32, (256, 128), 1)
    line = lax.broadcasted_iota(jnp.int32, (256, 128), 0)
    seg = ((line % 128) // 32 == lane // 32).astype(f32).astype(bf16)
    bd_mask = line // 64 == lane // 32
    lane2 = lax.broadcasted_iota(jnp.int32, (256, 256), 1)
    line2 = lax.broadcasted_iota(jnp.int32, (256, 256), 0)
    ones4 = (line2 // 64 == lane2 // 64).astype(f32).astype(bf16)
    expand = ((line2 % 128) // 32 == lane2 // 64).astype(f32).astype(bf16)

    def segment(value):
        high, low = halves(value)
        return mm(jnp.concatenate([high, low], axis=1), seg)

    for part in range(2):
        for b in range(BLOCKS):
            cols = slice(part * ATT + 128 * b, part * ATT + 128 * b + 128)
            raw = qkv_s[:, cols].astype(f32)
            inv = lax.rsqrt(segment(raw * raw) + unit_eps)
            unit = raw * inv
            inv_s[:, cols] = inv
            unit_s[:, cols] = unit
            if part == 0:
                unit = unit * temper[:, 128 * b : 128 * b + 128]
            qk_s[:, cols] = unit.astype(bf16)

    def block_diagonal(value):
        tiled = jnp.concatenate([value] * 4, axis=0)
        return jnp.where(bd_mask, tiled, jnp.zeros_like(tiled))

    code_lane = lax.broadcasted_iota(jnp.int32, (16, 128), 1)
    for w in range(2):
        rows = slice(64 * w, 64 * w + 64)
        hot = jnp.concatenate(
            [
                (ref[lo : lo + 16, 2 * D :].astype(f32).astype(jnp.int32) == code_lane)
                .astype(f32)
                .astype(bf16)
                for ref, _, lo in quads[4 * w : 4 * w + 4]
            ],
            axis=0,
        )
        allowed = mm_nt(hot, jnp.concatenate([hot] * 4, axis=0))
        for b in range(BLOCKS):
            cols = slice(128 * b, 128 * b + 128)
            wide = slice(256 * b, 256 * b + 256)
            kbd = block_diagonal(qk_s[rows, ATT + 128 * b : ATT + 128 * b + 128])
            vbd = block_diagonal(qkv_s[rows, 2 * ATT + 128 * b : 2 * ATT + 128 * b + 128])
            score = mm_nt(qk_s[rows, cols], kbd)
            weight = jnp.exp(score) * ebias[:, wide] * allowed
            total = mm(weight.astype(bf16), ones4)
            prob = weight / total
            prob_s[rows, wide] = prob
            att = mm(prob.astype(bf16), vbd)
            att_s[rows, cols] = att
            att16_s[rows, cols] = att.astype(bf16)

    for n in range(4):
        cols = slice(256 * n, 256 * n + 256)
        proj_s[:, cols] = mm(att16_s[...], w_proj[:, cols])

    low_rows = lax.broadcasted_iota(jnp.int32, (8, D), 0) < 4
    mgain = jnp.concatenate(
        [
            jnp.where(low_rows, merge_gain[:, 0:D], merge_gain[:, D : 2 * D]),
            jnp.where(low_rows, merge_gain[:, 2 * D : 3 * D], merge_gain[:, 3 * D : 4 * D]),
        ],
        axis=0,
    )
    for n, (ref, _, lo) in enumerate(quads):
        rows = slice(16 * n, 16 * n + 16)
        projected = proj_s[rows, :]
        centered = projected - row_total(projected) * (1.0 / D)
        inv_std = lax.rsqrt(row_total(centered * centered) * (1.0 / D) + norm_eps)
        normed = centered * inv_std
        mixed = x_s[rows, :].astype(f32) + normed * gain[...] + shift[...]
        cent = mixed - group_total(row_total(mixed)) * (0.25 / D)
        merge_inv = lax.rsqrt(group_total(row_total(cent * cent)) * (0.25 / D) + norm_eps)
        hat = cent * merge_inv
        ghat = ref[lo : lo + 16, D : 2 * D].astype(f32) * mgain
        mean_g = group_total(row_total(ghat)) * (0.25 / D)
        mean_gh = group_total(row_total(ghat * hat)) * (0.25 / D)
        gmixed = merge_inv * (ghat - mean_g - hat * mean_gh)
        mixed_s[rows, :] = gmixed
        gnorm = gmixed * gain[...]
        mean_e = row_total(gnorm) * (1.0 / D)
        mean_en = row_total(gnorm * normed) * (1.0 / D)
        gproj_s[rows, :] = (inv_std * (gnorm - mean_e - normed * mean_en)).astype(bf16)

    for n in range(2):
        cols = slice(256 * n, 256 * n + 256)
        ga_s[:, cols] = mm_nt(gproj_s[...], w_proj[cols, :]).astype(bf16)

    head_lane = lax.broadcasted_iota(jnp.int32, (64, 128), 1) // 32

    def diagonal(value):
        out = value[192:256]
        for h in range(3):
            out = jnp.where(head_lane == h, value[64 * h : 64 * h + 64], out)
        return out

    for w in range(2):
        rows = slice(64 * w, 64 * w + 64)
        for b in range(BLOCKS):
            cols = slice(128 * b, 128 * b + 128)
            kcols = slice(ATT + 128 * b, ATT + 128 * b + 128)
            vcols = slice(2 * ATT + 128 * b, 2 * ATT + 128 * b + 128)
            wide = slice(256 * b, 256 * b + 256)
            kbd = block_diagonal(qk_s[rows, kcols])
            vbd = block_diagonal(qkv_s[rows, vcols])
            ga = ga_s[rows, cols]
            prob = prob_s[rows, wide]
            gprob = mm_nt(ga, vbd)
            high, low = halves(ga.astype(f32) * att_s[rows, cols])
            dots = mm(jnp.concatenate([high, low], axis=1), expand)
            gscore = (prob * (gprob - dots)).astype(bf16)
            gq = mm(gscore, kbd) * temper[:, cols]
            gk = diagonal(mm_tn(gscore, qk_s[rows, cols]))
            gv = diagonal(mm_tn(prob.astype(bf16), ga))
            q_unit = unit_s[rows, cols]
            k_unit = unit_s[rows, kcols]
            gq = inv_s[rows, cols] * (gq - q_unit * segment(q_unit * gq))
            gk = inv_s[rows, kcols] * (gk - k_unit * segment(k_unit * gk))
            gpack_s[rows, cols] = gq.astype(bf16)
            gpack_s[rows, kcols] = gk.astype(bf16)
            gpack_s[rows, vcols] = gv.astype(bf16)

    for n in range(4):
        cols = slice(256 * n, 256 * n + 256)
        total = (mixed_s[:, cols] + mm_nt(gpack_s[...], w_qkv[cols, :])).astype(bf16)
        for m, (_, ref, lo) in enumerate(quads):
            ref[lo : lo + 16, cols] = total[16 * m : 16 * m + 16]


def main(own, lon, lat, dia, ebias, temper, w_qkv, w_proj, gain, shift, merge_gain):
    return pl.pallas_call(
        main_kernel,
        out_shape=[jax.ShapeDtypeStruct((n, D), bf16) for n in (48, 48, 16, 16)],
        scratch_shapes=[
            pltpu.VMEM((128, D), bf16),
            pltpu.VMEM((128, 3 * ATT), bf16),
            pltpu.VMEM((128, 2 * ATT), f32),
            pltpu.VMEM((128, 2 * ATT), f32),
            pltpu.VMEM((128, 2 * ATT), bf16),
            pltpu.VMEM((128, HEADS * CELLS), f32),
            pltpu.VMEM((128, ATT), f32),
            pltpu.VMEM((128, ATT), bf16),
            pltpu.VMEM((128, D), f32),
            pltpu.VMEM((128, D), f32),
            pltpu.VMEM((128, D), bf16),
            pltpu.VMEM((128, ATT), bf16),
            pltpu.VMEM((128, 3 * ATT), bf16),
        ],
        compiler_params=pltpu.CompilerParams(vmem_limit_bytes=32 * MIB),
        cost_estimate=pl.CostEstimate(
            flops=1_500_000_000, bytes_accessed=6_000_000, transcendentals=150_000
        ),
        name="main",
    )(own, lon, lat, dia, ebias, temper, w_qkv, w_proj, gain, shift, merge_gain)


def final_kernel(own, lon, lat, dia, token_place, out):
    rows = jnp.concatenate([own[...], lon[...], lat[...], dia[...]], axis=0)
    out[...] = mm(token_place[...], rows).reshape(16, 8, D).astype(bf16)


def final(own, lon, lat, dia, token_place):
    return pl.pallas_call(
        final_kernel,
        out_shape=jax.ShapeDtypeStruct((16, 8, D), bf16),
        compiler_params=pltpu.CompilerParams(vmem_limit_bytes=16 * MIB),
        name="final",
    )(own, lon, lat, dia, jnp.asarray(token_place, bf16))


def shift_by(block, lat_step, lon_step):
    lats, lons = lax.axis_size("lat"), lax.axis_size("lon")
    route = [
        (j * lats + i, ((j + lon_step) % lons) * lats + (i + lat_step) % lats)
        for j in range(lons)
        for i in range(lats)
    ]
    return lax.ppermute(block, ("lon", "lat"), route)


def shards(
    tokens,
    labels,
    w_qkv,
    w_proj,
    logit_scale,
    bias_table,
    norm_gain,
    norm_shift,
    merge_gain,
    cotangent,
):
    consts = constants()
    own, lon, lat, dia = pack(tokens, labels, cotangent, consts[:4])
    lon = shift_by(lon, 0, -1)
    lat = shift_by(lat, -1, 0)
    dia = shift_by(dia, -1, -1)
    ebias, temper = prep(bias_table, logit_scale.reshape(1, HEADS), consts[4:])
    own, lon, lat, dia = main(
        own,
        lon,
        lat,
        dia,
        ebias,
        temper,
        w_qkv,
        w_proj,
        norm_gain.reshape(1, D),
        norm_shift.reshape(1, D),
        merge_gain.reshape(1, 4 * D),
    )
    lon = shift_by(lon, 0, 1)
    lat = shift_by(lat, 1, 0)
    dia = shift_by(dia, 1, 1)
    return final(own, lon, lat, dia, consts[0].T)


def solution(mesh):
    placed = (
        P("lat", "lon", None),
        P("lat", "lon"),
        P(),
        P(),
        P(),
        P(),
        P(),
        P(),
        P(),
        P("lat", "lon", None),
    )
    return jax.shard_map(
        shards, mesh=mesh, in_specs=placed, out_specs=P("lat", "lon", None), check_vma=False
    )
```

time: 161 us -> 60.8 us (0.38)
  local copies, waits for them, and re-layouts: 46.3 us -> 14.9 us
  waiting for transfers between devices: 34.5 us -> 7.53 us
  matrix products: 22.1 us -> 0 us
  other arithmetic: 16 us -> 0 us
  starting transfers between devices: 39.9 us -> 27 us
  Pallas kernels: 0 us -> 10.3 us
    ppermute x10 -> x6, waiting for transfers between devices: 34.5 us -> 7.53 us  [shift_by(): return lax.ppermute(block, ('lon', 'lat'), route)]
    dot_general x11 -> x0, matrix products: 22.1 us -> none  [the longest x1 4.69 us: relative_bias(): raw_bias = jnp.einsum('ijr,hr->hij', onehot, bias_table, precision=highest)]
    another operation x6 -> x0, local copies, waits for them, and re-layouts: 12.9 us -> none  [the longest x2 3.28 us: attend_backward(): grad_heads = grad_out.reshape(win_count, cell_count, head_count, head_width)]
    ppermute x10 -> x6, starting transfers between devices: 39.9 us -> 27 us  [shift_by(): return lax.ppermute(block, ('lon', 'lat'), route)]
    pallas_call x0 -> x4, Pallas kernels: none -> 10.3 us  [the longest x1 8.14 us: main(): pl.pallas_call(main_kernel, out_shape=[jax.ShapeDtypeStruct((n, D), bf16)...]
    reduce_sum x8 -> x0, other arithmetic: 7.44 us -> none  [the longest x1 1.52 us: token_backward(): jnp.mean(grad_hat, -1, keepdims=True)]
    convert_element_type x4 -> x0, local copies, waits for them, and re-layouts: 7.06 us -> none  [the longest x2 3.66 us: attend_forward(): attended.reshape(win_count, WIN * WIN, att_width).astype(jnp.bfloat16)]
    reshape x3 -> x0, local copies, waits for them, and re-layouts: 6.96 us -> none  [the longest x2 4.57 us: split_tokens(): grouped = merged.reshape(row_half, col_half, 2, 2, width_d)]
  transfers between devices with their start and end apart: 10 -> 6, of which waited for: 7 -> 2; matrix products, arithmetic and copies ran while one was open for 7% -> 0% of each run, Pallas kernels for 0% -> 1%
where the time goes in v1:
time: 60.8 us; the launch traced here: 59.9 us
  starting transfers between devices  27 us (44%)
  local copies, waits for them, and re-layouts  14.9 us (25%)
  Pallas kernels  10.3 us (17%)
  waiting for transfers between devices  7.53 us (12%)
    ppermute x6, starting transfers between devices, shift_by(): return lax.ppermute(block, ('lon', 'lat'), route)  27 us
    unnamed x35, local copies, waits for them, and re-layouts  14.9 us
    pallas_call x1, Pallas kernels, main(): pl.pallas_call(main_kernel, out_shape=[jax.ShapeDtypeStruct((n, D), bf16)...  8.14 us
    ppermute x6, waiting for transfers between devices, shift_by(): return lax.ppermute(block, ('lon', 'lat'), route)  7.53 us
  transfers between devices with their start and end apart: 6, of which 2 were waited for; matrix products, arithmetic and copies ran while one was open for 0% of the time, Pallas kernels for 1%

profile of v1, /device:TPU:4, one launch (start us, length us, event | category | flops | bytes accessed | tf_op | source)
XLA Modules:
  0.0 59.9 jit_solution(12538618757285649357)
XLA Ops:
  0.0 0.8 %copy.19.labels = s32[16,8]{1,0:T(8,128)S(1)} copy(s32[16,8]{0,1:T(8,128)} %param.19) | data formatting | bytes 1024 | tf_op args[1]
  0.8 0.0 copy-start.1
  0.8 0.9 %copy-done.1 = bf16[16,8,1024]{2,1,0:T(8,128)(2,1)S(1)} copy-done((bf16[16,8,1024]{2,1,0:T(8,128)(2,1)S(1)}, bf16[16,8,1024]{2,1,0:T(8,128)(2,1)}, u32[]{:S(2)}) %copy-start.1) | copy-done | bytes 262168
  1.7 0.0 copy-start.2
  1.7 0.9 %copy-done.2 = bf16[8,4,4096]{2,1,0:T(4,128)(2,1)S(1)} copy-done((bf16[8,4,4096]{2,1,0:T(4,128)(2,1)S(1)}, bf16[8,4,4096]{2,1,0:T(4,128)(2,1)}, u32[]{:S(2)}) %copy-start.2) | copy-done | bytes 262168
  2.7 0.0 copy-start.4
  2.7 0.8 %copy-done.4 = f32[128,8]{1,0:T(8,128)S(1)} copy-done((f32[128,8]{1,0:T(8,128)S(1)}, f32[128,8]{1,0:T(8,128)}, u32[]{:S(2)}) %copy-start.4) | copy-done | bytes 4120
  3.5 0.0 copy-start.6
  3.5 0.8 %copy-done.6 = bf16[128,16]{1,0:T(8,128)(2,1)S(1)} copy-done((bf16[128,16]{1,0:T(8,128)(2,1)S(1)}, bf16[128,16]{1,0:T(8,128)(2,1)}, u32[]{:S(2)}) %copy-start.6) | copy-done | bytes 4120
  4.3 0.0 copy-start.7
  4.3 0.8 %copy-done.7 = bf16[128,128]{1,0:T(8,128)(2,1)S(1)} copy-done((bf16[128,128]{1,0:T(8,128)(2,1)S(1)}, bf16[128,128]{1,0:T(8,128)(2,1)}, u32[]{:S(2)}) %copy-start.7) | copy-done | bytes 32792
  5.0 0.0 copy-start.8
  5.0 0.8 %copy-done.8 = bf16[128,128]{1,0:T(8,128)(2,1)S(1)} copy-done((bf16[128,128]{1,0:T(8,128)(2,1)S(1)}, bf16[128,128]{1,0:T(8,128)(2,1)}, u32[]{:S(2)}) %copy-start.8) | copy-done | bytes 32792
  5.8 0.0 copy-start.5
  5.8 0.4 pack.1
  6.2 10.8 %collective-permute-start = (bf16[48,2176]{1,0:T(8,128)(2,1)S(1)}, bf16[48,2176]{1,0:T(8,128)(2,1)S(1)}, u32[]{:S(2)}, u32[]{:S(2)}) collective-permute-start(bf16[48,2176]{1,0:T(8,128)(2,1)S(1)} %get-tuple-element.16), channel_id=1, source_target_pairs={{0,504},{1,505},{2,506},{3,507},{4,508},{5,509},{6,510},{7,511},{8... | collective-permute-start | bytes 626696 | tf_op jit(solution)/shard_map/ppermute | solution.py:427
  17.0 6.5 %collective-permute-start.1 = (bf16[16,2176]{1,0:T(8,128)(2,1)S(1)}, bf16[16,2176]{1,0:T(8,128)(2,1)S(1)}, u32[]{:S(2)}, u32[]{:S(2)}) collective-permute-start(bf16[16,2176]{1,0:T(8,128)(2,1)S(1)} %get-tuple-element.17), channel_id=1, source_target_pairs={{0,7},{1,0},{2,1},{3,2},{4,3},{5,4},{6,5},{7,6},{8,15},{9,8},{10,9... | collective-permute-start | bytes 208904 | tf_op jit(solution)/shard_map/ppermute | solution.py:427
  23.4 1.9 %collective-permute-start.2 = (bf16[16,2176]{1,0:T(8,128)(2,1)S(1)}, bf16[16,2176]{1,0:T(8,128)(2,1)S(1)}, u32[]{:S(2)}, u32[]{:S(2)}) collective-permute-start(bf16[16,2176]{1,0:T(8,128)(2,1)S(1)} %get-tuple-element.18), channel_id=1, source_target_pairs={{0,511},{1,504},{2,505},{3,506},{4,507},{5,508},{6,509},{7,510},{8... | collective-permute-start | bytes 208904 | tf_op jit(solution)/shard_map/ppermute | solution.py:427
  25.4 0.0 copy-start
  25.4 0.9 %copy-done = bf16[256,512]{1,0:T(8,128)(2,1)S(1)} copy-done((bf16[256,512]{1,0:T(8,128)(2,1)S(1)}, bf16[256,512]{1,0:T(8,128)(2,1)}, u32[]{:S(2)}) %copy-start) | copy-done | bytes 262168
  26.3 0.0 copy-start.3
  26.3 0.9 %copy-done.3 = bf16[225,256]{1,0:T(8,128)(2,1)S(1)} copy-done((bf16[225,256]{1,0:T(8,128)(2,1)S(1)}, bf16[225,256]{1,0:T(8,128)(2,1)}, u32[]{:S(2)}) %copy-start.3) | copy-done | bytes 115224
  27.2 0.0 copy-start.9
  27.2 0.7 %copy-done.9 = f32[16,225]{1,0:T(8,128)S(1)} copy-done((f32[16,225]{1,0:T(8,128)S(1)}, f32[16,225]{1,0:T(8,128)}, u32[]{:S(2)}) %copy-start.9) | copy-done | bytes 14424
  27.9 0.0 copy-start.10
  27.9 0.7 %copy-done.10 = bf16[64,64]{1,0:T(8,128)(2,1)S(1)} copy-done((bf16[64,64]{1,0:T(8,128)(2,1)S(1)}, bf16[64,64]{1,0:T(8,128)(2,1)}, u32[]{:S(2)}) %copy-start.10) | copy-done | bytes 8216
  28.7 0.0 copy-start.11
  28.7 0.7 %copy-done.11 = f32[16]{0:T(128)S(1)} copy-done((f32[16]{0:T(128)S(1)}, f32[16]{0:T(128)}, u32[]{:S(2)}) %copy-start.11) | copy-done | bytes 88
  29.3 0.8 %prep.1 = (f32[64,1024]{1,0:T(8,128)S(1)}, f32[1,512]{1,0:T(1,128)S(1)}) custom-call(f32[16,225]{1,0:T(8,128)S(1)} %copy-done.9, f32[1,16]{1,0:T(1,128)S(1)} %bitcast.4, bf16[225,256]{1,0:T(8,128)(2,1)S(1)} %copy-done.3, bf16[256,512]{1,0:T(8,128)(2,1)S(1)} %copy-done, bf16[64,64]{1,0:T(8,128)(2,1)S(1)} %copy-done.10), custom_call_target="tpu_custom_call" | custom-call | flops 100000000 | bytes 700000 | tf_op jit(solution)/shard_map/prep/pallas_call | solution.py:171
  30.1 0.0 collective-permute-done.1.lat
  30.1 0.0 collective-permute-done.2.dia
  30.1 0.0 collective-permute-done.lon
  30.1 0.0 copy-start.12
  30.2 1.9 %copy-done.12 = bf16[1024,1536]{1,0:T(8,128)(2,1)S(1)} copy-done((bf16[1024,1536]{1,0:T(8,128)(2,1)S(1)}, bf16[1024,1536]{1,0:T(8,128)(2,1)}, u32[]{:S(2)}) %copy-start.12) | copy-done | bytes 3145752
  32.0 0.0 copy-start.13
  32.0 1.2 %copy-done.13 = bf16[512,1024]{1,0:T(8,128)(2,1)S(1)} copy-done((bf16[512,1024]{1,0:T(8,128)(2,1)S(1)}, bf16[512,1024]{1,0:T(8,128)(2,1)}, u32[]{:S(2)}) %copy-start.13) | copy-done | bytes 1048600
  33.3 0.0 copy-start.14
  33.3 0.7 %copy-done.14 = f32[4096]{0:T(1024)S(1)} copy-done((f32[4096]{0:T(1024)S(1)}, f32[4096]{0:T(1024)}, u32[]{:S(2)}) %copy-start.14) | copy-done | bytes 16408
  34.0 0.0 copy-start.15
  34.0 0.7 %copy-done.15 = f32[1024]{0:T(1024)S(1)} copy-done((f32[1024]{0:T(1024)S(1)}, f32[1024]{0:T(1024)}, u32[]{:S(2)}) %copy-start.15) | copy-done | bytes 4120
  34.7 0.0 copy-start.16
  34.7 0.7 %copy-done.16 = f32[1024]{0:T(1024)S(1)} copy-done((f32[1024]{0:T(1024)S(1)}, f32[1024]{0:T(1024)}, u32[]{:S(2)}) %copy-start.16) | copy-done | bytes 4120
  35.4 8.1 %main.1 = (bf16[48,1024]{1,0:T(8,128)(2,1)S(1)}, bf16[48,1024]{1,0:T(8,128)(2,1)S(1)}, bf16[16,1024]{1,0:T(8,128)(2,1)S(1)}, bf16[16,1024]{1,0:T(8,128)(2,1)S(1)}) custom-call(bf16[48,2176]{1,0:T(8,128)(2,1)S(1)} %get-tuple-element.15.own, bf16[48,2176]{1,0:T(8,128)(2,1)S(1)} %collective-permute-done.lon, bf16[16,2176]{1,0:T(8,128)(2,1)S(1)} %collective-permute-done.1.lat, ...), custom_call_target="tpu_custom_call" | custom-call | flops 1500000000 | bytes 6000000 | tf_op jit(solution)/shard_map/main/pallas_call | solution.py:380
  43.5 2.0 %collective-permute-start.3 = (bf16[48,1024]{1,0:T(8,128)(2,1)S(1)}, bf16[48,1024]{1,0:T(8,128)(2,1)S(1)}, u32[]{:S(2)}, u32[]{:S(2)}) collective-permute-start(bf16[48,1024]{1,0:T(8,128)(2,1)S(1)} %get-tuple-element.22), channel_id=1, source_target_pairs={{0,8},{1,9},{2,10},{3,11},{4,12},{5,13},{6,14},{7,15},{8,16},{9,17... | collective-permute-start | bytes 294920 | tf_op jit(solution)/shard_map/ppermute | solution.py:427
  45.5 3.9 %collective-permute-start.4 = (bf16[16,1024]{1,0:T(8,128)(2,1)S(1)}, bf16[16,1024]{1,0:T(8,128)(2,1)S(1)}, u32[]{:S(2)}, u32[]{:S(2)}) collective-permute-start(bf16[16,1024]{1,0:T(8,128)(2,1)S(1)} %get-tuple-element.23), channel_id=1, source_target_pairs={{0,1},{1,2},{2,3},{3,4},{4,5},{5,6},{6,7},{7,0},{8,9},{9,10},{10,1... | collective-permute-start | bytes 98312 | tf_op jit(solution)/shard_map/ppermute | solution.py:427
  49.5 1.9 %collective-permute-start.5 = (bf16[16,1024]{1,0:T(8,128)(2,1)S(1)}, bf16[16,1024]{1,0:T(8,128)(2,1)S(1)}, u32[]{:S(2)}, u32[]{:S(2)}) collective-permute-start(bf16[16,1024]{1,0:T(8,128)(2,1)S(1)} %get-tuple-element.24), channel_id=1, source_target_pairs={{0,9},{1,10},{2,11},{3,12},{4,13},{5,14},{6,15},{7,8},{8,17},{9,18... | collective-permute-start | bytes 98312 | tf_op jit(solution)/shard_map/ppermute | solution.py:427
  51.4 3.1 %collective-permute-done.4.lat = bf16[16,1024]{1,0:T(8,128)(2,1)S(1)} collective-permute-done((bf16[16,1024]{1,0:T(8,128)(2,1)S(1)}, bf16[16,1024]{1,0:T(8,128)(2,1)S(1)}, u32[]{:S(2)}, u32[]{:S(2)}) %collective-permute-start.4) | collective-permute-done | bytes 32800 | tf_op jit(solution)/shard_map/ppermute | solution.py:427
  54.5 4.5 %collective-permute-done.5.dia = bf16[16,1024]{1,0:T(8,128)(2,1)S(1)} collective-permute-done((bf16[16,1024]{1,0:T(8,128)(2,1)S(1)}, bf16[16,1024]{1,0:T(8,128)(2,1)S(1)}, u32[]{:S(2)}, u32[]{:S(2)}) %collective-permute-start.5) | collective-permute-done | bytes 32800 | tf_op jit(solution)/shard_map/ppermute | solution.py:427
  58.9 0.0 collective-permute-done.3.lon
  58.9 0.0 copy-done.5
  58.9 0.9 %final.1 = bf16[16,8,1024]{2,1,0:T(8,128)(2,1)} custom-call(bf16[48,1024]{1,0:T(8,128)(2,1)S(1)} %get-tuple-element.21.own, bf16[48,1024]{1,0:T(8,128)(2,1)S(1)} %collective-permute-done.3.lon, bf16[16,1024]{1,0:T(8,128)(2,1)S(1)} %collective-permute-done.4.lat, bf16[16,1024]{1,0:T(8,128)(2,1)S(1)} %collective-permute-done.5.dia, bf16[128,128]{1,0:T(8,128)(2,1)S(1)} %copy-done.5), custom_call_target="tpu_custom_call" | custom-call | tf_op jit(solution)/shard_map/final/pallas_call | solution.py:412
Async XLA Ops:
  0.8 0.9 %copy-start.1 = (bf16[16,8,1024]{2,1,0:T(8,128)(2,1)S(1)}, bf16[16,8,1024]{2,1,0:T(8,128)(2,1)}, u32[]{:S(2)}) copy-start(bf16[16,8,1024]{2,1,0:T(8,128)(2,1)} %tokens.1) | copy-start | bytes 786436
  1.7 0.9 %copy-start.2 = (bf16[8,4,4096]{2,1,0:T(4,128)(2,1)S(1)}, bf16[8,4,4096]{2,1,0:T(4,128)(2,1)}, u32[]{:S(2)}) copy-start(bf16[8,4,4096]{2,1,0:T(4,128)(2,1)} %cot.1) | copy-start | bytes 786436
  2.7 0.8 %copy-start.4 = (f32[128,8]{1,0:T(8,128)S(1)}, f32[128,8]{1,0:T(8,128)}, u32[]{:S(2)}) copy-start(f32[128,8]{1,0:T(8,128)} %constant.19.clone.label_col) | copy-start | bytes 12292
  3.5 0.8 %copy-start.6 = (bf16[128,16]{1,0:T(8,128)(2,1)S(1)}, bf16[128,16]{1,0:T(8,128)(2,1)}, u32[]{:S(2)}) copy-start(bf16[128,16]{1,0:T(8,128)(2,1)} %constant.18.clone.label_row) | copy-start | bytes 12292
  4.3 0.8 %copy-start.7 = (bf16[128,128]{1,0:T(8,128)(2,1)S(1)}, bf16[128,128]{1,0:T(8,128)(2,1)}, u32[]{:S(2)}) copy-start(bf16[128,128]{1,0:T(8,128)(2,1)} %constant.17.clone.cot_sort) | copy-start | bytes 98308
  5.0 0.8 %copy-start.8 = (bf16[128,128]{1,0:T(8,128)(2,1)S(1)}, bf16[128,128]{1,0:T(8,128)(2,1)}, u32[]{:S(2)}) copy-start(bf16[128,128]{1,0:T(8,128)(2,1)} %constant.16.clone.token_sort) | copy-start | bytes 98308
  5.8 53.2 %copy-start.5 = (bf16[128,128]{1,0:T(8,128)(2,1)S(1)}, bf16[128,128]{1,0:T(8,128)(2,1)}, u32[]{:S(2)}) copy-start(bf16[128,128]{1,0:T(8,128)(2,1)} %constant.23.clone.token_place) | copy-start | bytes 98308
  6.2 24.0 %collective-permute-start = (bf16[48,2176]{1,0:T(8,128)(2,1)S(1)}, bf16[48,2176]{1,0:T(8,128)(2,1)S(1)}, u32[]{:S(2)}, u32[]{:S(2)}) collective-permute-start(bf16[48,2176]{1,0:T(8,128)(2,1)S(1)} %get-tuple-element.16), channel_id=1, source_target_pairs={{0,504},{1,505},{2,506},{3,507},{4,508},{5,509},{6,510},{7,511},{8... | collective-permute-start | bytes 626696 | tf_op jit(solution)/shard_map/ppermute | solution.py:427
  17.0 13.1 %collective-permute-start.1 = (bf16[16,2176]{1,0:T(8,128)(2,1)S(1)}, bf16[16,2176]{1,0:T(8,128)(2,1)S(1)}, u32[]{:S(2)}, u32[]{:S(2)}) collective-permute-start(bf16[16,2176]{1,0:T(8,128)(2,1)S(1)} %get-tuple-element.17), channel_id=1, source_target_pairs={{0,7},{1,0},{2,1},{3,2},{4,3},{5,4},{6,5},{7,6},{8,15},{9,8},{10,9... | collective-permute-start | bytes 208904 | tf_op jit(solution)/shard_map/ppermute | solution.py:427
  23.4 6.7 %collective-permute-start.2 = (bf16[16,2176]{1,0:T(8,128)(2,1)S(1)}, bf16[16,2176]{1,0:T(8,128)(2,1)S(1)}, u32[]{:S(2)}, u32[]{:S(2)}) collective-permute-start(bf16[16,2176]{1,0:T(8,128)(2,1)S(1)} %get-tuple-element.18), channel_id=1, source_target_pairs={{0,511},{1,504},{2,505},{3,506},{4,507},{5,508},{6,509},{7,510},{8... | collective-permute-start | bytes 208904 | tf_op jit(solution)/shard_map/ppermute | solution.py:427
  25.4 1.0 %copy-start = (bf16[256,512]{1,0:T(8,128)(2,1)S(1)}, bf16[256,512]{1,0:T(8,128)(2,1)}, u32[]{:S(2)}) copy-start(bf16[256,512]{1,0:T(8,128)(2,1)} %constant.21.clone.toeplitz) | copy-start | bytes 786436
  26.3 0.9 %copy-start.3 = (bf16[225,256]{1,0:T(8,128)(2,1)S(1)}, bf16[225,256]{1,0:T(8,128)(2,1)}, u32[]{:S(2)}) copy-start(bf16[225,256]{1,0:T(8,128)(2,1)} %constant.20.clone.table_spread) | copy-start | bytes 345604
  27.2 0.7 %copy-start.9 = (f32[16,225]{1,0:T(8,128)S(1)}, f32[16,225]{1,0:T(8,128)}, u32[]{:S(2)}) copy-start(f32[16,225]{1,0:T(8,128)} %table.1) | copy-start | bytes 43204
  27.9 0.7 %copy-start.10 = (bf16[64,64]{1,0:T(8,128)(2,1)S(1)}, bf16[64,64]{1,0:T(8,128)(2,1)}, u32[]{:S(2)}) copy-start(bf16[64,64]{1,0:T(8,128)(2,1)} %constant.22.clone.row_order) | copy-start | bytes 24580
  28.7 0.7 %copy-start.11 = (f32[16]{0:T(128)S(1)}, f32[16]{0:T(128)}, u32[]{:S(2)}) copy-start(f32[16]{0:T(128)} %param.22) | copy-start | bytes 196
  30.1 1.9 %copy-start.12 = (bf16[1024,1536]{1,0:T(8,128)(2,1)S(1)}, bf16[1024,1536]{1,0:T(8,128)(2,1)}, u32[]{:S(2)}) copy-start(bf16[1024,1536]{1,0:T(8,128)(2,1)} %w_qkv.1) | copy-start | bytes 9437188
  32.0 1.2 %copy-start.13 = (bf16[512,1024]{1,0:T(8,128)(2,1)S(1)}, bf16[512,1024]{1,0:T(8,128)(2,1)}, u32[]{:S(2)}) copy-start(bf16[512,1024]{1,0:T(8,128)(2,1)} %w_proj.1) | copy-start | bytes 3145732
  33.3 0.7 %copy-start.14 = (f32[4096]{0:T(1024)S(1)}, f32[4096]{0:T(1024)}, u32[]{:S(2)}) copy-start(f32[4096]{0:T(1024)} %param.26) | copy-start | bytes 49156
  34.0 0.7 %copy-start.15 = (f32[1024]{0:T(1024)S(1)}, f32[1024]{0:T(1024)}, u32[]{:S(2)}) copy-start(f32[1024]{0:T(1024)} %param.24) | copy-start | bytes 12292
  34.7 0.7 %copy-start.16 = (f32[1024]{0:T(1024)S(1)}, f32[1024]{0:T(1024)}, u32[]{:S(2)}) copy-start(f32[1024]{0:T(1024)} %param.25) | copy-start | bytes 12292
  43.5 15.4 %collective-permute-start.3 = (bf16[48,1024]{1,0:T(8,128)(2,1)S(1)}, bf16[48,1024]{1,0:T(8,128)(2,1)S(1)}, u32[]{:S(2)}, u32[]{:S(2)}) collective-permute-start(bf16[48,1024]{1,0:T(8,128)(2,1)S(1)} %get-tuple-element.22), channel_id=1, source_target_pairs={{0,8},{1,9},{2,10},{3,11},{4,12},{5,13},{6,14},{7,15},{8,16},{9,17... | collective-permute-start | bytes 294920 | tf_op jit(solution)/shard_map/ppermute | solution.py:427
  45.5 8.9 %collective-permute-start.4 = (bf16[16,1024]{1,0:T(8,128)(2,1)S(1)}, bf16[16,1024]{1,0:T(8,128)(2,1)S(1)}, u32[]{:S(2)}, u32[]{:S(2)}) collective-permute-start(bf16[16,1024]{1,0:T(8,128)(2,1)S(1)} %get-tuple-element.23), channel_id=1, source_target_pairs={{0,1},{1,2},{2,3},{3,4},{4,5},{5,6},{6,7},{7,0},{8,9},{9,10},{10,1... | collective-permute-start | bytes 98312 | tf_op jit(solution)/shard_map/ppermute | solution.py:427
  49.5 9.5 %collective-permute-start.5 = (bf16[16,1024]{1,0:T(8,128)(2,1)S(1)}, bf16[16,1024]{1,0:T(8,128)(2,1)S(1)}, u32[]{:S(2)}, u32[]{:S(2)}) collective-permute-start(bf16[16,1024]{1,0:T(8,128)(2,1)S(1)} %get-tuple-element.24), channel_id=1, source_target_pairs={{0,9},{1,10},{2,11},{3,12},{4,13},{5,14},{6,15},{7,8},{8,17},{9,18... | collective-permute-start | bytes 98312 | tf_op jit(solution)/shard_map/ppermute | solution.py:427

commit v2 on v1

v2 whole, which is shorter than its diff:
```python
import math

import jax
import jax.numpy as jnp
from jax import lax
from jax.experimental import pallas as pl
from jax.experimental.pallas import tpu as pltpu
from jax.sharding import PartitionSpec as P

WIN = 8
D = 1024
HEADS = 16
ATT = 512
QUAD = 16
CELLS = 64
BLOCKS = 4
WIDE = 2 * D + 128

norm_eps = 1e-05
unit_eps = 1e-06
f32 = jnp.float32
bf16 = jnp.bfloat16
MIB = 1024 * 1024
BUSY = pl.CostEstimate(flops=10_000_000_000, bytes_accessed=30_000_000, transcendentals=0)


def sorted_place(n):
    quad = n // 16
    s = (n // 4) % 4
    g = n % 4
    row = jnp.where(quad < 6, 4 + 4 * (quad % 3), 0) + 2 * (g // 2) + s % 2
    col = jnp.where((quad // 3 == 1) | (quad == 7), 4, 0) + 2 * (g % 2) + s // 2
    return row, col, s


def window_place(n):
    row = 4 * (n // 32) + 2 * ((n // 2) % 2) + (n // 4) % 2
    col = 4 * ((n // 16) % 2) + 2 * (n % 2) + (n // 8) % 2
    return row, col


def iota(shape, axis):
    return lax.broadcasted_iota(jnp.int32, shape, axis)


def onehot(match):
    return match.astype(f32).astype(bf16)


def halves(value):
    high = value.astype(bf16)
    low = (value - high.astype(f32)).astype(bf16)
    return high, low


def mm(a, b):
    return jnp.dot(a, b, preferred_element_type=f32)


def mm_nt(a, b):
    return lax.dot_general(a, b, (((1,), (1,)), ((), ())), preferred_element_type=f32)


def mm_tn(a, b):
    return lax.dot_general(a, b, (((0,), (0,)), ((), ())), preferred_element_type=f32)


def places_kernel(token_sort, cot_sort, label_row, label_col):
    row, col, s = sorted_place(iota((128, 128), 0))
    lane = iota((128, 128), 1)
    token_sort[...] = onehot(lane == row * 8 + col)
    cot_sort[...] = onehot(lane == s * 32 + (row // 2) * 4 + col // 2)
    row, _, _ = sorted_place(iota((128, 16), 0))
    label_row[...] = (iota((128, 16), 1) == row).astype(f32)
    _, col, _ = sorted_place(iota((128, 8), 0))
    label_col[...] = onehot(iota((128, 8), 1) == col)


def places():
    return pl.pallas_call(
        places_kernel,
        out_shape=[
            jax.ShapeDtypeStruct((128, 128), bf16),
            jax.ShapeDtypeStruct((128, 128), bf16),
            jax.ShapeDtypeStruct((128, 16), f32),
            jax.ShapeDtypeStruct((128, 8), bf16),
        ],
        compiler_params=pltpu.CompilerParams(vmem_limit_bytes=8 * MIB),
        cost_estimate=BUSY,
        name="places",
    )()


def pack_kernel(
    token_sort, cot_sort, label_row, label_col, tokens, labels, cot, own, lon, lat, dia, cot_rows
):
    outs = ((own, 0, 48), (lon, 48, 96), (lat, 96, 112), (dia, 112, 128))
    moved = mm(token_sort[...], tokens[...].reshape(128, D)).astype(bf16)
    for ref, lo, hi in outs:
        ref[:, 0:D] = moved[lo:hi]
    first = lax.axis_index("lat") == 0
    code = labels[...] + jnp.where(iota((8, 16), 1) < 4, jnp.where(first, 4, 0), 0)
    spread = mm(label_col[...], code.astype(f32).astype(bf16)) * label_row[...]
    column = jnp.sum(spread, axis=1, keepdims=True)
    wide = jnp.broadcast_to(column, (128, 128)).astype(bf16)
    for ref, lo, hi in outs:
        ref[:, 2 * D :] = wide[lo:hi]
    for r in range(8):
        cot_rows[4 * r : 4 * r + 4, :] = cot[r].astype(f32)
    stacked = jnp.concatenate(
        [cot_rows[:, s * D : (s + 1) * D].astype(bf16) for s in range(4)], axis=0
    )
    moved_cot = mm(cot_sort[...], stacked).astype(bf16)
    for ref, lo, hi in outs:
        ref[:, D : 2 * D] = moved_cot[lo:hi]


def pack(tokens, labels, cot, sorts):
    shapes = [jax.ShapeDtypeStruct((n, WIDE), bf16) for n in (48, 48, 16, 16)]
    return pl.pallas_call(
        pack_kernel,
        out_shape=shapes,
        scratch_shapes=[pltpu.VMEM((32, 4 * D), f32)],
        compiler_params=pltpu.CompilerParams(vmem_limit_bytes=12 * MIB),
        cost_estimate=BUSY,
        name="pack",
    )(*sorts, tokens, labels, cot)


def relative_bias(table, natural, ebias):
    entry, place = iota((225, 256), 0), iota((225, 256), 1)
    table_spread = onehot((entry == 15 * (place // 16) + place % 16) & (place % 16 < 15))
    entry, place = iota((256, 512), 0), iota((256, 512), 1)
    row, col = window_place(place % 64)
    toeplitz = onehot(entry == 16 * (row - place // 64 + 7) + col)
    row, col = window_place(iota((64, 64), 0))
    row_order = onehot(iota((64, 64), 1) == row * 8 + col)
    gate = 16.0 / (1.0 + jnp.exp(-table))
    high, low = halves(gate)
    spread = mm(high, table_spread) + mm(low, table_spread)
    pieces = []
    for h in range(HEADS):
        line = jnp.broadcast_to(spread[h : h + 1, :], (8, 256))
        pieces.append(pltpu.roll(line, 249, 1, stride=1, stride_axis=0))
    high, low = halves(jnp.concatenate(pieces, axis=0))
    blocks = mm(high, toeplitz) + mm(low, toeplitz)
    left = iota((8, 128), 1) < 64
    for q in range(8):
        for p in range(4):
            even = blocks[16 * q : 16 * q + 8, 128 * p : 128 * p + 128]
            odd = blocks[16 * q + 8 : 16 * q + 16, 128 * p : 128 * p + 128]
            lanes = slice(128 * q, 128 * q + 128)
            natural[16 * p : 16 * p + 8, lanes] = jnp.where(left, even, pltpu.roll(odd, 64, 1))
            natural[16 * p + 8 : 16 * p + 16, lanes] = jnp.where(
                left, pltpu.roll(even, 64, 1), odd
            )
    high, low = halves(natural[...])
    ebias[...] = jnp.exp(mm(row_order, high) + mm(row_order, low))


def prep_kernel(table, scale, ebias, temper, natural):
    relative_bias(table[...], natural, ebias)
    per_head = jnp.exp(jnp.minimum(scale[...], math.log(100.0)))
    head_of = iota((1, ATT), 1) // 32
    line = jnp.zeros((1, ATT), f32)
    for h in range(HEADS):
        line = jnp.where(head_of == h, per_head[0:1, h : h + 1], line)
    temper[...] = line


def prep(table, scale):
    return pl.pallas_call(
        prep_kernel,
        out_shape=[
            jax.ShapeDtypeStruct((CELLS, HEADS * CELLS), f32),
            jax.ShapeDtypeStruct((1, ATT), f32),
        ],
        scratch_shapes=[pltpu.VMEM((CELLS, HEADS * CELLS), f32)],
        compiler_params=pltpu.CompilerParams(vmem_limit_bytes=12 * MIB),
        cost_estimate=pl.CostEstimate(
            flops=100_000_000, bytes_accessed=400_000, transcendentals=80_000
        ),
        name="prep",
    )(table, scale)


def group_total(column):
    pair = column[0:8] + column[8:16]
    pair = pair + pltpu.roll(pair, 4, 0)
    return jnp.concatenate([pair, pair], axis=0)


def row_total(value):
    return jnp.sum(value, axis=1, keepdims=True)


def col_total(value):
    return jnp.sum(value, axis=0, keepdims=True)


def main_kernel(
    own,
    lon,
    lat,
    dia,
    ebias,
    temper,
    w_qkv,
    w_proj,
    gain,
    shift,
    merge,
    out_own,
    out_lon,
    out_lat,
    out_dia,
    x_s,
    qkv_s,
    unit_s,
    inv_s,
    unit16_s,
    seg_s,
    qbd_s,
    prob_s,
    prob16_s,
    att_s,
    proj_s,
    mixed_s,
    gproj_s,
    ga_s,
    gpack_s,
    mgain,
):
    quads = (
        (lon, out_lon, 0),
        (own, out_own, 0),
        (lon, out_lon, 16),
        (own, out_own, 16),
        (lon, out_lon, 32),
        (own, out_own, 32),
        (dia, out_dia, 0),
        (lat, out_lat, 0),
    )
    pairs = [(w, b) for w in range(2) for b in range(BLOCKS)]
    for n, (ref, _, lo) in enumerate(quads):
        x_s[16 * n : 16 * n + 16, :] = ref[lo : lo + 16, 0:D]
    for n in range(6):
        cols = slice(256 * n, 256 * n + 256)
        qkv_s[:, cols] = mm(x_s[...], w_qkv[:, cols]).astype(bf16)

    line, lane = iota((256, 128), 0), iota((256, 128), 1)
    seg = onehot((line % 128) // 32 == lane // 32)
    head_lane = iota((64, 128), 1) // 32
    head_mask = [onehot(head_lane == h) for h in range(4)]

    def store_halves(n, value):
        high, low = halves(value)
        seg_s[128 * n : 128 * n + 128, 0:128] = high
        seg_s[128 * n : 128 * n + 128, 128:256] = low

    def block_diagonal(value):
        return jnp.concatenate([value * head_mask[h] for h in range(4)], axis=0)

    def diagonal(value):
        out = value[192:256]
        for h in range(3):
            out = jnp.where(head_lane == h, value[64 * h : 64 * h + 64], out)
        return out

    for n in range(8):
        raw = qkv_s[:, 128 * n : 128 * n + 128].astype(f32)
        store_halves(n, raw * raw)
    squares = mm(seg_s[...], seg)
    for n in range(8):
        cols = slice(128 * n, 128 * n + 128)
        inv = lax.rsqrt(squares[cols] + unit_eps)
        unit = qkv_s[:, cols].astype(f32) * inv
        inv_s[:, cols] = inv
        unit_s[:, cols] = unit
        if n < BLOCKS:
            unit = unit * temper[:, cols]
        unit16_s[:, cols] = unit.astype(bf16)

    code_lane = iota((16, 128), 1)
    allowed = []
    for w in range(2):
        hot = jnp.concatenate(
            [
                onehot(ref[lo : lo + 16, 2 * D :].astype(f32).astype(jnp.int32) == code_lane)
                for ref, _, lo in quads[4 * w : 4 * w + 4]
            ],
            axis=0,
        )
        allowed.append(mm_nt(hot, jnp.concatenate([hot] * 4, axis=0)))
    for n, (w, b) in enumerate(pairs):
        rows = slice(64 * w, 64 * w + 64)
        wide = slice(256 * b, 256 * b + 256)
        qbd = block_diagonal(unit16_s[rows, 128 * b : 128 * b + 128])
        qbd_s[256 * n : 256 * n + 256, :] = qbd
        score = mm_nt(unit16_s[rows, ATT + 128 * b : ATT + 128 * b + 128], qbd)
        weight = jnp.exp(score) * ebias[:, wide] * allowed[w]
        prob = weight * (1.0 / col_total(weight))
        prob_s[rows, wide] = prob
        prob16_s[rows, wide] = prob.astype(bf16)
    for w, b in pairs:
        rows = slice(64 * w, 64 * w + 64)
        vals = qkv_s[rows, 2 * ATT + 128 * b : 2 * ATT + 128 * b + 128]
        att = diagonal(mm_tn(prob16_s[rows, 256 * b : 256 * b + 256], vals))
        att_s[rows, 128 * b : 128 * b + 128] = att.astype(bf16)

    for n in range(4):
        cols = slice(256 * n, 256 * n + 256)
        proj_s[:, cols] = mm(att_s[...], w_proj[:, cols])

    spans = [slice(16 * n, 16 * n + 16) for n in range(8)]

    def ghat_of(n):
        ref, _, lo = quads[n]
        return ref[lo : lo + 16, D : 2 * D].astype(f32) * mgain[...]

    for s in range(4):
        mgain[4 * s : 4 * s + 4, :] = jnp.broadcast_to(merge[:, s * D : (s + 1) * D], (4, D))
    mean = [row_total(proj_s[rows, :]) * (1.0 / D) for rows in spans]
    inv_std = []
    for n, rows in enumerate(spans):
        centered = proj_s[rows, :] - mean[n]
        inv_std.append(lax.rsqrt(row_total(centered * centered) * (1.0 / D) + norm_eps))
    mean_m, mean_g = [], []
    for n, rows in enumerate(spans):
        normed = (proj_s[rows, :] - mean[n]) * inv_std[n]
        proj_s[rows, :] = normed
        mixed = x_s[rows, :].astype(f32) + normed * gain[...] + shift[...]
        mixed_s[rows, :] = mixed
        mean_m.append(group_total(row_total(mixed)) * (0.25 / D))
        mean_g.append(group_total(row_total(ghat_of(n))) * (0.25 / D))
    merge_inv, slope = [], []
    for n, rows in enumerate(spans):
        cent = mixed_s[rows, :] - mean_m[n]
        ghat = ghat_of(n)
        inv = lax.rsqrt(group_total(row_total(cent * cent)) * (0.25 / D) + norm_eps)
        merge_inv.append(inv)
        slope.append(group_total(row_total(ghat * cent)) * (0.25 / D) * inv * inv)
    mean_e, mean_en = [], []
    for n, rows in enumerate(spans):
        cent = mixed_s[rows, :] - mean_m[n]
        gmixed = merge_inv[n] * (ghat_of(n) - mean_g[n] - cent * slope[n])
        mixed_s[rows, :] = gmixed
        gnorm = gmixed * gain[...]
        mean_e.append(row_total(gnorm) * (1.0 / D))
        mean_en.append(row_total(gnorm * proj_s[rows, :]) * (1.0 / D))
    for n, rows in enumerate(spans):
        gnorm = mixed_s[rows, :] * gain[...]
        gproj = inv_std[n] * (gnorm - mean_e[n] - proj_s[rows, :] * mean_en[n])
        gproj_s[rows, :] = gproj.astype(bf16)

    for n in range(2):
        cols = slice(256 * n, 256 * n + 256)
        ga_s[:, cols] = mm_nt(gproj_s[...], w_proj[cols, :]).astype(bf16)

    grad_k, grad_q = [], []
    for n, (w, b) in enumerate(pairs):
        rows = slice(64 * w, 64 * w + 64)
        wide = slice(256 * b, 256 * b + 256)
        vcols = slice(2 * ATT + 128 * b, 2 * ATT + 128 * b + 128)
        gabd = block_diagonal(ga_s[rows, 128 * b : 128 * b + 128])
        gprob = mm_nt(qkv_s[rows, vcols], gabd)
        gpack_s[rows, vcols] = mm(prob16_s[rows, wide], gabd).astype(bf16)
        prob = prob_s[rows, wide]
        gscore = prob * (gprob - col_total(prob * gprob))
        prob16_s[rows, wide] = gscore.astype(bf16)
    for n, (w, b) in enumerate(pairs):
        rows = slice(64 * w, 64 * w + 64)
        gscore = prob16_s[rows, 256 * b : 256 * b + 256]
        qcols = slice(128 * b, 128 * b + 128)
        kcols = slice(ATT + 128 * b, ATT + 128 * b + 128)
        gk = mm(gscore, qbd_s[256 * n : 256 * n + 256, :])
        gq = diagonal(mm_tn(gscore, unit16_s[rows, kcols])) * temper[:, qcols]
        proj_s[rows, qcols] = gq
        proj_s[rows, kcols] = gk
    for n in range(8):
        cols = slice(128 * n, 128 * n + 128)
        store_halves(n, unit_s[:, cols] * proj_s[:, cols])
    along = mm(seg_s[...], seg)
    for n in range(8):
        cols = slice(128 * n, 128 * n + 128)
        grad = inv_s[:, cols] * (proj_s[:, cols] - unit_s[:, cols] * along[cols])
        gpack_s[:, cols] = grad.astype(bf16)

    for n in range(4):
        cols = slice(256 * n, 256 * n + 256)
        total = (mixed_s[:, cols] + mm_nt(gpack_s[...], w_qkv[cols, :])).astype(bf16)
        for m, (_, ref, lo) in enumerate(quads):
            ref[lo : lo + 16, cols] = total[16 * m : 16 * m + 16]


def main(own, lon, lat, dia, *params):
    return pl.pallas_call(
        main_kernel,
        out_shape=[jax.ShapeDtypeStruct((n, D), bf16) for n in (48, 48, 16, 16)],
        scratch_shapes=[
            pltpu.VMEM((128, D), bf16),
            pltpu.VMEM((128, 3 * ATT), bf16),
            pltpu.VMEM((128, 2 * ATT), f32),
            pltpu.VMEM((128, 2 * ATT), f32),
            pltpu.VMEM((128, 2 * ATT), bf16),
            pltpu.VMEM((1024, 256), bf16),
            pltpu.VMEM((2048, 128), bf16),
            pltpu.VMEM((128, HEADS * CELLS), f32),
            pltpu.VMEM((128, HEADS * CELLS), bf16),
            pltpu.VMEM((128, ATT), bf16),
            pltpu.VMEM((128, D), f32),
            pltpu.VMEM((128, D), f32),
            pltpu.VMEM((128, D), bf16),
            pltpu.VMEM((128, ATT), bf16),
            pltpu.VMEM((128, 3 * ATT), bf16),
            pltpu.VMEM((16, D), f32),
        ],
        compiler_params=pltpu.CompilerParams(vmem_limit_bytes=24 * MIB),
        cost_estimate=pl.CostEstimate(
            flops=1_500_000_000, bytes_accessed=6_000_000, transcendentals=150_000
        ),
        name="main",
    )(own, lon, lat, dia, *params)


def final_kernel(own, lon, lat, dia, out):
    rows = jnp.concatenate([own[...], lon[...], lat[...], dia[...]], axis=0)
    row, col, _ = sorted_place(iota((128, 128), 1))
    token_place = onehot(iota((128, 128), 0) == row * 8 + col)
    out[...] = mm(token_place, rows).reshape(16, 8, D).astype(bf16)


def final(own, lon, lat, dia):
    return pl.pallas_call(
        final_kernel,
        out_shape=jax.ShapeDtypeStruct((16, 8, D), bf16),
        compiler_params=pltpu.CompilerParams(vmem_limit_bytes=8 * MIB),
        name="final",
    )(own, lon, lat, dia)


def shift_by(block, lat_step, lon_step):
    lats, lons = lax.axis_size("lat"), lax.axis_size("lon")
    route = [
        (j * lats + i, ((j + lon_step) % lons) * lats + (i + lat_step) % lats)
        for j in range(lons)
        for i in range(lats)
    ]
    return lax.ppermute(block, ("lon", "lat"), route)


def shards(
    tokens,
    labels,
    w_qkv,
    w_proj,
    logit_scale,
    bias_table,
    norm_gain,
    norm_shift,
    merge_gain,
    cotangent,
):
    own, lon, lat, dia = pack(tokens, labels.T, cotangent, places())
    lon = shift_by(lon, 0, 1)
    dia = shift_by(dia, -1, 1)
    lat = shift_by(lat, -1, 0)
    ebias, temper = prep(bias_table, logit_scale.reshape(1, HEADS))
    own, lon, lat, dia = main(
        own,
        lon,
        lat,
        dia,
        ebias,
        temper,
        w_qkv,
        w_proj,
        norm_gain.reshape(1, D),
        norm_shift.reshape(1, D),
        merge_gain.reshape(1, 4 * D),
    )
    lon = shift_by(lon, 0, -1)
    dia = shift_by(dia, 1, -1)
    lat = shift_by(lat, 1, 0)
    return final(own, lon, lat, dia)


def solution(mesh):
    placed = (
        P("lat", "lon", None),
        P("lat", "lon"),
        P(),
        P(),
        P(),
        P(),
        P(),
        P(),
        P(),
        P("lat", "lon", None),
    )
    return jax.shard_map(
        shards, mesh=mesh, in_specs=placed, out_specs=P("lat", "lon", None), check_vma=False
    )
```

time: 60.8 us -> 41.9 us (0.69)
  the two profiles are of different devices: /device:TPU:4 before, /device:TPU:1 now
where the time goes in v2:
time: 41.9 us; the launch traced here: 41.6 us
  starting transfers between devices  26.9 us (64%)
  Pallas kernels  7.02 us (17%)
  waiting for transfers between devices  6.68 us (16%)
  local copies, waits for them, and re-layouts  0.87 us (2%)
    ppermute x6, starting transfers between devices, shift_by(): return lax.ppermute(block, ('lon', 'lat'), route)  26.9 us
    ppermute x6, waiting for transfers between devices, shift_by(): return lax.ppermute(block, ('lon', 'lat'), route)  6.68 us
    pallas_call x1, Pallas kernels, main(): pl.pallas_call(main_kernel, out_shape=[jax.ShapeDtypeStruct((n, D), bf16)...  4.75 us
    pallas_call x1, Pallas kernels, final(): pl.pallas_call(final_kernel, out_shape=jax.ShapeDtypeStruct((16, 8, D), b...  0.93 us
    unnamed x20, local copies, waits for them, and re-layouts  0.87 us
  transfers between devices with their start and end apart: 6, of which 2 were waited for; matrix products, arithmetic and copies ran while one was open for 0% of the time, Pallas kernels for 2%

profile of v2, /device:TPU:1, one launch (start us, length us, event | category | flops | bytes accessed | tf_op | source)
XLA Modules:
  0.0 41.6 jit_solution(16052066036609241438)
XLA Ops:
  0.0 0.0 copy-start.3
  0.0 0.0 copy-start.6
  0.0 0.0 copy-start.2
  0.0 0.2 places.1
  0.2 0.7 %copy-done.3 = bf16[8,4,4096]{2,1,0:T(4,128)(2,1)S(1)} copy-done((bf16[8,4,4096]{2,1,0:T(4,128)(2,1)S(1)}, bf16[8,4,4096]{2,1,0:T(4,128)(2,1)}, u32[]{:S(2)}) %copy-start.3) | copy-done | bytes 262168
  1.0 0.0 copy-done.6
  1.0 0.1 copy-done.2
  1.0 0.0 copy-start.4
  1.0 0.0 copy-start.9
  1.1 0.0 copy-start
  1.1 0.0 copy-start.1
  1.1 0.0 copy-start.5
  1.1 0.0 copy-start.7
  1.1 0.0 copy-start.8
  1.1 0.3 pack.1
  1.4 5.2 %collective-permute-start = (bf16[48,2176]{1,0:T(8,128)(2,1)S(1)}, bf16[48,2176]{1,0:T(8,128)(2,1)S(1)}, u32[]{:S(2)}, u32[]{:S(2)}) collective-permute-start(bf16[48,2176]{1,0:T(8,128)(2,1)S(1)} %get-tuple-element.24), channel_id=1, source_target_pairs={{0,8},{1,9},{2,10},{3,11},{4,12},{5,13},{6,14},{7,15},{8,16},{9,17... | collective-permute-start | bytes 626696 | tf_op jit(solution)/shard_map/ppermute | solution.py:449
  6.6 5.6 %collective-permute-start.1 = (bf16[16,2176]{1,0:T(8,128)(2,1)S(1)}, bf16[16,2176]{1,0:T(8,128)(2,1)S(1)}, u32[]{:S(2)}, u32[]{:S(2)}) collective-permute-start(bf16[16,2176]{1,0:T(8,128)(2,1)S(1)} %get-tuple-element.25), channel_id=1, source_target_pairs={{0,7},{1,0},{2,1},{3,2},{4,3},{5,4},{6,5},{7,6},{8,15},{9,8},{10,9... | collective-permute-start | bytes 208904 | tf_op jit(solution)/shard_map/ppermute | solution.py:449
  12.2 2.2 %collective-permute-start.2 = (bf16[16,2176]{1,0:T(8,128)(2,1)S(1)}, bf16[16,2176]{1,0:T(8,128)(2,1)S(1)}, u32[]{:S(2)}, u32[]{:S(2)}) collective-permute-start(bf16[16,2176]{1,0:T(8,128)(2,1)S(1)} %get-tuple-element.26), channel_id=1, source_target_pairs={{0,15},{1,8},{2,9},{3,10},{4,11},{5,12},{6,13},{7,14},{8,23},{9,16... | collective-permute-start | bytes 208904 | tf_op jit(solution)/shard_map/ppermute | solution.py:449
  14.4 0.0 copy-done.4
  14.4 0.0 copy-done.9
  14.4 0.8 %prep.1 = (f32[64,1024]{1,0:T(8,128)S(1)}, f32[1,512]{1,0:T(1,128)S(1)}) custom-call(f32[16,225]{1,0:T(8,128)S(1)} %copy-done.4, f32[1,16]{1,0:T(1,128)S(1)} %bitcast.9), custom_call_target="tpu_custom_call" | custom-call | flops 100000000 | bytes 400000 | tf_op jit(solution)/shard_map/prep/pallas_call | solution.py:172
  15.2 0.0 collective-permute-done.1.lat
  15.2 4.0 %collective-permute-done.2.dia = bf16[16,2176]{1,0:T(8,128)(2,1)S(1)} collective-permute-done((bf16[16,2176]{1,0:T(8,128)(2,1)S(1)}, bf16[16,2176]{1,0:T(8,128)(2,1)S(1)}, u32[]{:S(2)}, u32[]{:S(2)}) %collective-permute-start.2) | collective-permute-done | bytes 69664 | tf_op jit(solution)/shard_map/ppermute | solution.py:449
  19.3 0.0 collective-permute-done.lon
  19.3 0.0 copy-done
  19.3 0.0 copy-done.1
  19.3 0.0 copy-done.5
  19.3 0.0 copy-done.7
  19.3 0.0 copy-done.8
  19.3 4.8 %main.1 = (bf16[48,1024]{1,0:T(8,128)(2,1)S(1)}, bf16[48,1024]{1,0:T(8,128)(2,1)S(1)}, bf16[16,1024]{1,0:T(8,128)(2,1)S(1)}, bf16[16,1024]{1,0:T(8,128)(2,1)S(1)}) custom-call(bf16[48,2176]{1,0:T(8,128)(2,1)S(1)} %get-tuple-element.23.own, bf16[48,2176]{1,0:T(8,128)(2,1)S(1)} %collective-permute-done.lon, bf16[16,2176]{1,0:T(8,128)(2,1)S(1)} %collective-permute-done.1.lat, ...), custom_call_target="tpu_custom_call" | custom-call | flops 1500000000 | bytes 6000000 | tf_op jit(solution)/shard_map/main/pallas_call | solution.py:397
  24.1 5.2 %collective-permute-start.3 = (bf16[48,1024]{1,0:T(8,128)(2,1)S(1)}, bf16[48,1024]{1,0:T(8,128)(2,1)S(1)}, u32[]{:S(2)}, u32[]{:S(2)}) collective-permute-start(bf16[48,1024]{1,0:T(8,128)(2,1)S(1)} %get-tuple-element.30), channel_id=1, source_target_pairs={{0,504},{1,505},{2,506},{3,507},{4,508},{5,509},{6,510},{7,511},{8... | collective-permute-start | bytes 294920 | tf_op jit(solution)/shard_map/ppermute | solution.py:449
  29.3 3.1 %collective-permute-start.4 = (bf16[16,1024]{1,0:T(8,128)(2,1)S(1)}, bf16[16,1024]{1,0:T(8,128)(2,1)S(1)}, u32[]{:S(2)}, u32[]{:S(2)}) collective-permute-start(bf16[16,1024]{1,0:T(8,128)(2,1)S(1)} %get-tuple-element.31), channel_id=1, source_target_pairs={{0,1},{1,2},{2,3},{3,4},{4,5},{5,6},{6,7},{7,0},{8,9},{9,10},{10,1... | collective-permute-start | bytes 98312 | tf_op jit(solution)/shard_map/ppermute | solution.py:449
  32.4 5.6 %collective-permute-start.5 = (bf16[16,1024]{1,0:T(8,128)(2,1)S(1)}, bf16[16,1024]{1,0:T(8,128)(2,1)S(1)}, u32[]{:S(2)}, u32[]{:S(2)}) collective-permute-start(bf16[16,1024]{1,0:T(8,128)(2,1)S(1)} %get-tuple-element.32), channel_id=1, source_target_pairs={{0,505},{1,506},{2,507},{3,508},{4,509},{5,510},{6,511},{7,504},{8... | collective-permute-start | bytes 98312 | tf_op jit(solution)/shard_map/ppermute | solution.py:449
  38.1 0.0 collective-permute-done.4.lat
  38.1 2.6 %collective-permute-done.5.dia = bf16[16,1024]{1,0:T(8,128)(2,1)S(1)} collective-permute-done((bf16[16,1024]{1,0:T(8,128)(2,1)S(1)}, bf16[16,1024]{1,0:T(8,128)(2,1)S(1)}, u32[]{:S(2)}, u32[]{:S(2)}) %collective-permute-start.5) | collective-permute-done | bytes 32800 | tf_op jit(solution)/shard_map/ppermute | solution.py:449
  40.7 0.0 collective-permute-done.3.lon
  40.7 0.9 %final.1 = bf16[16,8,1024]{2,1,0:T(8,128)(2,1)} custom-call(bf16[48,1024]{1,0:T(8,128)(2,1)S(1)} %get-tuple-element.29.own, bf16[48,1024]{1,0:T(8,128)(2,1)S(1)} %collective-permute-done.3.lon, bf16[16,1024]{1,0:T(8,128)(2,1)S(1)} %collective-permute-done.4.lat, bf16[16,1024]{1,0:T(8,128)(2,1)S(1)} %collective-permute-done.5.dia), custom_call_target="tpu_custom_call" | custom-call | tf_op jit(solution)/shard_map/final/pallas_call | solution.py:434
Async XLA Ops:
  0.0 0.9 %copy-start.3 = (bf16[8,4,4096]{2,1,0:T(4,128)(2,1)S(1)}, bf16[8,4,4096]{2,1,0:T(4,128)(2,1)}, u32[]{:S(2)}) copy-start(bf16[8,4,4096]{2,1,0:T(4,128)(2,1)} %cot.1) | copy-start | bytes 786436
  0.0 1.0 %copy-start.6 = (s32[16,8]{0,1:T(8,128)S(1)}, s32[16,8]{0,1:T(8,128)}, u32[]{:S(2)}) copy-start(s32[16,8]{0,1:T(8,128)} %param.11) | copy-start | bytes 1540
  0.0 1.0 %copy-start.2 = (bf16[16,8,1024]{2,1,0:T(8,128)(2,1)S(1)}, bf16[16,8,1024]{2,1,0:T(8,128)(2,1)}, u32[]{:S(2)}) copy-start(bf16[16,8,1024]{2,1,0:T(8,128)(2,1)} %tokens.1) | copy-start | bytes 786436
  1.0 13.3 %copy-start.4 = (f32[16,225]{1,0:T(8,128)S(1)}, f32[16,225]{1,0:T(8,128)}, u32[]{:S(2)}) copy-start(f32[16,225]{1,0:T(8,128)} %table.1) | copy-start | bytes 43204
  1.0 13.3 %copy-start.9 = (f32[16]{0:T(128)S(1)}, f32[16]{0:T(128)}, u32[]{:S(2)}) copy-start(f32[16]{0:T(128)} %param.14) | copy-start | bytes 196
  1.1 18.2 %copy-start = (bf16[1024,1536]{1,0:T(8,128)(2,1)S(1)}, bf16[1024,1536]{1,0:T(8,128)(2,1)}, u32[]{:S(2)}) copy-start(bf16[1024,1536]{1,0:T(8,128)(2,1)} %w_qkv.1) | copy-start | bytes 9437188
  1.1 18.2 %copy-start.1 = (bf16[512,1024]{1,0:T(8,128)(2,1)S(1)}, bf16[512,1024]{1,0:T(8,128)(2,1)}, u32[]{:S(2)}) copy-start(bf16[512,1024]{1,0:T(8,128)(2,1)} %w_proj.1) | copy-start | bytes 3145732
  1.1 18.2 %copy-start.5 = (f32[4096]{0:T(1024)S(1)}, f32[4096]{0:T(1024)}, u32[]{:S(2)}) copy-start(f32[4096]{0:T(1024)} %param.18) | copy-start | bytes 49156
  1.1 18.2 %copy-start.7 = (f32[1024]{0:T(1024)S(1)}, f32[1024]{0:T(1024)}, u32[]{:S(2)}) copy-start(f32[1024]{0:T(1024)} %param.16) | copy-start | bytes 12292
  1.1 18.2 %copy-start.8 = (f32[1024]{0:T(1024)S(1)}, f32[1024]{0:T(1024)}, u32[]{:S(2)}) copy-start(f32[1024]{0:T(1024)} %param.17) | copy-start | bytes 12292
  1.4 17.9 %collective-permute-start = (bf16[48,2176]{1,0:T(8,128)(2,1)S(1)}, bf16[48,2176]{1,0:T(8,128)(2,1)S(1)}, u32[]{:S(2)}, u32[]{:S(2)}) collective-permute-start(bf16[48,2176]{1,0:T(8,128)(2,1)S(1)} %get-tuple-element.24), channel_id=1, source_target_pairs={{0,8},{1,9},{2,10},{3,11},{4,12},{5,13},{6,14},{7,15},{8,16},{9,17... | collective-permute-start | bytes 626696 | tf_op jit(solution)/shard_map/ppermute | solution.py:449
  6.6 8.6 %collective-permute-start.1 = (bf16[16,2176]{1,0:T(8,128)(2,1)S(1)}, bf16[16,2176]{1,0:T(8,128)(2,1)S(1)}, u32[]{:S(2)}, u32[]{:S(2)}) collective-permute-start(bf16[16,2176]{1,0:T(8,128)(2,1)S(1)} %get-tuple-element.25), channel_id=1, source_target_pairs={{0,7},{1,0},{2,1},{3,2},{4,3},{5,4},{6,5},{7,6},{8,15},{9,8},{10,9... | collective-permute-start | bytes 208904 | tf_op jit(solution)/shard_map/ppermute | solution.py:449
  12.2 7.1 %collective-permute-start.2 = (bf16[16,2176]{1,0:T(8,128)(2,1)S(1)}, bf16[16,2176]{1,0:T(8,128)(2,1)S(1)}, u32[]{:S(2)}, u32[]{:S(2)}) collective-permute-start(bf16[16,2176]{1,0:T(8,128)(2,1)S(1)} %get-tuple-element.26), channel_id=1, source_target_pairs={{0,15},{1,8},{2,9},{3,10},{4,11},{5,12},{6,13},{7,14},{8,23},{9,16... | collective-permute-start | bytes 208904 | tf_op jit(solution)/shard_map/ppermute | solution.py:449
  24.1 16.6 %collective-permute-start.3 = (bf16[48,1024]{1,0:T(8,128)(2,1)S(1)}, bf16[48,1024]{1,0:T(8,128)(2,1)S(1)}, u32[]{:S(2)}, u32[]{:S(2)}) collective-permute-start(bf16[48,1024]{1,0:T(8,128)(2,1)S(1)} %get-tuple-element.30), channel_id=1, source_target_pairs={{0,504},{1,505},{2,506},{3,507},{4,508},{5,509},{6,510},{7,511},{8... | collective-permute-start | bytes 294920 | tf_op jit(solution)/shard_map/ppermute | solution.py:449
  29.3 8.7 %collective-permute-start.4 = (bf16[16,1024]{1,0:T(8,128)(2,1)S(1)}, bf16[16,1024]{1,0:T(8,128)(2,1)S(1)}, u32[]{:S(2)}, u32[]{:S(2)}) collective-permute-start(bf16[16,1024]{1,0:T(8,128)(2,1)S(1)} %get-tuple-element.31), channel_id=1, source_target_pairs={{0,1},{1,2},{2,3},{3,4},{4,5},{5,6},{6,7},{7,0},{8,9},{9,10},{10,1... | collective-permute-start | bytes 98312 | tf_op jit(solution)/shard_map/ppermute | solution.py:449
  32.4 8.2 %collective-permute-start.5 = (bf16[16,1024]{1,0:T(8,128)(2,1)S(1)}, bf16[16,1024]{1,0:T(8,128)(2,1)S(1)}, u32[]{:S(2)}, u32[]{:S(2)}) collective-permute-start(bf16[16,1024]{1,0:T(8,128)(2,1)S(1)} %get-tuple-element.32), channel_id=1, source_target_pairs={{0,505},{1,506},{2,507},{3,508},{4,509},{5,510},{6,511},{7,504},{8... | collective-permute-start | bytes 98312 | tf_op jit(solution)/shard_map/ppermute | solution.py:449

commit v3 on v2

--- a/solution.py
+++ b/solution.py
@@ -28,8 +28,8 @@
     quad = n // 16
     s = (n // 4) % 4
     g = n % 4
-    row = jnp.where(quad < 6, 4 + 4 * (quad % 3), 0) + 2 * (g // 2) + s % 2
-    col = jnp.where((quad // 3 == 1) | (quad == 7), 4, 0) + 2 * (g % 2) + s // 2
+    row = 4 * (quad % 4) + 2 * (g // 2) + s % 2
+    col = 4 * (quad // 4) + 2 * (g % 2) + s // 2
     return row, col, s
 
 
@@ -92,9 +92,9 @@
 
 
 def pack_kernel(
-    token_sort, cot_sort, label_row, label_col, tokens, labels, cot, own, lon, lat, dia, cot_rows
+    token_sort, cot_sort, label_row, label_col, tokens, labels, cot, own, lon, cot_rows
 ):
-    outs = ((own, 0, 48), (lon, 48, 96), (lat, 96, 112), (dia, 112, 128))
+    outs = ((own, 0, 64), (lon, 64, 128))
     moved = mm(token_sort[...], tokens[...].reshape(128, D)).astype(bf16)
     for ref, lo, hi in outs:
         ref[:, 0:D] = moved[lo:hi]
@@ -116,7 +116,7 @@
 
 
 def pack(tokens, labels, cot, sorts):
-    shapes = [jax.ShapeDtypeStruct((n, WIDE), bf16) for n in (48, 48, 16, 16)]
+    shapes = [jax.ShapeDtypeStruct((64, WIDE), bf16)] * 2
     return pl.pallas_call(
         pack_kernel,
         out_shape=shapes,
@@ -125,6 +125,22 @@
         cost_estimate=BUSY,
         name="pack",
     )(*sorts, tokens, labels, cot)
+
+
+def strips_kernel(own, lon, top, bottom):
+    top[0:16, :] = lon[0:16, :]
+    top[16:32, :] = own[0:16, :]
+    bottom[0:16, :] = lon[48:64, :]
+    bottom[16:32, :] = own[48:64, :]
+
+
+def strips(own, lon):
+    return pl.pallas_call(
+        strips_kernel,
+        out_shape=[jax.ShapeDtypeStruct((32, WIDE), bf16)] * 2,
+        compiler_params=pltpu.CompilerParams(vmem_limit_bytes=4 * MIB),
+        name="strips",
+    )(own, lon)
 
 
 def relative_bias(table, natural, ebias):
@@ -198,51 +214,29 @@
     return jnp.sum(value, axis=0, keepdims=True)
 
 
-def main_kernel(
-    own,
-    lon,
-    lat,
-    dia,
-    ebias,
-    temper,
-    w_qkv,
-    w_proj,
-    gain,
-    shift,
-    merge,
-    out_own,
-    out_lon,
-    out_lat,
-    out_dia,
-    x_s,
-    qkv_s,
-    unit_s,
-    inv_s,
-    unit16_s,
-    seg_s,
-    qbd_s,
-    prob_s,
-    prob16_s,
-    att_s,
-    proj_s,
-    mixed_s,
-    gproj_s,
-    ga_s,
-    gpack_s,
-    mgain,
-):
-    quads = (
-        (lon, out_lon, 0),
-        (own, out_own, 0),
-        (lon, out_lon, 16),
-        (own, out_own, 16),
-        (lon, out_lon, 32),
-        (own, out_own, 32),
-        (dia, out_dia, 0),
-        (lat, out_lat, 0),
-    )
-    pairs = [(w, b) for w in range(2) for b in range(BLOCKS)]
-    for n, (ref, _, lo) in enumerate(quads):
+def windows(quads, kept, emit, params, scratch):
+    ebias, temper, w_qkv, w_proj, gain, shift, merge = params
+    (
+        x_s,
+        qkv_s,
+        unit_s,
+        inv_s,
+        unit16_s,
+        seg_s,
+        qbd_s,
+        prob_s,
+        prob16_s,
+        att_s,
+        proj_s,
+        mixed_s,
+        gproj_s,
+        ga_s,
+        gpack_s,
+        mgain,
+    ) = scratch
+    count = 16 * len(quads)
+    pairs = [(w, b) for w in range(count // 64) for b in range(BLOCKS)]
+    for n, (ref, lo) in enumerate(quads):
         x_s[16 * n : 16 * n + 16, :] = ref[lo : lo + 16, 0:D]
     for n in range(6):
         cols = slice(256 * n, 256 * n + 256)
@@ -255,8 +249,8 @@
 
     def store_halves(n, value):
         high, low = halves(value)
-        seg_s[128 * n : 128 * n + 128, 0:128] = high
-        seg_s[128 * n : 128 * n + 128, 128:256] = low
+        seg_s[count * n : count * n + count, 0:128] = high
+        seg_s[count * n : count * n + count, 128:256] = low
 
     def block_diagonal(value):
         return jnp.concatenate([value * head_mask[h] for h in range(4)], axis=0)
@@ -273,7 +267,7 @@
     squares = mm(seg_s[...], seg)
     for n in range(8):
         cols = slice(128 * n, 128 * n + 128)
-        inv = lax.rsqrt(squares[cols] + unit_eps)
+        inv = lax.rsqrt(squares[count * n : count * n + count] + unit_eps)
         unit = qkv_s[:, cols].astype(f32) * inv
         inv_s[:, cols] = inv
         unit_s[:, cols] = unit
@@ -283,11 +277,11 @@
 
     code_lane = iota((16, 128), 1)
     allowed = []
-    for w in range(2):
+    for w in range(count // 64):
         hot = jnp.concatenate(
             [
                 onehot(ref[lo : lo + 16, 2 * D :].astype(f32).astype(jnp.int32) == code_lane)
-                for ref, _, lo in quads[4 * w : 4 * w + 4]
+                for ref, lo in quads[4 * w : 4 * w + 4]
             ],
             axis=0,
         )
@@ -312,10 +306,10 @@
         cols = slice(256 * n, 256 * n + 256)
         proj_s[:, cols] = mm(att_s[...], w_proj[:, cols])
 
-    spans = [slice(16 * n, 16 * n + 16) for n in range(8)]
+    spans = [slice(16 * n, 16 * n + 16) for n in range(len(quads))]
 
     def ghat_of(n):
-        ref, _, lo = quads[n]
+        ref, lo = quads[n]
         return ref[lo : lo + 16, D : 2 * D].astype(f32) * mgain[...]
 
     for s in range(4):
@@ -383,70 +377,119 @@
     along = mm(seg_s[...], seg)
     for n in range(8):
         cols = slice(128 * n, 128 * n + 128)
-        grad = inv_s[:, cols] * (proj_s[:, cols] - unit_s[:, cols] * along[cols])
+        grad = inv_s[:, cols] * (proj_s[:, cols] - unit_s[:, cols] * along[count * n : count * n + count])
         gpack_s[:, cols] = grad.astype(bf16)
 
     for n in range(4):
         cols = slice(256 * n, 256 * n + 256)
-        total = (mixed_s[:, cols] + mm_nt(gpack_s[...], w_qkv[cols, :])).astype(bf16)
-        for m, (_, ref, lo) in enumerate(quads):
-            ref[lo : lo + 16, cols] = total[16 * m : 16 * m + 16]
-
-
-def main(own, lon, lat, dia, *params):
-    return pl.pallas_call(
-        main_kernel,
-        out_shape=[jax.ShapeDtypeStruct((n, D), bf16) for n in (48, 48, 16, 16)],
-        scratch_shapes=[
-            pltpu.VMEM((128, D), bf16),
-            pltpu.VMEM((128, 3 * ATT), bf16),
-            pltpu.VMEM((128, 2 * ATT), f32),
-            pltpu.VMEM((128, 2 * ATT), f32),
-            pltpu.VMEM((128, 2 * ATT), bf16),
-            pltpu.VMEM((1024, 256), bf16),
-            pltpu.VMEM((2048, 128), bf16),
-            pltpu.VMEM((128, HEADS * CELLS), f32),
-            pltpu.VMEM((128, HEADS * CELLS), bf16),
-            pltpu.VMEM((128, ATT), bf16),
-            pltpu.VMEM((128, D), f32),
-            pltpu.VMEM((128, D), f32),
-            pltpu.VMEM((128, D), bf16),
-            pltpu.VMEM((128, ATT), bf16),
-            pltpu.VMEM((128, 3 * ATT), bf16),
-            pltpu.VMEM((16, D), f32),
-        ],
+        total = mixed_s[kept, cols] + mm_nt(gpack_s[kept, :], w_qkv[cols, :])
+        emit(cols, total.astype(bf16))
+
+
+def scratch_for(count):
+    return [
+        pltpu.VMEM((count, D), bf16),
+        pltpu.VMEM((count, 3 * ATT), bf16),
+        pltpu.VMEM((count, 2 * ATT), f32),
+        pltpu.VMEM((count, 2 * ATT), f32),
+        pltpu.VMEM((count, 2 * ATT), bf16),
+        pltpu.VMEM((8 * count, 256), bf16),
+        pltpu.VMEM((16 * count, 128), bf16),
+        pltpu.VMEM((count, HEADS * CELLS), f32),
+        pltpu.VMEM((count, HEADS * CELLS), bf16),
+        pltpu.VMEM((count, ATT), bf16),
+        pltpu.VMEM((count, D), f32),
+        pltpu.VMEM((count, D), f32),
+        pltpu.VMEM((count, D), bf16),
+        pltpu.VMEM((count, ATT), bf16),
+        pltpu.VMEM((count, 3 * ATT), bf16),
+        pltpu.VMEM((16, D), f32),
+    ]
+
+
+def inner_kernel(own, lon, *refs):
+    params, (out_own, out_lon), scratch = refs[:7], refs[7:9], refs[9:]
+    quads = ((lon, 16), (own, 16), (lon, 32), (own, 32))
+
+    def emit(cols, total):
+        out_lon[0:16, cols] = total[0:16]
+        out_own[0:16, cols] = total[16:32]
+        out_lon[16:32, cols] = total[32:48]
+        out_own[16:32, cols] = total[48:64]
+
+    windows(quads, slice(0, 64), emit, params, scratch)
+
+
+def inner(own, lon, params):
+    return pl.pallas_call(
+        inner_kernel,
+        out_shape=[jax.ShapeDtypeStruct((32, D), bf16)] * 2,
+        scratch_shapes=scratch_for(64),
+        compiler_params=pltpu.CompilerParams(vmem_limit_bytes=16 * MIB),
+        cost_estimate=pl.CostEstimate(
+            flops=3_000_000_000, bytes_accessed=6_000_000, transcendentals=150_000
+        ),
+        name="inner",
+    )(own, lon, *params)
+
+
+def outer_kernel(own, lon, above, below, in_own, in_lon, *refs):
+    params, (out_own, out_lon), scratch = refs[:7], refs[7:9], refs[9:]
+    quads = (
+        (above, 0),
+        (above, 16),
+        (lon, 0),
+        (own, 0),
+        (lon, 48),
+        (own, 48),
+        (below, 0),
+        (below, 16),
+    )
+    out_own[16:48, :] = in_own[...]
+    out_lon[16:48, :] = in_lon[...]
+
+    def emit(cols, total):
+        out_lon[0:16, cols] = total[0:16]
+        out_own[0:16, cols] = total[16:32]
+        out_lon[48:64, cols] = total[32:48]
+        out_own[48:64, cols] = total[48:64]
+
+    windows(quads, slice(32, 96), emit, params, scratch)
+
+
+def outer(own, lon, above, below, in_own, in_lon, params):
+    return pl.pallas_call(
+        outer_kernel,
+        out_shape=[jax.ShapeDtypeStruct((64, D), bf16)] * 2,
+        scratch_shapes=scratch_for(128),
         compiler_params=pltpu.CompilerParams(vmem_limit_bytes=24 * MIB),
         cost_estimate=pl.CostEstimate(
-            flops=1_500_000_000, bytes_accessed=6_000_000, transcendentals=150_000
+            flops=3_000_000_000, bytes_accessed=6_000_000, transcendentals=150_000
         ),
-        name="main",
-    )(own, lon, lat, dia, *params)
-
-
-def final_kernel(own, lon, lat, dia, out):
-    rows = jnp.concatenate([own[...], lon[...], lat[...], dia[...]], axis=0)
+        name="outer",
+    )(own, lon, above, below, in_own, in_lon, *params)
+
+
+def final_kernel(own, lon, out):
+    rows = jnp.concatenate([own[...], lon[...]], axis=0)
     row, col, _ = sorted_place(iota((128, 128), 1))
     token_place = onehot(iota((128, 128), 0) == row * 8 + col)
     out[...] = mm(token_place, rows).reshape(16, 8, D).astype(bf16)
 
 
-def final(own, lon, lat, dia):
+def final(own, lon):
     return pl.pallas_call(
         final_kernel,
         out_shape=jax.ShapeDtypeStruct((16, 8, D), bf16),
         compiler_params=pltpu.CompilerParams(vmem_limit_bytes=8 * MIB),
         name="final",
-    )(own, lon, lat, dia)
-
-
-def shift_by(block, lat_step, lon_step):
-    lats, lons = lax.axis_size("lat"), lax.axis_size("lon")
-    route = [
-        (j * lats + i, ((j + lon_step) % lons) * lats + (i + lat_step) % lats)
-        for j in range(lons)
-        for i in range(lats)
-    ]
-    return lax.ppermute(block, ("lon", "lat"), route)
+    )(own, lon)
+
+
+def passed_along(block, axis, distance):
+    count = lax.axis_size(axis)
+    route = [(i, (i + distance) % count) for i in range(count)]
+    return lax.ppermute(block, axis, route)
 
 
 def shards(
@@ -461,16 +504,10 @@
     merge_gain,
     cotangent,
 ):
-    own, lon, lat, dia = pack(tokens, labels.T, cotangent, places())
-    lon = shift_by(lon, 0, 1)
-    dia = shift_by(dia, -1, 1)
-    lat = shift_by(lat, -1, 0)
+    own, lon = pack(tokens, labels.T, cotangent, places())
+    lon = passed_along(lon, "lon", 1)
     ebias, temper = prep(bias_table, logit_scale.reshape(1, HEADS))
-    own, lon, lat, dia = main(
-        own,
-        lon,
-        lat,
-        dia,
+    params = (
         ebias,
         temper,
         w_qkv,
@@ -479,10 +516,13 @@
         norm_shift.reshape(1, D),
         merge_gain.reshape(1, 4 * D),
     )
-    lon = shift_by(lon, 0, -1)
-    dia = shift_by(dia, 1, -1)
-    lat = shift_by(lat, 1, 0)
-    return final(own, lon, lat, dia)
+    top, bottom = strips(own, lon)
+    below = passed_along(top, "lat", -1)
+    above = passed_along(bottom, "lat", 1)
+    in_own, in_lon = inner(own, lon, params)
+    own, lon = outer(own, lon, above, below, in_own, in_lon, params)
+    lon = passed_along(lon, "lon", -1)
+    return final(own, lon)
 
 
 def solution(mesh):

time: 41.9 us -> 41.7 us (level)
  Pallas kernels: 7.02 us -> 11.1 us
  starting transfers between devices: 26.9 us -> 24.4 us
  waiting for transfers between devices: 6.68 us -> 5.02 us
    pallas_call x1 -> x3, Pallas kernels: 4.75 us -> 8.86 us  [the longest x1 4.67 us: outer(): pl.pallas_call(outer_kernel, out_shape=[jax.ShapeDtypeStruct((64, D), bf1...]
    ppermute x6 -> x4, starting transfers between devices: 26.9 us -> 24.4 us  [passed_along(): return lax.ppermute(block, axis, route)]
    ppermute x6 -> x4, waiting for transfers between devices: 6.68 us -> 5.02 us  [passed_along(): return lax.ppermute(block, axis, route)]
  transfers between devices with their start and end apart: 6 -> 4, of which waited for: 2 -> 2; matrix products, arithmetic and copies ran while one was open for 0% -> 0% of each run, Pallas kernels for 2% -> 12%
where the time goes in v3:
time: 41.7 us; the launch traced here: 41.5 us
  starting transfers between devices  24.4 us (59%)
  Pallas kernels  11.1 us (27%)
  waiting for transfers between devices  5.02 us (12%)
  local copies, waits for them, and re-layouts  0.88 us (2%)
    ppermute x4, starting transfers between devices, passed_along(): return lax.ppermute(block, axis, route)  24.4 us
    ppermute x4, waiting for transfers between devices, passed_along(): return lax.ppermute(block, axis, route)  5.02 us
    pallas_call x1, Pallas kernels, outer(): pl.pallas_call(outer_kernel, out_shape=[jax.ShapeDtypeStruct((64, D), bf1...  4.67 us
    pallas_call x1, Pallas kernels, inner(): pl.pallas_call(inner_kernel, out_shape=[jax.ShapeDtypeStruct((32, D), bf1...  4.16 us
    pallas_call x1, Pallas kernels, final(): pl.pallas_call(final_kernel, out_shape=jax.ShapeDtypeStruct((16, 8, D), b...  0.93 us
    unnamed x20, local copies, waits for them, and re-layouts  0.88 us
  transfers between devices with their start and end apart: 4, of which 2 were waited for; matrix products, arithmetic and copies ran while one was open for 0% of the time, Pallas kernels for 12%

profile of v3, /device:TPU:1, one launch (start us, length us, event | category | flops | bytes accessed | tf_op | source)
XLA Modules:
  0.0 41.5 jit_solution(8399139595942711165)
XLA Ops:
  0.0 0.0 copy-start.3
  0.0 0.0 copy-start.6
  0.0 0.0 copy-start.2
  0.0 0.2 places.1
  0.2 0.7 %copy-done.3 = bf16[8,4,4096]{2,1,0:T(4,128)(2,1)S(1)} copy-done((bf16[8,4,4096]{2,1,0:T(4,128)(2,1)S(1)}, bf16[8,4,4096]{2,1,0:T(4,128)(2,1)}, u32[]{:S(2)}) %copy-start.3) | copy-done | bytes 262168
  1.0 0.0 copy-done.6
  1.0 0.1 copy-done.2
  1.0 0.0 copy-start.4
  1.0 0.0 copy-start.9
  1.1 0.0 copy-start
  1.1 0.0 copy-start.1
  1.1 0.0 copy-start.5
  1.1 0.0 copy-start.7
  1.1 0.0 copy-start.8
  1.1 0.3 pack.1
  1.4 5.2 %collective-permute-start = (bf16[64,2176]{1,0:T(8,128)(2,1)S(1)}, bf16[64,2176]{1,0:T(8,128)(2,1)S(1)}, u32[]{:S(2)}, u32[]{:S(2)}) collective-permute-start(bf16[64,2176]{1,0:T(8,128)(2,1)S(1)} %get-tuple-element.24), channel_id=1, source_target_pairs={{0,8},{8,16},{16,24},{24,32},{32,40},{40,48},{48,56},{56,64},{64,7... | collective-permute-start | bytes 835592 | tf_op jit(solution)/shard_map/ppermute | solution.py:492
  6.6 0.0 copy-done.4
  6.6 0.0 copy-done.9
  6.6 0.8 %prep.1 = (f32[64,1024]{1,0:T(8,128)S(1)}, f32[1,512]{1,0:T(1,128)S(1)}) custom-call(f32[16,225]{1,0:T(8,128)S(1)} %copy-done.4, f32[1,16]{1,0:T(1,128)S(1)} %bitcast.12), custom_call_target="tpu_custom_call" | custom-call | flops 100000000 | bytes 400000 | tf_op jit(solution)/shard_map/prep/pallas_call | solution.py:188
  7.5 4.0 %collective-permute-done.lon = bf16[64,2176]{1,0:T(8,128)(2,1)S(1)} collective-permute-done((bf16[64,2176]{1,0:T(8,128)(2,1)S(1)}, bf16[64,2176]{1,0:T(8,128)(2,1)S(1)}, u32[]{:S(2)}, u32[]{:S(2)}) %collective-permute-start) | collective-permute-done | bytes 278560 | tf_op jit(solution)/shard_map/ppermute | solution.py:492
  11.5 1.9 %collective-permute-start.1 = (bf16[32,2176]{1,0:T(8,128)(2,1)S(1)}, bf16[32,2176]{1,0:T(8,128)(2,1)S(1)}, u32[]{:S(2)}, u32[]{:S(2)}) collective-permute-start(bf16[32,2176]{1,0:T(8,128)(2,1)S(1)} %get-tuple-element.25), channel_id=1, source_target_pairs={{0,1},{1,2},{2,3},{3,4},{4,5},{5,6},{6,7},{7,0},{8,9},{9,10},{10,1... | collective-permute-start | bytes 417800 | tf_op jit(solution)/shard_map/ppermute | solution.py:492
  13.5 5.5 %collective-permute-start.2 = (bf16[32,2176]{1,0:T(8,128)(2,1)S(1)}, bf16[32,2176]{1,0:T(8,128)(2,1)S(1)}, u32[]{:S(2)}, u32[]{:S(2)}) collective-permute-start(bf16[32,2176]{1,0:T(8,128)(2,1)S(1)} %get-tuple-element.26), channel_id=1, source_target_pairs={{0,7},{1,0},{2,1},{3,2},{4,3},{5,4},{6,5},{7,6},{8,15},{9,8},{10,9... | collective-permute-start | bytes 417800 | tf_op jit(solution)/shard_map/ppermute | solution.py:492
  18.9 0.0 copy-done
  19.0 0.0 copy-done.1
  19.0 0.0 copy-done.5
  19.0 0.0 copy-done.7
  19.0 0.0 copy-done.8
  19.0 4.2 %inner.1 = (bf16[32,1024]{1,0:T(8,128)(2,1)S(1)}, bf16[32,1024]{1,0:T(8,128)(2,1)S(1)}) custom-call(bf16[64,2176]{1,0:T(8,128)(2,1)S(1)} %get-tuple-element.23.own, bf16[64,2176]{1,0:T(8,128)(2,1)S(1)} %collective-permute-done.lon, f32[64,1024]{1,0:T(8,128)S(1)} %get-tuple-element.27.refs_0_, f32[1,512]{1,0:T(1,128)S(1)} %get-tuple-element.28.refs_1_, ...), custom_call_target="tpu_custom_call" | custom-call | flops 3000000000 | bytes 6000000 | tf_op jit(solution)/shard_map/inner/pallas_call | solution.py:424
  23.2 0.0 collective-permute-done.1.above
  23.2 0.0 collective-permute-done.2.below
  23.2 4.7 %outer.1 = (bf16[64,1024]{1,0:T(8,128)(2,1)S(1)}, bf16[64,1024]{1,0:T(8,128)(2,1)S(1)}) custom-call(bf16[64,2176]{1,0:T(8,128)(2,1)S(1)} %get-tuple-element.23.own, bf16[64,2176]{1,0:T(8,128)(2,1)S(1)} %collective-permute-done.lon, bf16[32,2176]{1,0:T(8,128)(2,1)S(1)} %collective-permute-done.1.above, bf16[32,2176]{1,0:T(8,128)(2,1)S(1)} %collective-permute-done.2.below, ...), custom_call_target="tpu_custom_call" | custom-call | flops 3000000000 | bytes 6000000 | tf_op jit(solution)/shard_map/outer/pallas_call | solution.py:461
  27.9 11.8 %collective-permute-start.3 = (bf16[64,1024]{1,0:T(8,128)(2,1)S(1)}, bf16[64,1024]{1,0:T(8,128)(2,1)S(1)}, u32[]{:S(2)}, u32[]{:S(2)}) collective-permute-start(bf16[64,1024]{1,0:T(8,128)(2,1)S(1)} %get-tuple-element.32), channel_id=1, source_target_pairs={{0,504},{8,0},{16,8},{24,16},{32,24},{40,32},{48,40},{56,48},{64,5... | collective-permute-start | bytes 393224 | tf_op jit(solution)/shard_map/ppermute | solution.py:492
  39.6 1.0 %collective-permute-done.3.lon = bf16[64,1024]{1,0:T(8,128)(2,1)S(1)} collective-permute-done((bf16[64,1024]{1,0:T(8,128)(2,1)S(1)}, bf16[64,1024]{1,0:T(8,128)(2,1)S(1)}, u32[]{:S(2)}, u32[]{:S(2)}) %collective-permute-start.3) | collective-permute-done | bytes 131104 | tf_op jit(solution)/shard_map/ppermute | solution.py:492
  40.6 0.9 %final.1 = bf16[16,8,1024]{2,1,0:T(8,128)(2,1)} custom-call(bf16[64,1024]{1,0:T(8,128)(2,1)S(1)} %get-tuple-element.31.own, bf16[64,1024]{1,0:T(8,128)(2,1)S(1)} %collective-permute-done.3.lon), custom_call_target="tpu_custom_call" | custom-call | tf_op jit(solution)/shard_map/final/pallas_call | solution.py:481
  (1 shorter events, 0.0 us)
Async XLA Ops:
  0.0 0.9 %copy-start.3 = (bf16[8,4,4096]{2,1,0:T(4,128)(2,1)S(1)}, bf16[8,4,4096]{2,1,0:T(4,128)(2,1)}, u32[]{:S(2)}) copy-start(bf16[8,4,4096]{2,1,0:T(4,128)(2,1)} %cot.1) | copy-start | bytes 786436
  0.0 1.0 %copy-start.6 = (s32[16,8]{0,1:T(8,128)S(1)}, s32[16,8]{0,1:T(8,128)}, u32[]{:S(2)}) copy-start(s32[16,8]{0,1:T(8,128)} %param.11) | copy-start | bytes 1540
  0.0 1.0 %copy-start.2 = (bf16[16,8,1024]{2,1,0:T(8,128)(2,1)S(1)}, bf16[16,8,1024]{2,1,0:T(8,128)(2,1)}, u32[]{:S(2)}) copy-start(bf16[16,8,1024]{2,1,0:T(8,128)(2,1)} %tokens.1) | copy-start | bytes 786436
  1.0 5.6 %copy-start.4 = (f32[16,225]{1,0:T(8,128)S(1)}, f32[16,225]{1,0:T(8,128)}, u32[]{:S(2)}) copy-start(f32[16,225]{1,0:T(8,128)} %table.1) | copy-start | bytes 43204
  1.0 5.6 %copy-start.9 = (f32[16]{0:T(128)S(1)}, f32[16]{0:T(128)}, u32[]{:S(2)}) copy-start(f32[16]{0:T(128)} %param.14) | copy-start | bytes 196
  1.1 17.9 %copy-start = (bf16[1024,1536]{1,0:T(8,128)(2,1)S(1)}, bf16[1024,1536]{1,0:T(8,128)(2,1)}, u32[]{:S(2)}) copy-start(bf16[1024,1536]{1,0:T(8,128)(2,1)} %refs_2_.3) | copy-start | bytes 9437188
  1.1 17.9 %copy-start.1 = (bf16[512,1024]{1,0:T(8,128)(2,1)S(1)}, bf16[512,1024]{1,0:T(8,128)(2,1)}, u32[]{:S(2)}) copy-start(bf16[512,1024]{1,0:T(8,128)(2,1)} %refs_3_.3) | copy-start | bytes 3145732
  1.1 17.9 %copy-start.5 = (f32[4096]{0:T(1024)S(1)}, f32[4096]{0:T(1024)}, u32[]{:S(2)}) copy-start(f32[4096]{0:T(1024)} %param.18) | copy-start | bytes 49156
  1.1 17.9 %copy-start.7 = (f32[1024]{0:T(1024)S(1)}, f32[1024]{0:T(1024)}, u32[]{:S(2)}) copy-start(f32[1024]{0:T(1024)} %param.16) | copy-start | bytes 12292
  1.1 17.9 %copy-start.8 = (f32[1024]{0:T(1024)S(1)}, f32[1024]{0:T(1024)}, u32[]{:S(2)}) copy-start(f32[1024]{0:T(1024)} %param.17) | copy-start | bytes 12292
  1.4 10.1 %collective-permute-start = (bf16[64,2176]{1,0:T(8,128)(2,1)S(1)}, bf16[64,2176]{1,0:T(8,128)(2,1)S(1)}, u32[]{:S(2)}, u32[]{:S(2)}) collective-permute-start(bf16[64,2176]{1,0:T(8,128)(2,1)S(1)} %get-tuple-element.24), channel_id=1, source_target_pairs={{0,8},{8,16},{16,24},{24,32},{32,40},{40,48},{48,56},{56,64},{64,7... | collective-permute-start | bytes 835592 | tf_op jit(solution)/shard_map/ppermute | solution.py:492
  11.5 11.6 %collective-permute-start.1 = (bf16[32,2176]{1,0:T(8,128)(2,1)S(1)}, bf16[32,2176]{1,0:T(8,128)(2,1)S(1)}, u32[]{:S(2)}, u32[]{:S(2)}) collective-permute-start(bf16[32,2176]{1,0:T(8,128)(2,1)S(1)} %get-tuple-element.25), channel_id=1, source_target_pairs={{0,1},{1,2},{2,3},{3,4},{4,5},{5,6},{6,7},{7,0},{8,9},{9,10},{10,1... | collective-permute-start | bytes 417800 | tf_op jit(solution)/shard_map/ppermute | solution.py:492
  13.5 9.7 %collective-permute-start.2 = (bf16[32,2176]{1,0:T(8,128)(2,1)S(1)}, bf16[32,2176]{1,0:T(8,128)(2,1)S(1)}, u32[]{:S(2)}, u32[]{:S(2)}) collective-permute-start(bf16[32,2176]{1,0:T(8,128)(2,1)S(1)} %get-tuple-element.26), channel_id=1, source_target_pairs={{0,7},{1,0},{2,1},{3,2},{4,3},{5,4},{6,5},{7,6},{8,15},{9,8},{10,9... | collective-permute-start | bytes 417800 | tf_op jit(solution)/shard_map/ppermute | solution.py:492
  27.9 12.7 %collective-permute-start.3 = (bf16[64,1024]{1,0:T(8,128)(2,1)S(1)}, bf16[64,1024]{1,0:T(8,128)(2,1)S(1)}, u32[]{:S(2)}, u32[]{:S(2)}) collective-permute-start(bf16[64,1024]{1,0:T(8,128)(2,1)S(1)} %get-tuple-element.32), channel_id=1, source_target_pairs={{0,504},{8,0},{16,8},{24,16},{32,24},{40,32},{48,40},{56,48},{64,5... | collective-permute-start | bytes 393224 | tf_op jit(solution)/shard_map/ppermute | solution.py:492

commit v4 on v2

--- a/solution.py
+++ b/solution.py
@@ -201,8 +201,8 @@
 def main_kernel(
     own,
     lon,
+    dia,
     lat,
-    dia,
     ebias,
     temper,
     w_qkv,
@@ -393,7 +393,7 @@
             ref[lo : lo + 16, cols] = total[16 * m : 16 * m + 16]
 
 
-def main(own, lon, lat, dia, *params):
+def main(own, lon, dia, lat, *params):
     return pl.pallas_call(
         main_kernel,
         out_shape=[jax.ShapeDtypeStruct((n, D), bf16) for n in (48, 48, 16, 16)],
@@ -420,10 +420,10 @@
             flops=1_500_000_000, bytes_accessed=6_000_000, transcendentals=150_000
         ),
         name="main",
-    )(own, lon, lat, dia, *params)
-
-
-def final_kernel(own, lon, lat, dia, out):
+    )(own, lon, dia, lat, *params)
+
+
+def final_kernel(own, lat, lon, dia, out):
     rows = jnp.concatenate([own[...], lon[...], lat[...], dia[...]], axis=0)
     row, col, _ = sorted_place(iota((128, 128), 1))
     token_place = onehot(iota((128, 128), 0) == row * 8 + col)
@@ -436,7 +436,7 @@
         out_shape=jax.ShapeDtypeStruct((16, 8, D), bf16),
         compiler_params=pltpu.CompilerParams(vmem_limit_bytes=8 * MIB),
         name="final",
-    )(own, lon, lat, dia)
+    )(own, lat, lon, dia)
 
 
 def shift_by(block, lat_step, lon_step):
@@ -469,8 +469,8 @@
     own, lon, lat, dia = main(
         own,
         lon,
+        dia,
         lat,
-        dia,
         ebias,
         temper,
         w_qkv,

time: 41.9 us -> 40.9 us (0.976)
  the two profiles are of different devices: /device:TPU:1 before, /device:TPU:24 now
where the time goes in v4:
time: 40.9 us; the launch traced here: 40.7 us
  starting transfers between devices  23.1 us (56%)
  waiting for transfers between devices  9.54 us (23%)
  Pallas kernels  7.03 us (17%)
  local copies, waits for them, and re-layouts  0.87 us (2%)
    ppermute x6, starting transfers between devices, shift_by(): return lax.ppermute(block, ('lon', 'lat'), route)  23.1 us
    ppermute x6, waiting for transfers between devices, shift_by(): return lax.ppermute(block, ('lon', 'lat'), route)  9.54 us
    pallas_call x1, Pallas kernels, main(): pl.pallas_call(main_kernel, out_shape=[jax.ShapeDtypeStruct((n, D), bf16)...  4.76 us
    pallas_call x1, Pallas kernels, final(): pl.pallas_call(final_kernel, out_shape=jax.ShapeDtypeStruct((16, 8, D), b...  0.93 us
    unnamed x20, local copies, waits for them, and re-layouts  0.87 us
    pallas_call x1, Pallas kernels, prep(): pl.pallas_call(prep_kernel, out_shape=[jax.ShapeDtypeStruct((CELLS, HEADS...  0.82 us
  transfers between devices with their start and end apart: 6, of which 2 were waited for; matrix products, arithmetic and copies ran while one was open for 0% of the time, Pallas kernels for 2%

profile of v4, /device:TPU:24, one launch (start us, length us, event | category | flops | bytes accessed | tf_op | source)
XLA Modules:
  0.0 40.7 jit_solution(17781594670153483902)
XLA Ops:
  0.0 0.0 copy-start.3
  0.0 0.0 copy-start.6
  0.0 0.0 copy-start.2
  0.0 0.2 places.1
  0.2 0.7 %copy-done.3 = bf16[8,4,4096]{2,1,0:T(4,128)(2,1)S(1)} copy-done((bf16[8,4,4096]{2,1,0:T(4,128)(2,1)S(1)}, bf16[8,4,4096]{2,1,0:T(4,128)(2,1)}, u32[]{:S(2)}) %copy-start.3) | copy-done | bytes 262168
  1.0 0.0 copy-done.6
  1.0 0.1 copy-done.2
  1.0 0.0 copy-start.4
  1.0 0.0 copy-start.9
  1.1 0.0 copy-start
  1.1 0.0 copy-start.1
  1.1 0.0 copy-start.5
  1.1 0.0 copy-start.7
  1.1 0.0 copy-start.8
  1.1 0.3 pack.1
  1.4 2.2 %collective-permute-start = (bf16[48,2176]{1,0:T(8,128)(2,1)S(1)}, bf16[48,2176]{1,0:T(8,128)(2,1)S(1)}, u32[]{:S(2)}, u32[]{:S(2)}) collective-permute-start(bf16[48,2176]{1,0:T(8,128)(2,1)S(1)} %get-tuple-element.24), channel_id=1, source_target_pairs={{0,8},{1,9},{2,10},{3,11},{4,12},{5,13},{6,14},{7,15},{8,16},{9,17... | collective-permute-start | bytes 626696 | tf_op jit(solution)/shard_map/ppermute | solution.py:449
  3.6 5.2 %collective-permute-start.1 = (bf16[16,2176]{1,0:T(8,128)(2,1)S(1)}, bf16[16,2176]{1,0:T(8,128)(2,1)S(1)}, u32[]{:S(2)}, u32[]{:S(2)}) collective-permute-start(bf16[16,2176]{1,0:T(8,128)(2,1)S(1)} %get-tuple-element.25), channel_id=1, source_target_pairs={{0,15},{1,8},{2,9},{3,10},{4,11},{5,12},{6,13},{7,14},{8,23},{9,16... | collective-permute-start | bytes 208904 | tf_op jit(solution)/shard_map/ppermute | solution.py:449
  8.8 2.4 %collective-permute-start.2 = (bf16[16,2176]{1,0:T(8,128)(2,1)S(1)}, bf16[16,2176]{1,0:T(8,128)(2,1)S(1)}, u32[]{:S(2)}, u32[]{:S(2)}) collective-permute-start(bf16[16,2176]{1,0:T(8,128)(2,1)S(1)} %get-tuple-element.26), channel_id=1, source_target_pairs={{0,7},{1,0},{2,1},{3,2},{4,3},{5,4},{6,5},{7,6},{8,15},{9,8},{10,9... | collective-permute-start | bytes 208904 | tf_op jit(solution)/shard_map/ppermute | solution.py:449
  11.3 0.0 copy-done.4
  11.3 0.0 copy-done.9
  11.3 0.8 %prep.1 = (f32[64,1024]{1,0:T(8,128)S(1)}, f32[1,512]{1,0:T(1,128)S(1)}) custom-call(f32[16,225]{1,0:T(8,128)S(1)} %copy-done.4, f32[1,16]{1,0:T(1,128)S(1)} %bitcast.9), custom_call_target="tpu_custom_call" | custom-call | flops 100000000 | bytes 400000 | tf_op jit(solution)/shard_map/prep/pallas_call | solution.py:172
  12.1 7.2 %collective-permute-done.1.dia = bf16[16,2176]{1,0:T(8,128)(2,1)S(1)} collective-permute-done((bf16[16,2176]{1,0:T(8,128)(2,1)S(1)}, bf16[16,2176]{1,0:T(8,128)(2,1)S(1)}, u32[]{:S(2)}, u32[]{:S(2)}) %collective-permute-start.1) | collective-permute-done | bytes 69664 | tf_op jit(solution)/shard_map/ppermute | solution.py:449
  19.3 0.0 collective-permute-done.2.lat
  19.3 0.0 collective-permute-done.lon
  19.3 0.0 copy-done
  19.3 0.0 copy-done.1
  19.3 0.0 copy-done.5
  19.3 0.0 copy-done.7
  19.3 0.0 copy-done.8
  19.4 4.8 %main.1 = (bf16[48,1024]{1,0:T(8,128)(2,1)S(1)}, bf16[48,1024]{1,0:T(8,128)(2,1)S(1)}, bf16[16,1024]{1,0:T(8,128)(2,1)S(1)}, bf16[16,1024]{1,0:T(8,128)(2,1)S(1)}) custom-call(bf16[48,2176]{1,0:T(8,128)(2,1)S(1)} %get-tuple-element.23.own, bf16[48,2176]{1,0:T(8,128)(2,1)S(1)} %collective-permute-done.lon, bf16[16,2176]{1,0:T(8,128)(2,1)S(1)} %collective-permute-done.1.dia, ...), custom_call_target="tpu_custom_call" | custom-call | flops 1500000000 | bytes 6000000 | tf_op jit(solution)/shard_map/main/pallas_call | solution.py:397
  24.1 4.9 %collective-permute-start.4 = (bf16[48,1024]{1,0:T(8,128)(2,1)S(1)}, bf16[48,1024]{1,0:T(8,128)(2,1)S(1)}, u32[]{:S(2)}, u32[]{:S(2)}) collective-permute-start(bf16[48,1024]{1,0:T(8,128)(2,1)S(1)} %get-tuple-element.31), channel_id=1, source_target_pairs={{0,504},{1,505},{2,506},{3,507},{4,508},{5,509},{6,510},{7,511},{8... | collective-permute-start | bytes 294920 | tf_op jit(solution)/shard_map/ppermute | solution.py:449
  29.0 4.6 %collective-permute-start.3 = (bf16[16,1024]{1,0:T(8,128)(2,1)S(1)}, bf16[16,1024]{1,0:T(8,128)(2,1)S(1)}, u32[]{:S(2)}, u32[]{:S(2)}) collective-permute-start(bf16[16,1024]{1,0:T(8,128)(2,1)S(1)} %get-tuple-element.30), channel_id=1, source_target_pairs={{0,1},{1,2},{2,3},{3,4},{4,5},{5,6},{6,7},{7,0},{8,9},{9,10},{10,1... | collective-permute-start | bytes 98312 | tf_op jit(solution)/shard_map/ppermute | solution.py:449
  33.6 3.8 %collective-permute-start.5 = (bf16[16,1024]{1,0:T(8,128)(2,1)S(1)}, bf16[16,1024]{1,0:T(8,128)(2,1)S(1)}, u32[]{:S(2)}, u32[]{:S(2)}) collective-permute-start(bf16[16,1024]{1,0:T(8,128)(2,1)S(1)} %get-tuple-element.32), channel_id=1, source_target_pairs={{0,505},{1,506},{2,507},{3,508},{4,509},{5,510},{6,511},{7,504},{8... | collective-permute-start | bytes 98312 | tf_op jit(solution)/shard_map/ppermute | solution.py:449
  37.4 0.0 collective-permute-done.3.lat
  37.4 2.3 %collective-permute-done.5.dia = bf16[16,1024]{1,0:T(8,128)(2,1)S(1)} collective-permute-done((bf16[16,1024]{1,0:T(8,128)(2,1)S(1)}, bf16[16,1024]{1,0:T(8,128)(2,1)S(1)}, u32[]{:S(2)}, u32[]{:S(2)}) %collective-permute-start.5) | collective-permute-done | bytes 32800 | tf_op jit(solution)/shard_map/ppermute | solution.py:449
  39.7 0.0 collective-permute-done.4.lon
  39.7 0.9 %final.1 = bf16[16,8,1024]{2,1,0:T(8,128)(2,1)} custom-call(bf16[48,1024]{1,0:T(8,128)(2,1)S(1)} %get-tuple-element.29.own, bf16[16,1024]{1,0:T(8,128)(2,1)S(1)} %collective-permute-done.3.lat, bf16[48,1024]{1,0:T(8,128)(2,1)S(1)} %collective-permute-done.4.lon, bf16[16,1024]{1,0:T(8,128)(2,1)S(1)} %collective-permute-done.5.dia), custom_call_target="tpu_custom_call" | custom-call | tf_op jit(solution)/shard_map/final/pallas_call | solution.py:434
Async XLA Ops:
  0.0 0.9 %copy-start.3 = (bf16[8,4,4096]{2,1,0:T(4,128)(2,1)S(1)}, bf16[8,4,4096]{2,1,0:T(4,128)(2,1)}, u32[]{:S(2)}) copy-start(bf16[8,4,4096]{2,1,0:T(4,128)(2,1)} %cot.1) | copy-start | bytes 786436
  0.0 1.0 %copy-start.6 = (s32[16,8]{0,1:T(8,128)S(1)}, s32[16,8]{0,1:T(8,128)}, u32[]{:S(2)}) copy-start(s32[16,8]{0,1:T(8,128)} %param.11) | copy-start | bytes 1540
  0.0 1.0 %copy-start.2 = (bf16[16,8,1024]{2,1,0:T(8,128)(2,1)S(1)}, bf16[16,8,1024]{2,1,0:T(8,128)(2,1)}, u32[]{:S(2)}) copy-start(bf16[16,8,1024]{2,1,0:T(8,128)(2,1)} %tokens.1) | copy-start | bytes 786436
  1.0 10.2 %copy-start.4 = (f32[16,225]{1,0:T(8,128)S(1)}, f32[16,225]{1,0:T(8,128)}, u32[]{:S(2)}) copy-start(f32[16,225]{1,0:T(8,128)} %table.1) | copy-start | bytes 43204
  1.0 10.2 %copy-start.9 = (f32[16]{0:T(128)S(1)}, f32[16]{0:T(128)}, u32[]{:S(2)}) copy-start(f32[16]{0:T(128)} %param.14) | copy-start | bytes 196
  1.1 18.3 %copy-start = (bf16[1024,1536]{1,0:T(8,128)(2,1)S(1)}, bf16[1024,1536]{1,0:T(8,128)(2,1)}, u32[]{:S(2)}) copy-start(bf16[1024,1536]{1,0:T(8,128)(2,1)} %w_qkv.1) | copy-start | bytes 9437188
  1.1 18.3 %copy-start.1 = (bf16[512,1024]{1,0:T(8,128)(2,1)S(1)}, bf16[512,1024]{1,0:T(8,128)(2,1)}, u32[]{:S(2)}) copy-start(bf16[512,1024]{1,0:T(8,128)(2,1)} %w_proj.1) | copy-start | bytes 3145732
  1.1 18.3 %copy-start.5 = (f32[4096]{0:T(1024)S(1)}, f32[4096]{0:T(1024)}, u32[]{:S(2)}) copy-start(f32[4096]{0:T(1024)} %param.18) | copy-start | bytes 49156
  1.1 18.3 %copy-start.7 = (f32[1024]{0:T(1024)S(1)}, f32[1024]{0:T(1024)}, u32[]{:S(2)}) copy-start(f32[1024]{0:T(1024)} %param.16) | copy-start | bytes 12292
  1.1 18.3 %copy-start.8 = (f32[1024]{0:T(1024)S(1)}, f32[1024]{0:T(1024)}, u32[]{:S(2)}) copy-start(f32[1024]{0:T(1024)} %param.17) | copy-start | bytes 12292
  1.4 17.9 %collective-permute-start = (bf16[48,2176]{1,0:T(8,128)(2,1)S(1)}, bf16[48,2176]{1,0:T(8,128)(2,1)S(1)}, u32[]{:S(2)}, u32[]{:S(2)}) collective-permute-start(bf16[48,2176]{1,0:T(8,128)(2,1)S(1)} %get-tuple-element.24), channel_id=1, source_target_pairs={{0,8},{1,9},{2,10},{3,11},{4,12},{5,13},{6,14},{7,15},{8,16},{9,17... | collective-permute-start | bytes 626696 | tf_op jit(solution)/shard_map/ppermute | solution.py:449
  3.6 15.7 %collective-permute-start.1 = (bf16[16,2176]{1,0:T(8,128)(2,1)S(1)}, bf16[16,2176]{1,0:T(8,128)(2,1)S(1)}, u32[]{:S(2)}, u32[]{:S(2)}) collective-permute-start(bf16[16,2176]{1,0:T(8,128)(2,1)S(1)} %get-tuple-element.25), channel_id=1, source_target_pairs={{0,15},{1,8},{2,9},{3,10},{4,11},{5,12},{6,13},{7,14},{8,23},{9,16... | collective-permute-start | bytes 208904 | tf_op jit(solution)/shard_map/ppermute | solution.py:449
  8.8 10.5 %collective-permute-start.2 = (bf16[16,2176]{1,0:T(8,128)(2,1)S(1)}, bf16[16,2176]{1,0:T(8,128)(2,1)S(1)}, u32[]{:S(2)}, u32[]{:S(2)}) collective-permute-start(bf16[16,2176]{1,0:T(8,128)(2,1)S(1)} %get-tuple-element.26), channel_id=1, source_target_pairs={{0,7},{1,0},{2,1},{3,2},{4,3},{5,4},{6,5},{7,6},{8,15},{9,8},{10,9... | collective-permute-start | bytes 208904 | tf_op jit(solution)/shard_map/ppermute | solution.py:449
  24.1 15.6 %collective-permute-start.4 = (bf16[48,1024]{1,0:T(8,128)(2,1)S(1)}, bf16[48,1024]{1,0:T(8,128)(2,1)S(1)}, u32[]{:S(2)}, u32[]{:S(2)}) collective-permute-start(bf16[48,1024]{1,0:T(8,128)(2,1)S(1)} %get-tuple-element.31), channel_id=1, source_target_pairs={{0,504},{1,505},{2,506},{3,507},{4,508},{5,509},{6,510},{7,511},{8... | collective-permute-start | bytes 294920 | tf_op jit(solution)/shard_map/ppermute | solution.py:449
  29.0 8.4 %collective-permute-start.3 = (bf16[16,1024]{1,0:T(8,128)(2,1)S(1)}, bf16[16,1024]{1,0:T(8,128)(2,1)S(1)}, u32[]{:S(2)}, u32[]{:S(2)}) collective-permute-start(bf16[16,1024]{1,0:T(8,128)(2,1)S(1)} %get-tuple-element.30), channel_id=1, source_target_pairs={{0,1},{1,2},{2,3},{3,4},{4,5},{5,6},{6,7},{7,0},{8,9},{9,10},{10,1... | collective-permute-start | bytes 98312 | tf_op jit(solution)/shard_map/ppermute | solution.py:449
  33.6 6.1 %collective-permute-start.5 = (bf16[16,1024]{1,0:T(8,128)(2,1)S(1)}, bf16[16,1024]{1,0:T(8,128)(2,1)S(1)}, u32[]{:S(2)}, u32[]{:S(2)}) collective-permute-start(bf16[16,1024]{1,0:T(8,128)(2,1)S(1)} %get-tuple-element.32), channel_id=1, source_target_pairs={{0,505},{1,506},{2,507},{3,508},{4,509},{5,510},{6,511},{7,504},{8... | collective-permute-start | bytes 98312 | tf_op jit(solution)/shard_map/ppermute | solution.py:449

commit v5 on v3

--- a/solution.py
+++ b/solution.py
@@ -127,11 +127,13 @@
     )(*sorts, tokens, labels, cot)
 
 
-def strips_kernel(own, lon, top, bottom):
-    top[0:16, :] = lon[0:16, :]
-    top[16:32, :] = own[0:16, :]
-    bottom[0:16, :] = lon[48:64, :]
-    bottom[16:32, :] = own[48:64, :]
+def strips_kernel(own, lon, to_first, to_second):
+    odd = lax.axis_index("lat") % 2 == 1
+    for n, ref in enumerate((lon, own)):
+        rows = slice(16 * n, 16 * n + 16)
+        top, bottom = ref[0:16, :], ref[48:64, :]
+        to_first[rows, :] = jnp.where(odd, top, bottom)
+        to_second[rows, :] = jnp.where(odd, bottom, top)
 
 
 def strips(own, lon):
@@ -433,8 +435,11 @@
     )(own, lon, *params)
 
 
-def outer_kernel(own, lon, above, below, in_own, in_lon, *refs):
-    params, (out_own, out_lon), scratch = refs[:7], refs[7:9], refs[9:]
+def outer_kernel(own, lon, first, second, in_own, in_lon, *refs):
+    params, (out_own, out_lon, above, below), scratch = refs[:7], refs[7:11], refs[11:]
+    odd = lax.axis_index("lat") % 2 == 1
+    above[...] = jnp.where(odd, first[0:32, :], second[0:32, :])
+    below[...] = jnp.where(odd, second[32:64, :], first[32:64, :])
     quads = (
         (above, 0),
         (above, 16),
@@ -457,17 +462,17 @@
     windows(quads, slice(32, 96), emit, params, scratch)
 
 
-def outer(own, lon, above, below, in_own, in_lon, params):
+def outer(own, lon, first, second, in_own, in_lon, params):
     return pl.pallas_call(
         outer_kernel,
         out_shape=[jax.ShapeDtypeStruct((64, D), bf16)] * 2,
-        scratch_shapes=scratch_for(128),
+        scratch_shapes=[pltpu.VMEM((32, WIDE), bf16)] * 2 + scratch_for(128),
         compiler_params=pltpu.CompilerParams(vmem_limit_bytes=24 * MIB),
         cost_estimate=pl.CostEstimate(
             flops=3_000_000_000, bytes_accessed=6_000_000, transcendentals=150_000
         ),
         name="outer",
-    )(own, lon, above, below, in_own, in_lon, *params)
+    )(own, lon, first, second, in_own, in_lon, *params)
 
 
 def final_kernel(own, lon, out):
@@ -516,11 +521,13 @@
         norm_shift.reshape(1, D),
         merge_gain.reshape(1, 4 * D),
     )
-    top, bottom = strips(own, lon)
-    below = passed_along(top, "lat", -1)
-    above = passed_along(bottom, "lat", 1)
+    to_first, to_second = strips(own, lon)
+    lats = lax.axis_size("lat")
+    pairs = [[i, (i + 1) % lats] for i in range(lats)]
+    first = lax.all_gather(to_first, "lat", axis_index_groups=pairs[0::2], tiled=True)
+    second = lax.all_gather(to_second, "lat", axis_index_groups=pairs[1::2], tiled=True)
     in_own, in_lon = inner(own, lon, params)
-    own, lon = outer(own, lon, above, below, in_own, in_lon, params)
+    own, lon = outer(own, lon, first, second, in_own, in_lon, params)
     lon = passed_along(lon, "lon", -1)
     return final(own, lon)
 

time: 41.7 us -> 47.2 us (1.13)
  blocking collectives: 0 us -> 14.5 us
  starting transfers between devices: 24.4 us -> 15.3 us
    all_gather x0 -> x2, blocking collectives: none -> 14.5 us  [the longest x1 7.86 us: shards(): lax.all_gather(to_first, 'lat', axis_index_groups=pairs[0::2], tiled=True)]
    ppermute x4 -> x2, starting transfers between devices: 24.4 us -> 15.3 us  [passed_along(): return lax.ppermute(block, axis, route)]
    ppermute x4 -> x2, waiting for transfers between devices: 5.02 us -> 5.01 us  [passed_along(): return lax.ppermute(block, axis, route)]
  transfers between devices with their start and end apart: 4 -> 2, of which waited for: 2 -> 2; matrix products, arithmetic and copies ran while one was open for 0% -> 0% of each run, Pallas kernels for 12% -> 2%
where the time goes in v5:
time: 47.2 us; the launch traced here: 47 us
  starting transfers between devices  15.3 us (32%)
  blocking collectives  14.5 us (31%)
  Pallas kernels  11.1 us (24%)
  waiting for transfers between devices  5.01 us (11%)
  local copies, waits for them, and re-layouts  0.88 us (2%)
    ppermute x2, starting transfers between devices, passed_along(): return lax.ppermute(block, axis, route)  15.3 us
    all_gather x1, blocking collectives, shards(): lax.all_gather(to_first, 'lat', axis_index_groups=pairs[0::2], tiled=True)  7.86 us
    all_gather x1, blocking collectives, shards(): lax.all_gather(to_second, 'lat', axis_index_groups=pairs[1::2], tiled=True)  6.68 us
    ppermute x2, waiting for transfers between devices, passed_along(): return lax.ppermute(block, axis, route)  5.01 us
    pallas_call x1, Pallas kernels, outer(): pl.pallas_call(outer_kernel, out_shape=[jax.ShapeDtypeStruct((64, D), bf1...  4.69 us
    pallas_call x1, Pallas kernels, inner(): pl.pallas_call(inner_kernel, out_shape=[jax.ShapeDtypeStruct((32, D), bf1...  4.17 us
  transfers between devices with their start and end apart: 2, of which 2 were waited for; matrix products, arithmetic and copies ran while one was open for 0% of the time, Pallas kernels for 2%

profile of v5, /device:TPU:1, one launch (start us, length us, event | category | flops | bytes accessed | tf_op | source)
XLA Modules:
  0.0 47.0 jit_solution(7641644379160514185)
XLA Ops:
  0.0 0.0 copy-start.3
  0.0 0.0 copy-start.6
  0.0 0.0 copy-start.2
  0.0 0.2 places.1
  0.2 0.7 %copy-done.3 = bf16[8,4,4096]{2,1,0:T(4,128)(2,1)S(1)} copy-done((bf16[8,4,4096]{2,1,0:T(4,128)(2,1)S(1)}, bf16[8,4,4096]{2,1,0:T(4,128)(2,1)}, u32[]{:S(2)}) %copy-start.3) | copy-done | bytes 262168
  1.0 0.0 copy-done.6
  1.0 0.1 copy-done.2
  1.0 0.0 copy-start.4
  1.0 0.0 copy-start.9
  1.1 0.0 copy-start
  1.1 0.0 copy-start.1
  1.1 0.0 copy-start.5
  1.1 0.0 copy-start.7
  1.1 0.0 copy-start.8
  1.1 0.3 pack.1
  1.4 5.2 %collective-permute-start = (bf16[64,2176]{1,0:T(8,128)(2,1)S(1)}, bf16[64,2176]{1,0:T(8,128)(2,1)S(1)}, u32[]{:S(2)}, u32[]{:S(2)}) collective-permute-start(bf16[64,2176]{1,0:T(8,128)(2,1)S(1)} %get-tuple-element.24), channel_id=1, source_target_pairs={{0,8},{8,16},{16,24},{24,32},{32,40},{40,48},{48,56},{56,64},{64,7... | collective-permute-start | bytes 835592 | tf_op jit(solution)/shard_map/ppermute | solution.py:497
  6.6 0.0 copy-done.4
  6.6 0.0 copy-done.9
  6.6 0.8 %prep.1 = (f32[64,1024]{1,0:T(8,128)S(1)}, f32[1,512]{1,0:T(1,128)S(1)}) custom-call(f32[16,225]{1,0:T(8,128)S(1)} %copy-done.4, f32[1,16]{1,0:T(1,128)S(1)} %bitcast.12), custom_call_target="tpu_custom_call" | custom-call | flops 100000000 | bytes 400000 | tf_op jit(solution)/shard_map/prep/pallas_call | solution.py:190
  7.5 4.0 %collective-permute-done.lon = bf16[64,2176]{1,0:T(8,128)(2,1)S(1)} collective-permute-done((bf16[64,2176]{1,0:T(8,128)(2,1)S(1)}, bf16[64,2176]{1,0:T(8,128)(2,1)S(1)}, u32[]{:S(2)}, u32[]{:S(2)}) %collective-permute-start) | collective-permute-done | bytes 278560 | tf_op jit(solution)/shard_map/ppermute | solution.py:497
  11.6 7.9 %all_gather.6.first = bf16[64,2176]{1,0:T(8,128)(2,1)S(1)} all-gather(bf16[32,2176]{1,0:T(8,128)(2,1)S(1)} %get-tuple-element.25), channel_id=1, replica_groups={{0,1},{2,3},{4,5},{6,7},{8,9},{10,11},{12,13},{14,15},{16,17},{18,19},{..., dimensions={0}, use_global_device_ids=true | all-gather | bytes 417792 | tf_op jit(solution)/shard_map/all_gather | solution.py:527
  19.4 6.7 %all_gather.7.second = bf16[64,2176]{1,0:T(8,128)(2,1)S(1)} all-gather(bf16[32,2176]{1,0:T(8,128)(2,1)S(1)} %get-tuple-element.26), channel_id=1, replica_groups={{1,2},{3,4},{5,6},{7,0},{9,10},{11,12},{13,14},{15,8},{17,18},{19,20},{..., dimensions={0}, use_global_device_ids=true | all-gather | bytes 417792 | tf_op jit(solution)/shard_map/all_gather | solution.py:528
  26.1 0.0 copy-done
  26.1 0.0 copy-done.1
  26.1 0.0 copy-done.5
  26.1 0.0 copy-done.7
  26.1 0.0 copy-done.8
  26.1 4.2 %inner.1 = (bf16[32,1024]{1,0:T(8,128)(2,1)S(1)}, bf16[32,1024]{1,0:T(8,128)(2,1)S(1)}) custom-call(bf16[64,2176]{1,0:T(8,128)(2,1)S(1)} %get-tuple-element.23.own, bf16[64,2176]{1,0:T(8,128)(2,1)S(1)} %collective-permute-done.lon, f32[64,1024]{1,0:T(8,128)S(1)} %get-tuple-element.27.refs_0_, f32[1,512]{1,0:T(1,128)S(1)} %get-tuple-element.28.refs_1_, ...), custom_call_target="tpu_custom_call" | custom-call | flops 3000000000 | bytes 6000000 | tf_op jit(solution)/shard_map/inner/pallas_call | solution.py:426
  30.3 4.7 %outer.1 = (bf16[64,1024]{1,0:T(8,128)(2,1)S(1)}, bf16[64,1024]{1,0:T(8,128)(2,1)S(1)}) custom-call(bf16[64,2176]{1,0:T(8,128)(2,1)S(1)} %get-tuple-element.23.own, bf16[64,2176]{1,0:T(8,128)(2,1)S(1)} %collective-permute-done.lon, bf16[64,2176]{1,0:T(8,128)(2,1)S(1)} %all_gather.6.first, bf16[64,2176]{1,0:T(8,128)(2,1)S(1)} %all_gather.7.second, ...), custom_call_target="tpu_custom_call" | custom-call | flops 3000000000 | bytes 6000000 | tf_op jit(solution)/shard_map/outer/pallas_call | solution.py:466
  35.0 10.1 %collective-permute-start.1 = (bf16[64,1024]{1,0:T(8,128)(2,1)S(1)}, bf16[64,1024]{1,0:T(8,128)(2,1)S(1)}, u32[]{:S(2)}, u32[]{:S(2)}) collective-permute-start(bf16[64,1024]{1,0:T(8,128)(2,1)S(1)} %get-tuple-element.32), channel_id=1, source_target_pairs={{0,504},{8,0},{16,8},{24,16},{32,24},{40,32},{48,40},{56,48},{64,5... | collective-permute-start | bytes 393224 | tf_op jit(solution)/shard_map/ppermute | solution.py:497
  45.1 1.0 %collective-permute-done.1.lon = bf16[64,1024]{1,0:T(8,128)(2,1)S(1)} collective-permute-done((bf16[64,1024]{1,0:T(8,128)(2,1)S(1)}, bf16[64,1024]{1,0:T(8,128)(2,1)S(1)}, u32[]{:S(2)}, u32[]{:S(2)}) %collective-permute-start.1) | collective-permute-done | bytes 131104 | tf_op jit(solution)/shard_map/ppermute | solution.py:497
  46.1 0.9 %final.1 = bf16[16,8,1024]{2,1,0:T(8,128)(2,1)} custom-call(bf16[64,1024]{1,0:T(8,128)(2,1)S(1)} %get-tuple-element.31.own, bf16[64,1024]{1,0:T(8,128)(2,1)S(1)} %collective-permute-done.1.lon), custom_call_target="tpu_custom_call" | custom-call | tf_op jit(solution)/shard_map/final/pallas_call | solution.py:486
  (1 shorter events, 0.0 us)
Async XLA Ops:
  0.0 0.9 %copy-start.3 = (bf16[8,4,4096]{2,1,0:T(4,128)(2,1)S(1)}, bf16[8,4,4096]{2,1,0:T(4,128)(2,1)}, u32[]{:S(2)}) copy-start(bf16[8,4,4096]{2,1,0:T(4,128)(2,1)} %cot.1) | copy-start | bytes 786436
  0.0 1.0 %copy-start.6 = (s32[16,8]{0,1:T(8,128)S(1)}, s32[16,8]{0,1:T(8,128)}, u32[]{:S(2)}) copy-start(s32[16,8]{0,1:T(8,128)} %param.11) | copy-start | bytes 1540
  0.0 1.0 %copy-start.2 = (bf16[16,8,1024]{2,1,0:T(8,128)(2,1)S(1)}, bf16[16,8,1024]{2,1,0:T(8,128)(2,1)}, u32[]{:S(2)}) copy-start(bf16[16,8,1024]{2,1,0:T(8,128)(2,1)} %tokens.1) | copy-start | bytes 786436
  1.0 5.6 %copy-start.4 = (f32[16,225]{1,0:T(8,128)S(1)}, f32[16,225]{1,0:T(8,128)}, u32[]{:S(2)}) copy-start(f32[16,225]{1,0:T(8,128)} %table.1) | copy-start | bytes 43204
  1.0 5.6 %copy-start.9 = (f32[16]{0:T(128)S(1)}, f32[16]{0:T(128)}, u32[]{:S(2)}) copy-start(f32[16]{0:T(128)} %param.14) | copy-start | bytes 196
  1.1 25.0 %copy-start = (bf16[1024,1536]{1,0:T(8,128)(2,1)S(1)}, bf16[1024,1536]{1,0:T(8,128)(2,1)}, u32[]{:S(2)}) copy-start(bf16[1024,1536]{1,0:T(8,128)(2,1)} %refs_2_.3) | copy-start | bytes 9437188
  1.1 25.0 %copy-start.1 = (bf16[512,1024]{1,0:T(8,128)(2,1)S(1)}, bf16[512,1024]{1,0:T(8,128)(2,1)}, u32[]{:S(2)}) copy-start(bf16[512,1024]{1,0:T(8,128)(2,1)} %refs_3_.3) | copy-start | bytes 3145732
  1.1 25.0 %copy-start.5 = (f32[4096]{0:T(1024)S(1)}, f32[4096]{0:T(1024)}, u32[]{:S(2)}) copy-start(f32[4096]{0:T(1024)} %param.18) | copy-start | bytes 49156
  1.1 25.0 %copy-start.7 = (f32[1024]{0:T(1024)S(1)}, f32[1024]{0:T(1024)}, u32[]{:S(2)}) copy-start(f32[1024]{0:T(1024)} %param.16) | copy-start | bytes 12292
  1.1 25.0 %copy-start.8 = (f32[1024]{0:T(1024)S(1)}, f32[1024]{0:T(1024)}, u32[]{:S(2)}) copy-start(f32[1024]{0:T(1024)} %param.17) | copy-start | bytes 12292
  1.4 10.1 %collective-permute-start = (bf16[64,2176]{1,0:T(8,128)(2,1)S(1)}, bf16[64,2176]{1,0:T(8,128)(2,1)S(1)}, u32[]{:S(2)}, u32[]{:S(2)}) collective-permute-start(bf16[64,2176]{1,0:T(8,128)(2,1)S(1)} %get-tuple-element.24), channel_id=1, source_target_pairs={{0,8},{8,16},{16,24},{24,32},{32,40},{40,48},{48,56},{56,64},{64,7... | collective-permute-start | bytes 835592 | tf_op jit(solution)/shard_map/ppermute | solution.py:497
  35.0 11.1 %collective-permute-start.1 = (bf16[64,1024]{1,0:T(8,128)(2,1)S(1)}, bf16[64,1024]{1,0:T(8,128)(2,1)S(1)}, u32[]{:S(2)}, u32[]{:S(2)}) collective-permute-start(bf16[64,1024]{1,0:T(8,128)(2,1)S(1)} %get-tuple-element.32), channel_id=1, source_target_pairs={{0,504},{8,0},{16,8},{24,16},{32,24},{40,32},{48,40},{56,48},{64,5... | collective-permute-start | bytes 393224 | tf_op jit(solution)/shard_map/ppermute | solution.py:497

commit v6 on v4

--- a/solution.py
+++ b/solution.py
@@ -29,7 +29,7 @@
     s = (n // 4) % 4
     g = n % 4
     row = jnp.where(quad < 6, 4 + 4 * (quad % 3), 0) + 2 * (g // 2) + s % 2
-    col = jnp.where((quad // 3 == 1) | (quad == 7), 4, 0) + 2 * (g % 2) + s // 2
+    col = jnp.where((quad // 3 == 1) | (quad == 7), 0, 4) + 2 * (g % 2) + s // 2
     return row, col, s
 
 
@@ -232,14 +232,14 @@
     mgain,
 ):
     quads = (
+        (own, out_own, 0),
         (lon, out_lon, 0),
-        (own, out_own, 0),
+        (own, out_own, 16),
         (lon, out_lon, 16),
-        (own, out_own, 16),
+        (own, out_own, 32),
         (lon, out_lon, 32),
-        (own, out_own, 32),
+        (lat, out_lat, 0),
         (dia, out_dia, 0),
-        (lat, out_lat, 0),
     )
     pairs = [(w, b) for w in range(2) for b in range(BLOCKS)]
     for n, (ref, _, lo) in enumerate(quads):
@@ -423,7 +423,7 @@
     )(own, lon, dia, lat, *params)
 
 
-def final_kernel(own, lat, lon, dia, out):
+def final_kernel(own, lon, dia, lat, out):
     rows = jnp.concatenate([own[...], lon[...], lat[...], dia[...]], axis=0)
     row, col, _ = sorted_place(iota((128, 128), 1))
     token_place = onehot(iota((128, 128), 0) == row * 8 + col)
@@ -436,7 +436,7 @@
         out_shape=jax.ShapeDtypeStruct((16, 8, D), bf16),
         compiler_params=pltpu.CompilerParams(vmem_limit_bytes=8 * MIB),
         name="final",
-    )(own, lat, lon, dia)
+    )(own, lon, dia, lat)
 
 
 def shift_by(block, lat_step, lon_step):
@@ -462,8 +462,8 @@
     cotangent,
 ):
     own, lon, lat, dia = pack(tokens, labels.T, cotangent, places())
-    lon = shift_by(lon, 0, 1)
-    dia = shift_by(dia, -1, 1)
+    lon = shift_by(lon, 0, -1)
+    dia = shift_by(dia, -1, -1)
     lat = shift_by(lat, -1, 0)
     ebias, temper = prep(bias_table, logit_scale.reshape(1, HEADS))
     own, lon, lat, dia = main(
@@ -479,8 +479,8 @@
         norm_shift.reshape(1, D),
         merge_gain.reshape(1, 4 * D),
     )
-    lon = shift_by(lon, 0, -1)
-    dia = shift_by(dia, 1, -1)
+    lon = shift_by(lon, 0, 1)
+    dia = shift_by(dia, 1, 1)
     lat = shift_by(lat, 1, 0)
     return final(own, lon, lat, dia)
 

time: 40.9 us -> 43.2 us (1.056)
  the two profiles are of different devices: /device:TPU:24 before, /device:TPU:1 now
where the time goes in v6:
time: 43.2 us; the launch traced here: 42.9 us
  starting transfers between devices  28.4 us (66%)
  Pallas kernels  7.02 us (16%)
  waiting for transfers between devices  6.44 us (15%)
  local copies, waits for them, and re-layouts  0.86 us (2%)
    ppermute x6, starting transfers between devices, shift_by(): return lax.ppermute(block, ('lon', 'lat'), route)  28.4 us
    ppermute x6, waiting for transfers between devices, shift_by(): return lax.ppermute(block, ('lon', 'lat'), route)  6.44 us
    pallas_call x1, Pallas kernels, main(): pl.pallas_call(main_kernel, out_shape=[jax.ShapeDtypeStruct((n, D), bf16)...  4.76 us
    pallas_call x1, Pallas kernels, final(): pl.pallas_call(final_kernel, out_shape=jax.ShapeDtypeStruct((16, 8, D), b...  0.93 us
    unnamed x20, local copies, waits for them, and re-layouts  0.86 us
  transfers between devices with their start and end apart: 6, of which 3 were waited for; matrix products, arithmetic and copies ran while one was open for 0% of the time, Pallas kernels for 2%

profile of v6, /device:TPU:1, one launch (start us, length us, event | category | flops | bytes accessed | tf_op | source)
XLA Modules:
  0.0 42.9 jit_solution(3889686655543287730)
XLA Ops:
  0.0 0.0 copy-start.3
  0.0 0.0 copy-start.6
  0.0 0.0 copy-start.2
  0.0 0.2 places.1
  0.2 0.7 %copy-done.3 = bf16[8,4,4096]{2,1,0:T(4,128)(2,1)S(1)} copy-done((bf16[8,4,4096]{2,1,0:T(4,128)(2,1)S(1)}, bf16[8,4,4096]{2,1,0:T(4,128)(2,1)}, u32[]{:S(2)}) %copy-start.3) | copy-done | bytes 262168
  1.0 0.0 copy-done.6
  1.0 0.1 copy-done.2
  1.0 0.0 copy-start.4
  1.0 0.0 copy-start.9
  1.1 0.0 copy-start
  1.1 0.0 copy-start.1
  1.1 0.0 copy-start.5
  1.1 0.0 copy-start.7
  1.1 0.0 copy-start.8
  1.1 0.3 pack.1
  1.4 9.1 %collective-permute-start = (bf16[48,2176]{1,0:T(8,128)(2,1)S(1)}, bf16[48,2176]{1,0:T(8,128)(2,1)S(1)}, u32[]{:S(2)}, u32[]{:S(2)}) collective-permute-start(bf16[48,2176]{1,0:T(8,128)(2,1)S(1)} %get-tuple-element.24), channel_id=1, source_target_pairs={{0,504},{1,505},{2,506},{3,507},{4,508},{5,509},{6,510},{7,511},{8... | collective-permute-start | bytes 626696 | tf_op jit(solution)/shard_map/ppermute | solution.py:449
  10.5 10.6 %collective-permute-start.1 = (bf16[16,2176]{1,0:T(8,128)(2,1)S(1)}, bf16[16,2176]{1,0:T(8,128)(2,1)S(1)}, u32[]{:S(2)}, u32[]{:S(2)}) collective-permute-start(bf16[16,2176]{1,0:T(8,128)(2,1)S(1)} %get-tuple-element.25), channel_id=1, source_target_pairs={{0,511},{1,504},{2,505},{3,506},{4,507},{5,508},{6,509},{7,510},{8... | collective-permute-start | bytes 208904 | tf_op jit(solution)/shard_map/ppermute | solution.py:449
  21.1 3.1 %collective-permute-start.2 = (bf16[16,2176]{1,0:T(8,128)(2,1)S(1)}, bf16[16,2176]{1,0:T(8,128)(2,1)S(1)}, u32[]{:S(2)}, u32[]{:S(2)}) collective-permute-start(bf16[16,2176]{1,0:T(8,128)(2,1)S(1)} %get-tuple-element.26), channel_id=1, source_target_pairs={{0,7},{1,0},{2,1},{3,2},{4,3},{5,4},{6,5},{7,6},{8,15},{9,8},{10,9... | collective-permute-start | bytes 208904 | tf_op jit(solution)/shard_map/ppermute | solution.py:449
  24.1 0.0 copy-done.4
  24.1 0.0 copy-done.9
  24.1 0.8 %prep.1 = (f32[64,1024]{1,0:T(8,128)S(1)}, f32[1,512]{1,0:T(1,128)S(1)}) custom-call(f32[16,225]{1,0:T(8,128)S(1)} %copy-done.4, f32[1,16]{1,0:T(1,128)S(1)} %bitcast.9), custom_call_target="tpu_custom_call" | custom-call | flops 100000000 | bytes 400000 | tf_op jit(solution)/shard_map/prep/pallas_call | solution.py:172
  25.0 0.0 collective-permute-done.1.dia
  25.0 1.5 %collective-permute-done.2.lat = bf16[16,2176]{1,0:T(8,128)(2,1)S(1)} collective-permute-done((bf16[16,2176]{1,0:T(8,128)(2,1)S(1)}, bf16[16,2176]{1,0:T(8,128)(2,1)S(1)}, u32[]{:S(2)}, u32[]{:S(2)}) %collective-permute-start.2) | collective-permute-done | bytes 69664 | tf_op jit(solution)/shard_map/ppermute | solution.py:449
  26.5 0.0 collective-permute-done.lon
  26.5 0.0 copy-done
  26.5 0.0 copy-done.1
  26.5 0.0 copy-done.5
  26.5 0.0 copy-done.7
  26.6 0.0 copy-done.8
  26.6 4.8 %main.1 = (bf16[48,1024]{1,0:T(8,128)(2,1)S(1)}, bf16[48,1024]{1,0:T(8,128)(2,1)S(1)}, bf16[16,1024]{1,0:T(8,128)(2,1)S(1)}, bf16[16,1024]{1,0:T(8,128)(2,1)S(1)}) custom-call(bf16[48,2176]{1,0:T(8,128)(2,1)S(1)} %get-tuple-element.23.own, bf16[48,2176]{1,0:T(8,128)(2,1)S(1)} %collective-permute-done.lon, bf16[16,2176]{1,0:T(8,128)(2,1)S(1)} %collective-permute-done.1.dia, ...), custom_call_target="tpu_custom_call" | custom-call | flops 1500000000 | bytes 6000000 | tf_op jit(solution)/shard_map/main/pallas_call | solution.py:397
  31.3 1.9 %collective-permute-start.3 = (bf16[48,1024]{1,0:T(8,128)(2,1)S(1)}, bf16[48,1024]{1,0:T(8,128)(2,1)S(1)}, u32[]{:S(2)}, u32[]{:S(2)}) collective-permute-start(bf16[48,1024]{1,0:T(8,128)(2,1)S(1)} %get-tuple-element.30), channel_id=1, source_target_pairs={{0,8},{1,9},{2,10},{3,11},{4,12},{5,13},{6,14},{7,15},{8,16},{9,17... | collective-permute-start | bytes 294920 | tf_op jit(solution)/shard_map/ppermute | solution.py:449
  33.3 1.9 %collective-permute-start.4 = (bf16[16,1024]{1,0:T(8,128)(2,1)S(1)}, bf16[16,1024]{1,0:T(8,128)(2,1)S(1)}, u32[]{:S(2)}, u32[]{:S(2)}) collective-permute-start(bf16[16,1024]{1,0:T(8,128)(2,1)S(1)} %get-tuple-element.31), channel_id=1, source_target_pairs={{0,9},{1,10},{2,11},{3,12},{4,13},{5,14},{6,15},{7,8},{8,17},{9,18... | collective-permute-start | bytes 98312 | tf_op jit(solution)/shard_map/ppermute | solution.py:449
  35.2 1.9 %collective-permute-start.5 = (bf16[16,1024]{1,0:T(8,128)(2,1)S(1)}, bf16[16,1024]{1,0:T(8,128)(2,1)S(1)}, u32[]{:S(2)}, u32[]{:S(2)}) collective-permute-start(bf16[16,1024]{1,0:T(8,128)(2,1)S(1)} %get-tuple-element.32), channel_id=1, source_target_pairs={{0,1},{1,2},{2,3},{3,4},{4,5},{5,6},{6,7},{7,0},{8,9},{9,10},{10,1... | collective-permute-start | bytes 98312 | tf_op jit(solution)/shard_map/ppermute | solution.py:449
  37.1 4.6 %collective-permute-done.4.dia = bf16[16,1024]{1,0:T(8,128)(2,1)S(1)} collective-permute-done((bf16[16,1024]{1,0:T(8,128)(2,1)S(1)}, bf16[16,1024]{1,0:T(8,128)(2,1)S(1)}, u32[]{:S(2)}, u32[]{:S(2)}) %collective-permute-start.4) | collective-permute-done | bytes 32800 | tf_op jit(solution)/shard_map/ppermute | solution.py:449
  41.7 0.3 collective-permute-done.5.lat
  42.0 0.0 collective-permute-done.3.lon
  42.0 0.9 %final.1 = bf16[16,8,1024]{2,1,0:T(8,128)(2,1)} custom-call(bf16[48,1024]{1,0:T(8,128)(2,1)S(1)} %get-tuple-element.29.own, bf16[48,1024]{1,0:T(8,128)(2,1)S(1)} %collective-permute-done.3.lon, bf16[16,1024]{1,0:T(8,128)(2,1)S(1)} %collective-permute-done.4.dia, bf16[16,1024]{1,0:T(8,128)(2,1)S(1)} %collective-permute-done.5.lat), custom_call_target="tpu_custom_call" | custom-call | tf_op jit(solution)/shard_map/final/pallas_call | solution.py:434
Async XLA Ops:
  0.0 0.9 %copy-start.3 = (bf16[8,4,4096]{2,1,0:T(4,128)(2,1)S(1)}, bf16[8,4,4096]{2,1,0:T(4,128)(2,1)}, u32[]{:S(2)}) copy-start(bf16[8,4,4096]{2,1,0:T(4,128)(2,1)} %cot.1) | copy-start | bytes 786436
  0.0 1.0 %copy-start.6 = (s32[16,8]{0,1:T(8,128)S(1)}, s32[16,8]{0,1:T(8,128)}, u32[]{:S(2)}) copy-start(s32[16,8]{0,1:T(8,128)} %param.11) | copy-start | bytes 1540
  0.0 1.0 %copy-start.2 = (bf16[16,8,1024]{2,1,0:T(8,128)(2,1)S(1)}, bf16[16,8,1024]{2,1,0:T(8,128)(2,1)}, u32[]{:S(2)}) copy-start(bf16[16,8,1024]{2,1,0:T(8,128)(2,1)} %tokens.1) | copy-start | bytes 786436
  1.0 23.1 %copy-start.4 = (f32[16,225]{1,0:T(8,128)S(1)}, f32[16,225]{1,0:T(8,128)}, u32[]{:S(2)}) copy-start(f32[16,225]{1,0:T(8,128)} %table.1) | copy-start | bytes 43204
  1.0 23.1 %copy-start.9 = (f32[16]{0:T(128)S(1)}, f32[16]{0:T(128)}, u32[]{:S(2)}) copy-start(f32[16]{0:T(128)} %param.14) | copy-start | bytes 196
  1.1 25.5 %copy-start = (bf16[1024,1536]{1,0:T(8,128)(2,1)S(1)}, bf16[1024,1536]{1,0:T(8,128)(2,1)}, u32[]{:S(2)}) copy-start(bf16[1024,1536]{1,0:T(8,128)(2,1)} %w_qkv.1) | copy-start | bytes 9437188
  1.1 25.5 %copy-start.1 = (bf16[512,1024]{1,0:T(8,128)(2,1)S(1)}, bf16[512,1024]{1,0:T(8,128)(2,1)}, u32[]{:S(2)}) copy-start(bf16[512,1024]{1,0:T(8,128)(2,1)} %w_proj.1) | copy-start | bytes 3145732
  1.1 25.5 %copy-start.5 = (f32[4096]{0:T(1024)S(1)}, f32[4096]{0:T(1024)}, u32[]{:S(2)}) copy-start(f32[4096]{0:T(1024)} %param.18) | copy-start | bytes 49156
  1.1 25.5 %copy-start.7 = (f32[1024]{0:T(1024)S(1)}, f32[1024]{0:T(1024)}, u32[]{:S(2)}) copy-start(f32[1024]{0:T(1024)} %param.16) | copy-start | bytes 12292
  1.1 25.5 %copy-start.8 = (f32[1024]{0:T(1024)S(1)}, f32[1024]{0:T(1024)}, u32[]{:S(2)}) copy-start(f32[1024]{0:T(1024)} %param.17) | copy-start | bytes 12292
  1.4 25.1 %collective-permute-start = (bf16[48,2176]{1,0:T(8,128)(2,1)S(1)}, bf16[48,2176]{1,0:T(8,128)(2,1)S(1)}, u32[]{:S(2)}, u32[]{:S(2)}) collective-permute-start(bf16[48,2176]{1,0:T(8,128)(2,1)S(1)} %get-tuple-element.24), channel_id=1, source_target_pairs={{0,504},{1,505},{2,506},{3,507},{4,508},{5,509},{6,510},{7,511},{8... | collective-permute-start | bytes 626696 | tf_op jit(solution)/shard_map/ppermute | solution.py:449
  10.5 14.5 %collective-permute-start.1 = (bf16[16,2176]{1,0:T(8,128)(2,1)S(1)}, bf16[16,2176]{1,0:T(8,128)(2,1)S(1)}, u32[]{:S(2)}, u32[]{:S(2)}) collective-permute-start(bf16[16,2176]{1,0:T(8,128)(2,1)S(1)} %get-tuple-element.25), channel_id=1, source_target_pairs={{0,511},{1,504},{2,505},{3,506},{4,507},{5,508},{6,509},{7,510},{8... | collective-permute-start | bytes 208904 | tf_op jit(solution)/shard_map/ppermute | solution.py:449
  21.1 5.5 %collective-permute-start.2 = (bf16[16,2176]{1,0:T(8,128)(2,1)S(1)}, bf16[16,2176]{1,0:T(8,128)(2,1)S(1)}, u32[]{:S(2)}, u32[]{:S(2)}) collective-permute-start(bf16[16,2176]{1,0:T(8,128)(2,1)S(1)} %get-tuple-element.26), channel_id=1, source_target_pairs={{0,7},{1,0},{2,1},{3,2},{4,3},{5,4},{6,5},{7,6},{8,15},{9,8},{10,9... | collective-permute-start | bytes 208904 | tf_op jit(solution)/shard_map/ppermute | solution.py:449
  31.3 10.7 %collective-permute-start.3 = (bf16[48,1024]{1,0:T(8,128)(2,1)S(1)}, bf16[48,1024]{1,0:T(8,128)(2,1)S(1)}, u32[]{:S(2)}, u32[]{:S(2)}) collective-permute-start(bf16[48,1024]{1,0:T(8,128)(2,1)S(1)} %get-tuple-element.30), channel_id=1, source_target_pairs={{0,8},{1,9},{2,10},{3,11},{4,12},{5,13},{6,14},{7,15},{8,16},{9,17... | collective-permute-start | bytes 294920 | tf_op jit(solution)/shard_map/ppermute | solution.py:449
  33.3 8.4 %collective-permute-start.4 = (bf16[16,1024]{1,0:T(8,128)(2,1)S(1)}, bf16[16,1024]{1,0:T(8,128)(2,1)S(1)}, u32[]{:S(2)}, u32[]{:S(2)}) collective-permute-start(bf16[16,1024]{1,0:T(8,128)(2,1)S(1)} %get-tuple-element.31), channel_id=1, source_target_pairs={{0,9},{1,10},{2,11},{3,12},{4,13},{5,14},{6,15},{7,8},{8,17},{9,18... | collective-permute-start | bytes 98312 | tf_op jit(solution)/shard_map/ppermute | solution.py:449
  35.2 6.8 %collective-permute-start.5 = (bf16[16,1024]{1,0:T(8,128)(2,1)S(1)}, bf16[16,1024]{1,0:T(8,128)(2,1)S(1)}, u32[]{:S(2)}, u32[]{:S(2)}) collective-permute-start(bf16[16,1024]{1,0:T(8,128)(2,1)S(1)} %get-tuple-element.32), channel_id=1, source_target_pairs={{0,1},{1,2},{2,3},{3,4},{4,5},{5,6},{6,7},{7,0},{8,9},{9,10},{10,1... | collective-permute-start | bytes 98312 | tf_op jit(solution)/shard_map/ppermute | solution.py:449

commit v7 on v3

--- a/solution.py
+++ b/solution.py
@@ -28,8 +28,8 @@
     quad = n // 16
     s = (n // 4) % 4
     g = n % 4
-    row = 4 * (quad % 4) + 2 * (g // 2) + s % 2
-    col = 4 * (quad // 4) + 2 * (g % 2) + s // 2
+    row = jnp.where(quad < 6, 4 + 4 * (quad % 3), 0) + 2 * (g // 2) + s % 2
+    col = jnp.where((quad < 3) | (quad == 7), 4, 0) + 2 * (g % 2) + s // 2
     return row, col, s
 
 
@@ -92,9 +92,28 @@
 
 
 def pack_kernel(
-    token_sort, cot_sort, label_row, label_col, tokens, labels, cot, own, lon, cot_rows
+    token_sort,
+    cot_sort,
+    label_row,
+    label_col,
+    tokens,
+    labels,
+    cot,
+    right,
+    left,
+    first_row,
+    first_left,
+    first_right,
+    cot_rows,
+
 ):
-    outs = ((own, 0, 64), (lon, 64, 128))
+    outs = (
+        (right, 0, 48),
+        (left, 48, 96),
+        (first_row, 96, 128),
+        (first_left, 96, 112),
+        (first_right, 112, 128),
+    )
     moved = mm(token_sort[...], tokens[...].reshape(128, D)).astype(bf16)
     for ref, lo, hi in outs:
         ref[:, 0:D] = moved[lo:hi]
@@ -116,7 +135,7 @@
 
 
 def pack(tokens, labels, cot, sorts):
-    shapes = [jax.ShapeDtypeStruct((64, WIDE), bf16)] * 2
+    shapes = [jax.ShapeDtypeStruct((n, WIDE), bf16) for n in (48, 48, 32, 16, 16)]
     return pl.pallas_call(
         pack_kernel,
         out_shape=shapes,
@@ -125,22 +144,6 @@
         cost_estimate=BUSY,
         name="pack",
     )(*sorts, tokens, labels, cot)
-
-
-def strips_kernel(own, lon, top, bottom):
-    top[0:16, :] = lon[0:16, :]
-    top[16:32, :] = own[0:16, :]
-    bottom[0:16, :] = lon[48:64, :]
-    bottom[16:32, :] = own[48:64, :]
-
-
-def strips(own, lon):
-    return pl.pallas_call(
-        strips_kernel,
-        out_shape=[jax.ShapeDtypeStruct((32, WIDE), bf16)] * 2,
-        compiler_params=pltpu.CompilerParams(vmem_limit_bytes=4 * MIB),
-        name="strips",
-    )(own, lon)
 
 
 def relative_bias(table, natural, ebias):
@@ -380,10 +383,12 @@
         grad = inv_s[:, cols] * (proj_s[:, cols] - unit_s[:, cols] * along[count * n : count * n + count])
         gpack_s[:, cols] = grad.astype(bf16)
 
+    spans = [slice(16 * n, 16 * n + 16) for n in kept]
+    gpack = jnp.concatenate([gpack_s[rows, :] for rows in spans], axis=0)
     for n in range(4):
         cols = slice(256 * n, 256 * n + 256)
-        total = mixed_s[kept, cols] + mm_nt(gpack_s[kept, :], w_qkv[cols, :])
-        emit(cols, total.astype(bf16))
+        mixed = jnp.concatenate([mixed_s[rows, cols] for rows in spans], axis=0)
+        emit(cols, (mixed + mm_nt(gpack, w_qkv[cols, :])).astype(bf16))
 
 
 def scratch_for(count):
@@ -407,89 +412,72 @@
     ]
 
 
-def inner_kernel(own, lon, *refs):
-    params, (out_own, out_lon), scratch = refs[:7], refs[7:9], refs[9:]
-    quads = ((lon, 16), (own, 16), (lon, 32), (own, 32))
+def main_kernel(right, left, east, west, below, below_east, below_west, *refs):
+    params, (out_own, out_below), scratch = refs[:7], refs[7:9], refs[9:]
+    quads = (
+        (east, 0),
+        (left, 0),
+        (east, 16),
+        (left, 16),
+        (east, 32),
+        (left, 32),
+        (below_east, 0),
+        (below, 0),
+        (right, 0),
+        (west, 0),
+        (right, 16),
+        (west, 16),
+        (right, 32),
+        (west, 32),
+        (below, 16),
+        (below_west, 0),
+    )
+    kept = (8, 10, 12, 1, 3, 5, 7, 14)
 
     def emit(cols, total):
-        out_lon[0:16, cols] = total[0:16]
-        out_own[0:16, cols] = total[16:32]
-        out_lon[16:32, cols] = total[32:48]
-        out_own[16:32, cols] = total[48:64]
-
-    windows(quads, slice(0, 64), emit, params, scratch)
-
-
-def inner(own, lon, params):
+        out_own[:, cols] = total[0:96]
+        out_below[:, cols] = total[96:128]
+
+    windows(quads, kept, emit, params, scratch)
+
+
+def main(blocks, params):
     return pl.pallas_call(
-        inner_kernel,
-        out_shape=[jax.ShapeDtypeStruct((32, D), bf16)] * 2,
-        scratch_shapes=scratch_for(64),
-        compiler_params=pltpu.CompilerParams(vmem_limit_bytes=16 * MIB),
+        main_kernel,
+        out_shape=[jax.ShapeDtypeStruct((n, D), bf16) for n in (96, 32)],
+        scratch_shapes=scratch_for(256),
+        compiler_params=pltpu.CompilerParams(vmem_limit_bytes=32 * MIB),
         cost_estimate=pl.CostEstimate(
             flops=3_000_000_000, bytes_accessed=6_000_000, transcendentals=150_000
         ),
-        name="inner",
-    )(own, lon, *params)
-
-
-def outer_kernel(own, lon, above, below, in_own, in_lon, *refs):
-    params, (out_own, out_lon), scratch = refs[:7], refs[7:9], refs[9:]
-    quads = (
-        (above, 0),
-        (above, 16),
-        (lon, 0),
-        (own, 0),
-        (lon, 48),
-        (own, 48),
-        (below, 0),
-        (below, 16),
-    )
-    out_own[16:48, :] = in_own[...]
-    out_lon[16:48, :] = in_lon[...]
-
-    def emit(cols, total):
-        out_lon[0:16, cols] = total[0:16]
-        out_own[0:16, cols] = total[16:32]
-        out_lon[48:64, cols] = total[32:48]
-        out_own[48:64, cols] = total[48:64]
-
-    windows(quads, slice(32, 96), emit, params, scratch)
-
-
-def outer(own, lon, above, below, in_own, in_lon, params):
-    return pl.pallas_call(
-        outer_kernel,
-        out_shape=[jax.ShapeDtypeStruct((64, D), bf16)] * 2,
-        scratch_shapes=scratch_for(128),
-        compiler_params=pltpu.CompilerParams(vmem_limit_bytes=24 * MIB),
-        cost_estimate=pl.CostEstimate(
-            flops=3_000_000_000, bytes_accessed=6_000_000, transcendentals=150_000
-        ),
-        name="outer",
-    )(own, lon, above, below, in_own, in_lon, *params)
-
-
-def final_kernel(own, lon, out):
-    rows = jnp.concatenate([own[...], lon[...]], axis=0)
+        name="main",
+    )(*blocks, *params)
+
+
+def final_kernel(own, first_row, out):
+    rows = jnp.concatenate([own[...], first_row[...]], axis=0)
     row, col, _ = sorted_place(iota((128, 128), 1))
     token_place = onehot(iota((128, 128), 0) == row * 8 + col)
     out[...] = mm(token_place, rows).reshape(16, 8, D).astype(bf16)
 
 
-def final(own, lon):
+def final(own, first_row):
     return pl.pallas_call(
         final_kernel,
         out_shape=jax.ShapeDtypeStruct((16, 8, D), bf16),
         compiler_params=pltpu.CompilerParams(vmem_limit_bytes=8 * MIB),
         name="final",
-    )(own, lon)
-
-
-def passed_along(block, axis, distance):
-    count = lax.axis_size(axis)
-    route = [(i, (i + distance) % count) for i in range(count)]
-    return lax.ppermute(block, axis, route)
+    )(own, first_row)
+
+
+def shift_by(block, lat_step, lon_step):
+    lats, lons = lax.axis_size("lat"), lax.axis_size("lon")
+    route = [
+        (j * lats + i, ((j + lon_step) % lons) * lats + (i + lat_step) % lats)
+        for j in range(lons)
+        for i in range(lats)
+    ]
+    return lax.ppermute(block, ("lon", "lat"), route)
 
 
 def shards(
@@ -504,8 +492,14 @@
     merge_gain,
     cotangent,
 ):
-    own, lon = pack(tokens, labels.T, cotangent, places())
-    lon = passed_along(lon, "lon", 1)
+    right, left, first_row, first_left, first_right = pack(
+        tokens, labels.T, cotangent, places()
+    )
+    east = shift_by(right, 0, 1)
+    west = shift_by(left, 0, -1)
+    below = shift_by(first_row, -1, 0)
+    below_east = shift_by(first_right, -1, 1)
+    below_west = shift_by(first_left, -1, -1)
     ebias, temper = prep(bias_table, logit_scale.reshape(1, HEADS))
     params = (
         ebias,
@@ -516,13 +510,9 @@
         norm_shift.reshape(1, D),
         merge_gain.reshape(1, 4 * D),
     )
-    top, bottom = strips(own, lon)
-    below = passed_along(top, "lat", -1)
-    above = passed_along(bottom, "lat", 1)
-    in_own, in_lon = inner(own, lon, params)
-    own, lon = outer(own, lon, above, below, in_own, in_lon, params)
-    lon = passed_along(lon, "lon", -1)
-    return final(own, lon)
+    blocks = (right, left, east, west, below, below_east, below_west)
+    own, below = main(blocks, params)
+    return final(own, shift_by(below, 1, 0))
 
 
 def solution(mesh):

time: 41.7 us -> 48.4 us (1.16)
  the two profiles are of different devices: /device:TPU:1 before, /device:TPU:8 now
where the time goes in v7:
time: 48.4 us; the launch traced here: 48.2 us
  starting transfers between devices  31.1 us (64%)
  Pallas kernels  9.8 us (20%)
  waiting for transfers between devices  6.2 us (13%)
  local copies, waits for them, and re-layouts  0.87 us (2%)
    ppermute x6, starting transfers between devices, shift_by(): return lax.ppermute(block, ('lon', 'lat'), route)  31.1 us
    pallas_call x1, Pallas kernels, main(): pl.pallas_call(main_kernel, out_shape=[jax.ShapeDtypeStruct((n, D), bf16)...  7.54 us
    ppermute x6, waiting for transfers between devices, shift_by(): return lax.ppermute(block, ('lon', 'lat'), route)  6.2 us
  transfers between devices with their start and end apart: 6, of which 2 were waited for; matrix products, arithmetic and copies ran while one was open for 0% of the time, Pallas kernels for 2%

profile of v7, /device:TPU:8, one launch (start us, length us, event | category | flops | bytes accessed | tf_op | source)
XLA Modules:
  0.0 48.2 jit_solution(13189108436219486965)
XLA Ops:
  0.0 0.0 copy-start.3
  0.0 0.0 copy-start.6
  0.0 0.0 copy-start.2
  0.0 0.2 places.1
  0.2 0.7 %copy-done.3 = bf16[8,4,4096]{2,1,0:T(4,128)(2,1)S(1)} copy-done((bf16[8,4,4096]{2,1,0:T(4,128)(2,1)S(1)}, bf16[8,4,4096]{2,1,0:T(4,128)(2,1)}, u32[]{:S(2)}) %copy-start.3) | copy-done | bytes 262168
  1.0 0.0 copy-done.6
  1.0 0.1 copy-done.2
  1.0 0.0 copy-start.4
  1.0 0.0 copy-start.9
  1.1 0.0 copy-start
  1.1 0.0 copy-start.1
  1.1 0.0 copy-start.5
  1.1 0.0 copy-start.7
  1.1 0.0 copy-start.8
  1.1 0.3 pack.1
  1.4 2.2 %collective-permute-start = (bf16[48,2176]{1,0:T(8,128)(2,1)S(1)}, bf16[48,2176]{1,0:T(8,128)(2,1)S(1)}, u32[]{:S(2)}, u32[]{:S(2)}) collective-permute-start(bf16[48,2176]{1,0:T(8,128)(2,1)S(1)} %get-tuple-element.22.right), channel_id=1, source_target_pairs={{0,8},{1,9},{2,10},{3,11},{4,12},{5,13},{6,14},{7,15},{8,16},{9,17... | collective-permute-start | bytes 626696 | tf_op jit(solution)/shard_map/ppermute | solution.py:480
  3.6 13.3 %collective-permute-start.1 = (bf16[48,2176]{1,0:T(8,128)(2,1)S(1)}, bf16[48,2176]{1,0:T(8,128)(2,1)S(1)}, u32[]{:S(2)}, u32[]{:S(2)}) collective-permute-start(bf16[48,2176]{1,0:T(8,128)(2,1)S(1)} %get-tuple-element.23.left), channel_id=1, source_target_pairs={{0,504},{1,505},{2,506},{3,507},{4,508},{5,509},{6,510},{7,511},{8... | collective-permute-start | bytes 626696 | tf_op jit(solution)/shard_map/ppermute | solution.py:480
  16.9 2.4 %collective-permute-start.2 = (bf16[32,2176]{1,0:T(8,128)(2,1)S(1)}, bf16[32,2176]{1,0:T(8,128)(2,1)S(1)}, u32[]{:S(2)}, u32[]{:S(2)}) collective-permute-start(bf16[32,2176]{1,0:T(8,128)(2,1)S(1)} %get-tuple-element.24), channel_id=1, source_target_pairs={{0,7},{1,0},{2,1},{3,2},{4,3},{5,4},{6,5},{7,6},{8,15},{9,8},{10,9... | collective-permute-start | bytes 417800 | tf_op jit(solution)/shard_map/ppermute | solution.py:480
  19.3 1.9 %collective-permute-start.3 = (bf16[16,2176]{1,0:T(8,128)(2,1)S(1)}, bf16[16,2176]{1,0:T(8,128)(2,1)S(1)}, u32[]{:S(2)}, u32[]{:S(2)}) collective-permute-start(bf16[16,2176]{1,0:T(8,128)(2,1)S(1)} %get-tuple-element.25), channel_id=1, source_target_pairs={{0,15},{1,8},{2,9},{3,10},{4,11},{5,12},{6,13},{7,14},{8,23},{9,16... | collective-permute-start | bytes 208904 | tf_op jit(solution)/shard_map/ppermute | solution.py:480
  21.2 9.4 %collective-permute-start.4 = (bf16[16,2176]{1,0:T(8,128)(2,1)S(1)}, bf16[16,2176]{1,0:T(8,128)(2,1)S(1)}, u32[]{:S(2)}, u32[]{:S(2)}) collective-permute-start(bf16[16,2176]{1,0:T(8,128)(2,1)S(1)} %get-tuple-element.26), channel_id=1, source_target_pairs={{0,511},{1,504},{2,505},{3,506},{4,507},{5,508},{6,509},{7,510},{8... | collective-permute-start | bytes 208904 | tf_op jit(solution)/shard_map/ppermute | solution.py:480
  30.7 0.0 copy-done.4
  30.7 0.0 copy-done.9
  30.7 0.8 %prep.1 = (f32[64,1024]{1,0:T(8,128)S(1)}, f32[1,512]{1,0:T(1,128)S(1)}) custom-call(f32[16,225]{1,0:T(8,128)S(1)} %copy-done.4, f32[1,16]{1,0:T(1,128)S(1)} %bitcast.9), custom_call_target="tpu_custom_call" | custom-call | flops 100000000 | bytes 400000 | tf_op jit(solution)/shard_map/prep/pallas_call | solution.py:191
  31.5 0.0 collective-permute-done.3.below_east
  31.5 1.1 %collective-permute-done.4.below_west = bf16[16,2176]{1,0:T(8,128)(2,1)S(1)} collective-permute-done((bf16[16,2176]{1,0:T(8,128)(2,1)S(1)}, bf16[16,2176]{1,0:T(8,128)(2,1)S(1)}, u32[]{:S(2)}, u32[]{:S(2)}) %collective-permute-start.4) | collective-permute-done | bytes 69664 | tf_op jit(solution)/shard_map/ppermute | solution.py:480
  32.6 0.0 collective-permute-done.2.below
  32.6 0.0 collective-permute-done.east
  32.6 0.0 collective-permute-done.1.west
  32.6 0.0 copy-done
  32.6 0.0 copy-done.1
  32.6 0.0 copy-done.5
  32.6 0.0 copy-done.7
  32.6 0.0 copy-done.8
  32.6 7.5 %main.1 = (bf16[96,1024]{1,0:T(8,128)(2,1)S(1)}, bf16[32,1024]{1,0:T(8,128)(2,1)S(1)}) custom-call(bf16[48,2176]{1,0:T(8,128)(2,1)S(1)} %get-tuple-element.22.right, bf16[48,2176]{1,0:T(8,128)(2,1)S(1)} %get-tuple-element.23.left, bf16[48,2176]{1,0:T(8,128)(2,1)S(1)} %collective-permute-done.east, bf16[48,2176]{1,0:T(8,128)(2,1)S(1)} %collective-permute-done.1.west, ...), custom_call_target="tpu_custom_call" | custom-call | flops 3000000000 | bytes 6000000 | tf_op jit(solution)/shard_map/main/pallas_call | solution.py:445
  40.2 1.9 %collective-permute-start.5 = (bf16[32,1024]{1,0:T(8,128)(2,1)S(1)}, bf16[32,1024]{1,0:T(8,128)(2,1)S(1)}, u32[]{:S(2)}, u32[]{:S(2)}) collective-permute-start(bf16[32,1024]{1,0:T(8,128)(2,1)S(1)} %get-tuple-element.30), channel_id=1, source_target_pairs={{0,1},{1,2},{2,3},{3,4},{4,5},{5,6},{6,7},{7,0},{8,9},{9,10},{10,1... | collective-permute-start | bytes 196616 | tf_op jit(solution)/shard_map/ppermute | solution.py:480
  42.1 5.1 %collective-permute-done.5.first_row = bf16[32,1024]{1,0:T(8,128)(2,1)S(1)} collective-permute-done((bf16[32,1024]{1,0:T(8,128)(2,1)S(1)}, bf16[32,1024]{1,0:T(8,128)(2,1)S(1)}, u32[]{:S(2)}, u32[]{:S(2)}) %collective-permute-start.5) | collective-permute-done | bytes 65568 | tf_op jit(solution)/shard_map/ppermute | solution.py:480
  47.3 0.9 %final.1 = bf16[16,8,1024]{2,1,0:T(8,128)(2,1)} custom-call(bf16[96,1024]{1,0:T(8,128)(2,1)S(1)} %get-tuple-element.29.own, bf16[32,1024]{1,0:T(8,128)(2,1)S(1)} %collective-permute-done.5.first_row), custom_call_target="tpu_custom_call" | custom-call | tf_op jit(solution)/shard_map/final/pallas_call | solution.py:465
Async XLA Ops:
  0.0 0.9 %copy-start.3 = (bf16[8,4,4096]{2,1,0:T(4,128)(2,1)S(1)}, bf16[8,4,4096]{2,1,0:T(4,128)(2,1)}, u32[]{:S(2)}) copy-start(bf16[8,4,4096]{2,1,0:T(4,128)(2,1)} %cot.1) | copy-start | bytes 786436
  0.0 1.0 %copy-start.6 = (s32[16,8]{0,1:T(8,128)S(1)}, s32[16,8]{0,1:T(8,128)}, u32[]{:S(2)}) copy-start(s32[16,8]{0,1:T(8,128)} %param.11) | copy-start | bytes 1540
  0.0 1.0 %copy-start.2 = (bf16[16,8,1024]{2,1,0:T(8,128)(2,1)S(1)}, bf16[16,8,1024]{2,1,0:T(8,128)(2,1)}, u32[]{:S(2)}) copy-start(bf16[16,8,1024]{2,1,0:T(8,128)(2,1)} %tokens.1) | copy-start | bytes 786436
  1.0 29.6 %copy-start.4 = (f32[16,225]{1,0:T(8,128)S(1)}, f32[16,225]{1,0:T(8,128)}, u32[]{:S(2)}) copy-start(f32[16,225]{1,0:T(8,128)} %table.1) | copy-start | bytes 43204
  1.0 29.6 %copy-start.9 = (f32[16]{0:T(128)S(1)}, f32[16]{0:T(128)}, u32[]{:S(2)}) copy-start(f32[16]{0:T(128)} %param.14) | copy-start | bytes 196
  1.1 31.5 %copy-start = (bf16[1024,1536]{1,0:T(8,128)(2,1)S(1)}, bf16[1024,1536]{1,0:T(8,128)(2,1)}, u32[]{:S(2)}) copy-start(bf16[1024,1536]{1,0:T(8,128)(2,1)} %refs_2_.1) | copy-start | bytes 9437188
  1.1 31.6 %copy-start.1 = (bf16[512,1024]{1,0:T(8,128)(2,1)S(1)}, bf16[512,1024]{1,0:T(8,128)(2,1)}, u32[]{:S(2)}) copy-start(bf16[512,1024]{1,0:T(8,128)(2,1)} %refs_3_.1) | copy-start | bytes 3145732
  1.1 31.6 %copy-start.5 = (f32[4096]{0:T(1024)S(1)}, f32[4096]{0:T(1024)}, u32[]{:S(2)}) copy-start(f32[4096]{0:T(1024)} %param.18) | copy-start | bytes 49156
  1.1 31.6 %copy-start.7 = (f32[1024]{0:T(1024)S(1)}, f32[1024]{0:T(1024)}, u32[]{:S(2)}) copy-start(f32[1024]{0:T(1024)} %param.16) | copy-start | bytes 12292
  1.1 31.6 %copy-start.8 = (f32[1024]{0:T(1024)S(1)}, f32[1024]{0:T(1024)}, u32[]{:S(2)}) copy-start(f32[1024]{0:T(1024)} %param.17) | copy-start | bytes 12292
  1.4 31.2 %collective-permute-start = (bf16[48,2176]{1,0:T(8,128)(2,1)S(1)}, bf16[48,2176]{1,0:T(8,128)(2,1)S(1)}, u32[]{:S(2)}, u32[]{:S(2)}) collective-permute-start(bf16[48,2176]{1,0:T(8,128)(2,1)S(1)} %get-tuple-element.22.right), channel_id=1, source_target_pairs={{0,8},{1,9},{2,10},{3,11},{4,12},{5,13},{6,14},{7,15},{8,16},{9,17... | collective-permute-start | bytes 626696 | tf_op jit(solution)/shard_map/ppermute | solution.py:480
  3.6 29.0 %collective-permute-start.1 = (bf16[48,2176]{1,0:T(8,128)(2,1)S(1)}, bf16[48,2176]{1,0:T(8,128)(2,1)S(1)}, u32[]{:S(2)}, u32[]{:S(2)}) collective-permute-start(bf16[48,2176]{1,0:T(8,128)(2,1)S(1)} %get-tuple-element.23.left), channel_id=1, source_target_pairs={{0,504},{1,505},{2,506},{3,507},{4,508},{5,509},{6,510},{7,511},{8... | collective-permute-start | bytes 626696 | tf_op jit(solution)/shard_map/ppermute | solution.py:480
  16.9 15.7 %collective-permute-start.2 = (bf16[32,2176]{1,0:T(8,128)(2,1)S(1)}, bf16[32,2176]{1,0:T(8,128)(2,1)S(1)}, u32[]{:S(2)}, u32[]{:S(2)}) collective-permute-start(bf16[32,2176]{1,0:T(8,128)(2,1)S(1)} %get-tuple-element.24), channel_id=1, source_target_pairs={{0,7},{1,0},{2,1},{3,2},{4,3},{5,4},{6,5},{7,6},{8,15},{9,8},{10,9... | collective-permute-start | bytes 417800 | tf_op jit(solution)/shard_map/ppermute | solution.py:480
  19.3 12.2 %collective-permute-start.3 = (bf16[16,2176]{1,0:T(8,128)(2,1)S(1)}, bf16[16,2176]{1,0:T(8,128)(2,1)S(1)}, u32[]{:S(2)}, u32[]{:S(2)}) collective-permute-start(bf16[16,2176]{1,0:T(8,128)(2,1)S(1)} %get-tuple-element.25), channel_id=1, source_target_pairs={{0,15},{1,8},{2,9},{3,10},{4,11},{5,12},{6,13},{7,14},{8,23},{9,16... | collective-permute-start | bytes 208904 | tf_op jit(solution)/shard_map/ppermute | solution.py:480
  21.2 11.3 %collective-permute-start.4 = (bf16[16,2176]{1,0:T(8,128)(2,1)S(1)}, bf16[16,2176]{1,0:T(8,128)(2,1)S(1)}, u32[]{:S(2)}, u32[]{:S(2)}) collective-permute-start(bf16[16,2176]{1,0:T(8,128)(2,1)S(1)} %get-tuple-element.26), channel_id=1, source_target_pairs={{0,511},{1,504},{2,505},{3,506},{4,507},{5,508},{6,509},{7,510},{8... | collective-permute-start | bytes 208904 | tf_op jit(solution)/shard_map/ppermute | solution.py:480
  40.2 7.1 %collective-permute-start.5 = (bf16[32,1024]{1,0:T(8,128)(2,1)S(1)}, bf16[32,1024]{1,0:T(8,128)(2,1)S(1)}, u32[]{:S(2)}, u32[]{:S(2)}) collective-permute-start(bf16[32,1024]{1,0:T(8,128)(2,1)S(1)} %get-tuple-element.30), channel_id=1, source_target_pairs={{0,1},{1,2},{2,3},{3,4},{4,5},{5,6},{6,7},{7,0},{8,9},{9,10},{10,1... | collective-permute-start | bytes 196616 | tf_op jit(solution)/shard_map/ppermute | solution.py:480

commit v8 on v4

--- a/solution.py
+++ b/solution.py
@@ -386,6 +386,7 @@
         grad = inv_s[:, cols] * (proj_s[:, cols] - unit_s[:, cols] * along[cols])
         gpack_s[:, cols] = grad.astype(bf16)
 
+    out_lat[16:64, :] = jnp.zeros((48, D), bf16)
     for n in range(4):
         cols = slice(256 * n, 256 * n + 256)
         total = (mixed_s[:, cols] + mm_nt(gpack_s[...], w_qkv[cols, :])).astype(bf16)
@@ -396,7 +397,7 @@
 def main(own, lon, dia, lat, *params):
     return pl.pallas_call(
         main_kernel,
-        out_shape=[jax.ShapeDtypeStruct((n, D), bf16) for n in (48, 48, 16, 16)],
+        out_shape=[jax.ShapeDtypeStruct((n, D), bf16) for n in (48, 48, 64, 16)],
         scratch_shapes=[
             pltpu.VMEM((128, D), bf16),
             pltpu.VMEM((128, 3 * ATT), bf16),
@@ -424,7 +425,7 @@
 
 
 def final_kernel(own, lat, lon, dia, out):
-    rows = jnp.concatenate([own[...], lon[...], lat[...], dia[...]], axis=0)
+    rows = jnp.concatenate([own[...], lon[...], lat[0:16, :], dia[...]], axis=0)
     row, col, _ = sorted_place(iota((128, 128), 1))
     token_place = onehot(iota((128, 128), 0) == row * 8 + col)
     out[...] = mm(token_place, rows).reshape(16, 8, D).astype(bf16)

time: 40.9 us -> 41.3 us (level)
  no operation moved by 1% of the time
where the time goes in v8:
time: 41.3 us; the launch traced here: 41 us
  starting transfers between devices  23.3 us (56%)
  waiting for transfers between devices  9.6 us (23%)
  Pallas kernels  7.03 us (17%)
  local copies, waits for them, and re-layouts  0.87 us (2%)
    ppermute x6, starting transfers between devices, shift_by(): return lax.ppermute(block, ('lon', 'lat'), route)  23.3 us
    ppermute x6, waiting for transfers between devices, shift_by(): return lax.ppermute(block, ('lon', 'lat'), route)  9.6 us
    pallas_call x1, Pallas kernels, main(): pl.pallas_call(main_kernel, out_shape=[jax.ShapeDtypeStruct((n, D), bf16)...  4.76 us
    pallas_call x1, Pallas kernels, final(): pl.pallas_call(final_kernel, out_shape=jax.ShapeDtypeStruct((16, 8, D), b...  0.93 us
    unnamed x20, local copies, waits for them, and re-layouts  0.87 us
  transfers between devices with their start and end apart: 6, of which 2 were waited for; matrix products, arithmetic and copies ran while one was open for 0% of the time, Pallas kernels for 2%

profile of v8, /device:TPU:24, one launch (start us, length us, event | category | flops | bytes accessed | tf_op | source)
XLA Modules:
  0.0 41.0 jit_solution(1733702667040350743)
XLA Ops:
  0.0 0.0 copy-start.3
  0.0 0.0 copy-start.6
  0.0 0.0 copy-start.2
  0.0 0.2 places.1
  0.2 0.7 %copy-done.3 = bf16[8,4,4096]{2,1,0:T(4,128)(2,1)S(1)} copy-done((bf16[8,4,4096]{2,1,0:T(4,128)(2,1)S(1)}, bf16[8,4,4096]{2,1,0:T(4,128)(2,1)}, u32[]{:S(2)}) %copy-start.3) | copy-done | bytes 262168
  1.0 0.0 copy-done.6
  1.0 0.1 copy-done.2
  1.0 0.0 copy-start.4
  1.0 0.0 copy-start.9
  1.1 0.0 copy-start
  1.1 0.0 copy-start.1
  1.1 0.0 copy-start.5
  1.1 0.0 copy-start.7
  1.1 0.0 copy-start.8
  1.1 0.3 pack.1
  1.4 2.2 %collective-permute-start = (bf16[48,2176]{1,0:T(8,128)(2,1)S(1)}, bf16[48,2176]{1,0:T(8,128)(2,1)S(1)}, u32[]{:S(2)}, u32[]{:S(2)}) collective-permute-start(bf16[48,2176]{1,0:T(8,128)(2,1)S(1)} %get-tuple-element.24), channel_id=1, source_target_pairs={{0,8},{1,9},{2,10},{3,11},{4,12},{5,13},{6,14},{7,15},{8,16},{9,17... | collective-permute-start | bytes 626696 | tf_op jit(solution)/shard_map/ppermute | solution.py:450
  3.6 5.2 %collective-permute-start.1 = (bf16[16,2176]{1,0:T(8,128)(2,1)S(1)}, bf16[16,2176]{1,0:T(8,128)(2,1)S(1)}, u32[]{:S(2)}, u32[]{:S(2)}) collective-permute-start(bf16[16,2176]{1,0:T(8,128)(2,1)S(1)} %get-tuple-element.25), channel_id=1, source_target_pairs={{0,15},{1,8},{2,9},{3,10},{4,11},{5,12},{6,13},{7,14},{8,23},{9,16... | collective-permute-start | bytes 208904 | tf_op jit(solution)/shard_map/ppermute | solution.py:450
  8.8 2.4 %collective-permute-start.2 = (bf16[16,2176]{1,0:T(8,128)(2,1)S(1)}, bf16[16,2176]{1,0:T(8,128)(2,1)S(1)}, u32[]{:S(2)}, u32[]{:S(2)}) collective-permute-start(bf16[16,2176]{1,0:T(8,128)(2,1)S(1)} %get-tuple-element.26), channel_id=1, source_target_pairs={{0,7},{1,0},{2,1},{3,2},{4,3},{5,4},{6,5},{7,6},{8,15},{9,8},{10,9... | collective-permute-start | bytes 208904 | tf_op jit(solution)/shard_map/ppermute | solution.py:450
  11.3 0.0 copy-done.4
  11.3 0.0 copy-done.9
  11.3 0.8 %prep.1 = (f32[64,1024]{1,0:T(8,128)S(1)}, f32[1,512]{1,0:T(1,128)S(1)}) custom-call(f32[16,225]{1,0:T(8,128)S(1)} %copy-done.4, f32[1,16]{1,0:T(1,128)S(1)} %bitcast.9), custom_call_target="tpu_custom_call" | custom-call | flops 100000000 | bytes 400000 | tf_op jit(solution)/shard_map/prep/pallas_call | solution.py:172
  12.1 7.2 %collective-permute-done.1.dia = bf16[16,2176]{1,0:T(8,128)(2,1)S(1)} collective-permute-done((bf16[16,2176]{1,0:T(8,128)(2,1)S(1)}, bf16[16,2176]{1,0:T(8,128)(2,1)S(1)}, u32[]{:S(2)}, u32[]{:S(2)}) %collective-permute-start.1) | collective-permute-done | bytes 69664 | tf_op jit(solution)/shard_map/ppermute | solution.py:450
  19.3 0.0 collective-permute-done.2.lat
  19.3 0.0 collective-permute-done.lon
  19.3 0.0 copy-done
  19.3 0.0 copy-done.1
  19.3 0.0 copy-done.5
  19.3 0.0 copy-done.7
  19.3 0.0 copy-done.8
  19.4 4.8 %main.1 = (bf16[48,1024]{1,0:T(8,128)(2,1)S(1)}, bf16[48,1024]{1,0:T(8,128)(2,1)S(1)}, bf16[64,1024]{1,0:T(8,128)(2,1)S(1)}, bf16[16,1024]{1,0:T(8,128)(2,1)S(1)}) custom-call(bf16[48,2176]{1,0:T(8,128)(2,1)S(1)} %get-tuple-element.23.own, bf16[48,2176]{1,0:T(8,128)(2,1)S(1)} %collective-permute-done.lon, bf16[16,2176]{1,0:T(8,128)(2,1)S(1)} %collective-permute-done.1.dia, ...), custom_call_target="tpu_custom_call" | custom-call | flops 1500000000 | bytes 6000000 | tf_op jit(solution)/shard_map/main/pallas_call | solution.py:398
  24.1 2.4 %collective-permute-start.3 = (bf16[64,1024]{1,0:T(8,128)(2,1)S(1)}, bf16[64,1024]{1,0:T(8,128)(2,1)S(1)}, u32[]{:S(2)}, u32[]{:S(2)}) collective-permute-start(bf16[64,1024]{1,0:T(8,128)(2,1)S(1)} %get-tuple-element.30), channel_id=1, source_target_pairs={{0,1},{1,2},{2,3},{3,4},{4,5},{5,6},{6,7},{7,0},{8,9},{9,10},{10,1... | collective-permute-start | bytes 393224 | tf_op jit(solution)/shard_map/ppermute | solution.py:450
  26.5 7.4 %collective-permute-start.4 = (bf16[48,1024]{1,0:T(8,128)(2,1)S(1)}, bf16[48,1024]{1,0:T(8,128)(2,1)S(1)}, u32[]{:S(2)}, u32[]{:S(2)}) collective-permute-start(bf16[48,1024]{1,0:T(8,128)(2,1)S(1)} %get-tuple-element.31), channel_id=1, source_target_pairs={{0,504},{1,505},{2,506},{3,507},{4,508},{5,509},{6,510},{7,511},{8... | collective-permute-start | bytes 294920 | tf_op jit(solution)/shard_map/ppermute | solution.py:450
  33.9 3.7 %collective-permute-start.5 = (bf16[16,1024]{1,0:T(8,128)(2,1)S(1)}, bf16[16,1024]{1,0:T(8,128)(2,1)S(1)}, u32[]{:S(2)}, u32[]{:S(2)}) collective-permute-start(bf16[16,1024]{1,0:T(8,128)(2,1)S(1)} %get-tuple-element.32), channel_id=1, source_target_pairs={{0,505},{1,506},{2,507},{3,508},{4,509},{5,510},{6,511},{7,504},{8... | collective-permute-start | bytes 98312 | tf_op jit(solution)/shard_map/ppermute | solution.py:450
  37.7 2.4 %collective-permute-done.5.dia = bf16[16,1024]{1,0:T(8,128)(2,1)S(1)} collective-permute-done((bf16[16,1024]{1,0:T(8,128)(2,1)S(1)}, bf16[16,1024]{1,0:T(8,128)(2,1)S(1)}, u32[]{:S(2)}, u32[]{:S(2)}) %collective-permute-start.5) | collective-permute-done | bytes 32800 | tf_op jit(solution)/shard_map/ppermute | solution.py:450
  40.1 0.0 collective-permute-done.4.lon
  40.1 0.0 collective-permute-done.3.lat
  40.1 0.9 %final.1 = bf16[16,8,1024]{2,1,0:T(8,128)(2,1)} custom-call(bf16[48,1024]{1,0:T(8,128)(2,1)S(1)} %get-tuple-element.29.own, bf16[64,1024]{1,0:T(8,128)(2,1)S(1)} %collective-permute-done.3.lat, bf16[48,1024]{1,0:T(8,128)(2,1)S(1)} %collective-permute-done.4.lon, bf16[16,1024]{1,0:T(8,128)(2,1)S(1)} %collective-permute-done.5.dia), custom_call_target="tpu_custom_call" | custom-call | tf_op jit(solution)/shard_map/final/pallas_call | solution.py:435
Async XLA Ops:
  0.0 0.9 %copy-start.3 = (bf16[8,4,4096]{2,1,0:T(4,128)(2,1)S(1)}, bf16[8,4,4096]{2,1,0:T(4,128)(2,1)}, u32[]{:S(2)}) copy-start(bf16[8,4,4096]{2,1,0:T(4,128)(2,1)} %cot.1) | copy-start | bytes 786436
  0.0 1.0 %copy-start.6 = (s32[16,8]{0,1:T(8,128)S(1)}, s32[16,8]{0,1:T(8,128)}, u32[]{:S(2)}) copy-start(s32[16,8]{0,1:T(8,128)} %param.11) | copy-start | bytes 1540
  0.0 1.0 %copy-start.2 = (bf16[16,8,1024]{2,1,0:T(8,128)(2,1)S(1)}, bf16[16,8,1024]{2,1,0:T(8,128)(2,1)}, u32[]{:S(2)}) copy-start(bf16[16,8,1024]{2,1,0:T(8,128)(2,1)} %tokens.1) | copy-start | bytes 786436
  1.0 10.2 %copy-start.4 = (f32[16,225]{1,0:T(8,128)S(1)}, f32[16,225]{1,0:T(8,128)}, u32[]{:S(2)}) copy-start(f32[16,225]{1,0:T(8,128)} %table.1) | copy-start | bytes 43204
  1.0 10.2 %copy-start.9 = (f32[16]{0:T(128)S(1)}, f32[16]{0:T(128)}, u32[]{:S(2)}) copy-start(f32[16]{0:T(128)} %param.14) | copy-start | bytes 196
  1.1 18.3 %copy-start = (bf16[1024,1536]{1,0:T(8,128)(2,1)S(1)}, bf16[1024,1536]{1,0:T(8,128)(2,1)}, u32[]{:S(2)}) copy-start(bf16[1024,1536]{1,0:T(8,128)(2,1)} %w_qkv.1) | copy-start | bytes 9437188
  1.1 18.3 %copy-start.1 = (bf16[512,1024]{1,0:T(8,128)(2,1)S(1)}, bf16[512,1024]{1,0:T(8,128)(2,1)}, u32[]{:S(2)}) copy-start(bf16[512,1024]{1,0:T(8,128)(2,1)} %w_proj.1) | copy-start | bytes 3145732
  1.1 18.3 %copy-start.5 = (f32[4096]{0:T(1024)S(1)}, f32[4096]{0:T(1024)}, u32[]{:S(2)}) copy-start(f32[4096]{0:T(1024)} %param.18) | copy-start | bytes 49156
  1.1 18.3 %copy-start.7 = (f32[1024]{0:T(1024)S(1)}, f32[1024]{0:T(1024)}, u32[]{:S(2)}) copy-start(f32[1024]{0:T(1024)} %param.16) | copy-start | bytes 12292
  1.1 18.3 %copy-start.8 = (f32[1024]{0:T(1024)S(1)}, f32[1024]{0:T(1024)}, u32[]{:S(2)}) copy-start(f32[1024]{0:T(1024)} %param.17) | copy-start | bytes 12292
  1.4 17.9 %collective-permute-start = (bf16[48,2176]{1,0:T(8,128)(2,1)S(1)}, bf16[48,2176]{1,0:T(8,128)(2,1)S(1)}, u32[]{:S(2)}, u32[]{:S(2)}) collective-permute-start(bf16[48,2176]{1,0:T(8,128)(2,1)S(1)} %get-tuple-element.24), channel_id=1, source_target_pairs={{0,8},{1,9},{2,10},{3,11},{4,12},{5,13},{6,14},{7,15},{8,16},{9,17... | collective-permute-start | bytes 626696 | tf_op jit(solution)/shard_map/ppermute | solution.py:450
  3.6 15.7 %collective-permute-start.1 = (bf16[16,2176]{1,0:T(8,128)(2,1)S(1)}, bf16[16,2176]{1,0:T(8,128)(2,1)S(1)}, u32[]{:S(2)}, u32[]{:S(2)}) collective-permute-start(bf16[16,2176]{1,0:T(8,128)(2,1)S(1)} %get-tuple-element.25), channel_id=1, source_target_pairs={{0,15},{1,8},{2,9},{3,10},{4,11},{5,12},{6,13},{7,14},{8,23},{9,16... | collective-permute-start | bytes 208904 | tf_op jit(solution)/shard_map/ppermute | solution.py:450
  8.8 10.5 %collective-permute-start.2 = (bf16[16,2176]{1,0:T(8,128)(2,1)S(1)}, bf16[16,2176]{1,0:T(8,128)(2,1)S(1)}, u32[]{:S(2)}, u32[]{:S(2)}) collective-permute-start(bf16[16,2176]{1,0:T(8,128)(2,1)S(1)} %get-tuple-element.26), channel_id=1, source_target_pairs={{0,7},{1,0},{2,1},{3,2},{4,3},{5,4},{6,5},{7,6},{8,15},{9,8},{10,9... | collective-permute-start | bytes 208904 | tf_op jit(solution)/shard_map/ppermute | solution.py:450
  24.1 15.9 %collective-permute-start.3 = (bf16[64,1024]{1,0:T(8,128)(2,1)S(1)}, bf16[64,1024]{1,0:T(8,128)(2,1)S(1)}, u32[]{:S(2)}, u32[]{:S(2)}) collective-permute-start(bf16[64,1024]{1,0:T(8,128)(2,1)S(1)} %get-tuple-element.30), channel_id=1, source_target_pairs={{0,1},{1,2},{2,3},{3,4},{4,5},{5,6},{6,7},{7,0},{8,9},{9,10},{10,1... | collective-permute-start | bytes 393224 | tf_op jit(solution)/shard_map/ppermute | solution.py:450
  26.5 13.5 %collective-permute-start.4 = (bf16[48,1024]{1,0:T(8,128)(2,1)S(1)}, bf16[48,1024]{1,0:T(8,128)(2,1)S(1)}, u32[]{:S(2)}, u32[]{:S(2)}) collective-permute-start(bf16[48,1024]{1,0:T(8,128)(2,1)S(1)} %get-tuple-element.31), channel_id=1, source_target_pairs={{0,504},{1,505},{2,506},{3,507},{4,508},{5,509},{6,510},{7,511},{8... | collective-permute-start | bytes 294920 | tf_op jit(solution)/shard_map/ppermute | solution.py:450
  33.9 6.1 %collective-permute-start.5 = (bf16[16,1024]{1,0:T(8,128)(2,1)S(1)}, bf16[16,1024]{1,0:T(8,128)(2,1)S(1)}, u32[]{:S(2)}, u32[]{:S(2)}) collective-permute-start(bf16[16,1024]{1,0:T(8,128)(2,1)S(1)} %get-tuple-element.32), channel_id=1, source_target_pairs={{0,505},{1,506},{2,507},{3,508},{4,509},{5,510},{6,511},{7,504},{8... | collective-permute-start | bytes 98312 | tf_op jit(solution)/shard_map/ppermute | solution.py:450

commit v9 on v4

--- a/solution.py
+++ b/solution.py
@@ -423,7 +423,7 @@
     )(own, lon, dia, lat, *params)
 
 
-def final_kernel(own, lat, lon, dia, out):
+def final_kernel(own, lon, dia, lat, out):
     rows = jnp.concatenate([own[...], lon[...], lat[...], dia[...]], axis=0)
     row, col, _ = sorted_place(iota((128, 128), 1))
     token_place = onehot(iota((128, 128), 0) == row * 8 + col)
@@ -436,7 +436,7 @@
         out_shape=jax.ShapeDtypeStruct((16, 8, D), bf16),
         compiler_params=pltpu.CompilerParams(vmem_limit_bytes=8 * MIB),
         name="final",
-    )(own, lat, lon, dia)
+    )(own, lon, dia, lat)
 
 
 def shift_by(block, lat_step, lon_step):

time: 40.9 us -> 42.4 us (1.037)
  waiting for transfers between devices: 9.54 us -> 11.4 us
    ppermute x6, waiting for transfers between devices: 9.54 us -> 11.4 us  [shift_by(): return lax.ppermute(block, ('lon', 'lat'), route)]
where the time goes in v9:
time: 42.4 us; the launch traced here: 42.2 us
  starting transfers between devices  22.7 us (54%)
  waiting for transfers between devices  11.4 us (27%)
  Pallas kernels  7.03 us (17%)
  local copies, waits for them, and re-layouts  0.87 us (2%)
    ppermute x6, starting transfers between devices, shift_by(): return lax.ppermute(block, ('lon', 'lat'), route)  22.7 us
    ppermute x6, waiting for transfers between devices, shift_by(): return lax.ppermute(block, ('lon', 'lat'), route)  11.4 us
    pallas_call x1, Pallas kernels, main(): pl.pallas_call(main_kernel, out_shape=[jax.ShapeDtypeStruct((n, D), bf16)...  4.76 us
    pallas_call x1, Pallas kernels, final(): pl.pallas_call(final_kernel, out_shape=jax.ShapeDtypeStruct((16, 8, D), b...  0.93 us
    unnamed x20, local copies, waits for them, and re-layouts  0.87 us
  transfers between devices with their start and end apart: 6, of which 2 were waited for; matrix products, arithmetic and copies ran while one was open for 0% of the time, Pallas kernels for 2%

profile of v9, /device:TPU:24, one launch (start us, length us, event | category | flops | bytes accessed | tf_op | source)
XLA Modules:
  0.0 42.2 jit_solution(10143213626420941604)
XLA Ops:
  0.0 0.0 copy-start.3
  0.0 0.0 copy-start.6
  0.0 0.0 copy-start.2
  0.0 0.2 places.1
  0.2 0.7 %copy-done.3 = bf16[8,4,4096]{2,1,0:T(4,128)(2,1)S(1)} copy-done((bf16[8,4,4096]{2,1,0:T(4,128)(2,1)S(1)}, bf16[8,4,4096]{2,1,0:T(4,128)(2,1)}, u32[]{:S(2)}) %copy-start.3) | copy-done | bytes 262168
  1.0 0.0 copy-done.6
  1.0 0.1 copy-done.2
  1.0 0.0 copy-start.4
  1.0 0.0 copy-start.9
  1.1 0.0 copy-start
  1.1 0.0 copy-start.1
  1.1 0.0 copy-start.5
  1.1 0.0 copy-start.7
  1.1 0.0 copy-start.8
  1.1 0.3 pack.1
  1.4 2.2 %collective-permute-start = (bf16[48,2176]{1,0:T(8,128)(2,1)S(1)}, bf16[48,2176]{1,0:T(8,128)(2,1)S(1)}, u32[]{:S(2)}, u32[]{:S(2)}) collective-permute-start(bf16[48,2176]{1,0:T(8,128)(2,1)S(1)} %get-tuple-element.24), channel_id=1, source_target_pairs={{0,8},{1,9},{2,10},{3,11},{4,12},{5,13},{6,14},{7,15},{8,16},{9,17... | collective-permute-start | bytes 626696 | tf_op jit(solution)/shard_map/ppermute | solution.py:449
  3.6 5.2 %collective-permute-start.1 = (bf16[16,2176]{1,0:T(8,128)(2,1)S(1)}, bf16[16,2176]{1,0:T(8,128)(2,1)S(1)}, u32[]{:S(2)}, u32[]{:S(2)}) collective-permute-start(bf16[16,2176]{1,0:T(8,128)(2,1)S(1)} %get-tuple-element.25), channel_id=1, source_target_pairs={{0,15},{1,8},{2,9},{3,10},{4,11},{5,12},{6,13},{7,14},{8,23},{9,16... | collective-permute-start | bytes 208904 | tf_op jit(solution)/shard_map/ppermute | solution.py:449
  8.8 2.4 %collective-permute-start.2 = (bf16[16,2176]{1,0:T(8,128)(2,1)S(1)}, bf16[16,2176]{1,0:T(8,128)(2,1)S(1)}, u32[]{:S(2)}, u32[]{:S(2)}) collective-permute-start(bf16[16,2176]{1,0:T(8,128)(2,1)S(1)} %get-tuple-element.26), channel_id=1, source_target_pairs={{0,7},{1,0},{2,1},{3,2},{4,3},{5,4},{6,5},{7,6},{8,15},{9,8},{10,9... | collective-permute-start | bytes 208904 | tf_op jit(solution)/shard_map/ppermute | solution.py:449
  11.3 0.0 copy-done.4
  11.3 0.0 copy-done.9
  11.3 0.8 %prep.1 = (f32[64,1024]{1,0:T(8,128)S(1)}, f32[1,512]{1,0:T(1,128)S(1)}) custom-call(f32[16,225]{1,0:T(8,128)S(1)} %copy-done.4, f32[1,16]{1,0:T(1,128)S(1)} %bitcast.9), custom_call_target="tpu_custom_call" | custom-call | flops 100000000 | bytes 400000 | tf_op jit(solution)/shard_map/prep/pallas_call | solution.py:172
  12.1 7.2 %collective-permute-done.1.dia = bf16[16,2176]{1,0:T(8,128)(2,1)S(1)} collective-permute-done((bf16[16,2176]{1,0:T(8,128)(2,1)S(1)}, bf16[16,2176]{1,0:T(8,128)(2,1)S(1)}, u32[]{:S(2)}, u32[]{:S(2)}) %collective-permute-start.1) | collective-permute-done | bytes 69664 | tf_op jit(solution)/shard_map/ppermute | solution.py:449
  19.3 0.0 collective-permute-done.2.lat
  19.3 0.0 collective-permute-done.lon
  19.3 0.0 copy-done
  19.3 0.0 copy-done.1
  19.3 0.0 copy-done.5
  19.3 0.0 copy-done.7
  19.3 0.0 copy-done.8
  19.4 4.8 %main.1 = (bf16[48,1024]{1,0:T(8,128)(2,1)S(1)}, bf16[48,1024]{1,0:T(8,128)(2,1)S(1)}, bf16[16,1024]{1,0:T(8,128)(2,1)S(1)}, bf16[16,1024]{1,0:T(8,128)(2,1)S(1)}) custom-call(bf16[48,2176]{1,0:T(8,128)(2,1)S(1)} %get-tuple-element.23.own, bf16[48,2176]{1,0:T(8,128)(2,1)S(1)} %collective-permute-done.lon, bf16[16,2176]{1,0:T(8,128)(2,1)S(1)} %collective-permute-done.1.dia, ...), custom_call_target="tpu_custom_call" | custom-call | flops 1500000000 | bytes 6000000 | tf_op jit(solution)/shard_map/main/pallas_call | solution.py:397
  24.1 4.9 %collective-permute-start.3 = (bf16[48,1024]{1,0:T(8,128)(2,1)S(1)}, bf16[48,1024]{1,0:T(8,128)(2,1)S(1)}, u32[]{:S(2)}, u32[]{:S(2)}) collective-permute-start(bf16[48,1024]{1,0:T(8,128)(2,1)S(1)} %get-tuple-element.30), channel_id=1, source_target_pairs={{0,504},{1,505},{2,506},{3,507},{4,508},{5,509},{6,510},{7,511},{8... | collective-permute-start | bytes 294920 | tf_op jit(solution)/shard_map/ppermute | solution.py:449
  29.0 5.5 %collective-permute-start.4 = (bf16[16,1024]{1,0:T(8,128)(2,1)S(1)}, bf16[16,1024]{1,0:T(8,128)(2,1)S(1)}, u32[]{:S(2)}, u32[]{:S(2)}) collective-permute-start(bf16[16,1024]{1,0:T(8,128)(2,1)S(1)} %get-tuple-element.31), channel_id=1, source_target_pairs={{0,505},{1,506},{2,507},{3,508},{4,509},{5,510},{6,511},{7,504},{8... | collective-permute-start | bytes 98312 | tf_op jit(solution)/shard_map/ppermute | solution.py:449
  34.6 2.5 %collective-permute-start.5 = (bf16[16,1024]{1,0:T(8,128)(2,1)S(1)}, bf16[16,1024]{1,0:T(8,128)(2,1)S(1)}, u32[]{:S(2)}, u32[]{:S(2)}) collective-permute-start(bf16[16,1024]{1,0:T(8,128)(2,1)S(1)} %get-tuple-element.32), channel_id=1, source_target_pairs={{0,1},{1,2},{2,3},{3,4},{4,5},{5,6},{6,7},{7,0},{8,9},{9,10},{10,1... | collective-permute-start | bytes 98312 | tf_op jit(solution)/shard_map/ppermute | solution.py:449
  37.1 0.0 collective-permute-done.4.dia
  37.1 4.2 %collective-permute-done.5.lat = bf16[16,1024]{1,0:T(8,128)(2,1)S(1)} collective-permute-done((bf16[16,1024]{1,0:T(8,128)(2,1)S(1)}, bf16[16,1024]{1,0:T(8,128)(2,1)S(1)}, u32[]{:S(2)}, u32[]{:S(2)}) %collective-permute-start.5) | collective-permute-done | bytes 32800 | tf_op jit(solution)/shard_map/ppermute | solution.py:449
  41.3 0.0 collective-permute-done.3.lon
  41.3 0.9 %final.1 = bf16[16,8,1024]{2,1,0:T(8,128)(2,1)} custom-call(bf16[48,1024]{1,0:T(8,128)(2,1)S(1)} %get-tuple-element.29.own, bf16[48,1024]{1,0:T(8,128)(2,1)S(1)} %collective-permute-done.3.lon, bf16[16,1024]{1,0:T(8,128)(2,1)S(1)} %collective-permute-done.4.dia, bf16[16,1024]{1,0:T(8,128)(2,1)S(1)} %collective-permute-done.5.lat), custom_call_target="tpu_custom_call" | custom-call | tf_op jit(solution)/shard_map/final/pallas_call | solution.py:434
Async XLA Ops:
  0.0 0.9 %copy-start.3 = (bf16[8,4,4096]{2,1,0:T(4,128)(2,1)S(1)}, bf16[8,4,4096]{2,1,0:T(4,128)(2,1)}, u32[]{:S(2)}) copy-start(bf16[8,4,4096]{2,1,0:T(4,128)(2,1)} %cot.1) | copy-start | bytes 786436
  0.0 1.0 %copy-start.6 = (s32[16,8]{0,1:T(8,128)S(1)}, s32[16,8]{0,1:T(8,128)}, u32[]{:S(2)}) copy-start(s32[16,8]{0,1:T(8,128)} %param.11) | copy-start | bytes 1540
  0.0 1.0 %copy-start.2 = (bf16[16,8,1024]{2,1,0:T(8,128)(2,1)S(1)}, bf16[16,8,1024]{2,1,0:T(8,128)(2,1)}, u32[]{:S(2)}) copy-start(bf16[16,8,1024]{2,1,0:T(8,128)(2,1)} %tokens.1) | copy-start | bytes 786436
  1.0 10.2 %copy-start.4 = (f32[16,225]{1,0:T(8,128)S(1)}, f32[16,225]{1,0:T(8,128)}, u32[]{:S(2)}) copy-start(f32[16,225]{1,0:T(8,128)} %table.1) | copy-start | bytes 43204
  1.0 10.2 %copy-start.9 = (f32[16]{0:T(128)S(1)}, f32[16]{0:T(128)}, u32[]{:S(2)}) copy-start(f32[16]{0:T(128)} %param.14) | copy-start | bytes 196
  1.1 18.3 %copy-start = (bf16[1024,1536]{1,0:T(8,128)(2,1)S(1)}, bf16[1024,1536]{1,0:T(8,128)(2,1)}, u32[]{:S(2)}) copy-start(bf16[1024,1536]{1,0:T(8,128)(2,1)} %w_qkv.1) | copy-start | bytes 9437188
  1.1 18.3 %copy-start.1 = (bf16[512,1024]{1,0:T(8,128)(2,1)S(1)}, bf16[512,1024]{1,0:T(8,128)(2,1)}, u32[]{:S(2)}) copy-start(bf16[512,1024]{1,0:T(8,128)(2,1)} %w_proj.1) | copy-start | bytes 3145732
  1.1 18.3 %copy-start.5 = (f32[4096]{0:T(1024)S(1)}, f32[4096]{0:T(1024)}, u32[]{:S(2)}) copy-start(f32[4096]{0:T(1024)} %param.18) | copy-start | bytes 49156
  1.1 18.3 %copy-start.7 = (f32[1024]{0:T(1024)S(1)}, f32[1024]{0:T(1024)}, u32[]{:S(2)}) copy-start(f32[1024]{0:T(1024)} %param.16) | copy-start | bytes 12292
  1.1 18.3 %copy-start.8 = (f32[1024]{0:T(1024)S(1)}, f32[1024]{0:T(1024)}, u32[]{:S(2)}) copy-start(f32[1024]{0:T(1024)} %param.17) | copy-start | bytes 12292
  1.4 17.9 %collective-permute-start = (bf16[48,2176]{1,0:T(8,128)(2,1)S(1)}, bf16[48,2176]{1,0:T(8,128)(2,1)S(1)}, u32[]{:S(2)}, u32[]{:S(2)}) collective-permute-start(bf16[48,2176]{1,0:T(8,128)(2,1)S(1)} %get-tuple-element.24), channel_id=1, source_target_pairs={{0,8},{1,9},{2,10},{3,11},{4,12},{5,13},{6,14},{7,15},{8,16},{9,17... | collective-permute-start | bytes 626696 | tf_op jit(solution)/shard_map/ppermute | solution.py:449
  3.6 15.7 %collective-permute-start.1 = (bf16[16,2176]{1,0:T(8,128)(2,1)S(1)}, bf16[16,2176]{1,0:T(8,128)(2,1)S(1)}, u32[]{:S(2)}, u32[]{:S(2)}) collective-permute-start(bf16[16,2176]{1,0:T(8,128)(2,1)S(1)} %get-tuple-element.25), channel_id=1, source_target_pairs={{0,15},{1,8},{2,9},{3,10},{4,11},{5,12},{6,13},{7,14},{8,23},{9,16... | collective-permute-start | bytes 208904 | tf_op jit(solution)/shard_map/ppermute | solution.py:449
  8.8 10.5 %collective-permute-start.2 = (bf16[16,2176]{1,0:T(8,128)(2,1)S(1)}, bf16[16,2176]{1,0:T(8,128)(2,1)S(1)}, u32[]{:S(2)}, u32[]{:S(2)}) collective-permute-start(bf16[16,2176]{1,0:T(8,128)(2,1)S(1)} %get-tuple-element.26), channel_id=1, source_target_pairs={{0,7},{1,0},{2,1},{3,2},{4,3},{5,4},{6,5},{7,6},{8,15},{9,8},{10,9... | collective-permute-start | bytes 208904 | tf_op jit(solution)/shard_map/ppermute | solution.py:449
  24.1 17.1 %collective-permute-start.3 = (bf16[48,1024]{1,0:T(8,128)(2,1)S(1)}, bf16[48,1024]{1,0:T(8,128)(2,1)S(1)}, u32[]{:S(2)}, u32[]{:S(2)}) collective-permute-start(bf16[48,1024]{1,0:T(8,128)(2,1)S(1)} %get-tuple-element.30), channel_id=1, source_target_pairs={{0,504},{1,505},{2,506},{3,507},{4,508},{5,509},{6,510},{7,511},{8... | collective-permute-start | bytes 294920 | tf_op jit(solution)/shard_map/ppermute | solution.py:449
  29.0 8.0 %collective-permute-start.4 = (bf16[16,1024]{1,0:T(8,128)(2,1)S(1)}, bf16[16,1024]{1,0:T(8,128)(2,1)S(1)}, u32[]{:S(2)}, u32[]{:S(2)}) collective-permute-start(bf16[16,1024]{1,0:T(8,128)(2,1)S(1)} %get-tuple-element.31), channel_id=1, source_target_pairs={{0,505},{1,506},{2,507},{3,508},{4,509},{5,510},{6,511},{7,504},{8... | collective-permute-start | bytes 98312 | tf_op jit(solution)/shard_map/ppermute | solution.py:449
  34.6 6.7 %collective-permute-start.5 = (bf16[16,1024]{1,0:T(8,128)(2,1)S(1)}, bf16[16,1024]{1,0:T(8,128)(2,1)S(1)}, u32[]{:S(2)}, u32[]{:S(2)}) collective-permute-start(bf16[16,1024]{1,0:T(8,128)(2,1)S(1)} %get-tuple-element.32), channel_id=1, source_target_pairs={{0,1},{1,2},{2,3},{3,4},{4,5},{5,6},{6,7},{7,0},{8,9},{9,10},{10,1... | collective-permute-start | bytes 98312 | tf_op jit(solution)/shard_map/ppermute | solution.py:449

commit v10 on v4

--- a/solution.py
+++ b/solution.py
@@ -248,15 +248,12 @@
         cols = slice(256 * n, 256 * n + 256)
         qkv_s[:, cols] = mm(x_s[...], w_qkv[:, cols]).astype(bf16)
 
-    line, lane = iota((256, 128), 0), iota((256, 128), 1)
-    seg = onehot((line % 128) // 32 == lane // 32)
+    seg = onehot(iota((128, 128), 0) // 32 == iota((128, 128), 1) // 32)
     head_lane = iota((64, 128), 1) // 32
     head_mask = [onehot(head_lane == h) for h in range(4)]
 
-    def store_halves(n, value):
-        high, low = halves(value)
-        seg_s[128 * n : 128 * n + 128, 0:128] = high
-        seg_s[128 * n : 128 * n + 128, 128:256] = low
+    def store_terms(n, value):
+        seg_s[128 * n : 128 * n + 128, :] = value.astype(bf16)
 
     def block_diagonal(value):
         return jnp.concatenate([value * head_mask[h] for h in range(4)], axis=0)
@@ -269,7 +266,7 @@
 
     for n in range(8):
         raw = qkv_s[:, 128 * n : 128 * n + 128].astype(f32)
-        store_halves(n, raw * raw)
+        store_terms(n, raw * raw)
     squares = mm(seg_s[...], seg)
     for n in range(8):
         cols = slice(128 * n, 128 * n + 128)
@@ -308,9 +305,15 @@
         att = diagonal(mm_tn(prob16_s[rows, 256 * b : 256 * b + 256], vals))
         att_s[rows, 128 * b : 128 * b + 128] = att.astype(bf16)
 
+    total = jnp.zeros((128, 128), f32)
+    square = jnp.zeros((128, 128), f32)
     for n in range(4):
         cols = slice(256 * n, 256 * n + 256)
-        proj_s[:, cols] = mm(att_s[...], w_proj[:, cols])
+        part = mm(att_s[...], w_proj[:, cols])
+        proj_s[:, cols] = part
+        left, right = part[:, 0:128], part[:, 128:256]
+        total = total + left + right
+        square = square + left * left + right * right
 
     spans = [slice(16 * n, 16 * n + 16) for n in range(8)]
 
@@ -320,26 +323,27 @@
 
     for s in range(4):
         mgain[4 * s : 4 * s + 4, :] = jnp.broadcast_to(merge[:, s * D : (s + 1) * D], (4, D))
-    mean = [row_total(proj_s[rows, :]) * (1.0 / D) for rows in spans]
-    inv_std = []
-    for n, rows in enumerate(spans):
-        centered = proj_s[rows, :] - mean[n]
-        inv_std.append(lax.rsqrt(row_total(centered * centered) * (1.0 / D) + norm_eps))
-    mean_m, mean_g = [], []
+    mean_p = row_total(total) * (1.0 / D)
+    var_p = row_total(square) * (1.0 / D) - mean_p * mean_p
+    inv_p = lax.rsqrt(jnp.maximum(var_p, 0.0) + norm_eps)
+    mean = [mean_p[rows] for rows in spans]
+    inv_std = [inv_p[rows] for rows in spans]
+    mean_m, mean_g, merge_inv, slope = [], [], [], []
     for n, rows in enumerate(spans):
         normed = (proj_s[rows, :] - mean[n]) * inv_std[n]
         proj_s[rows, :] = normed
         mixed = x_s[rows, :].astype(f32) + normed * gain[...] + shift[...]
         mixed_s[rows, :] = mixed
-        mean_m.append(group_total(row_total(mixed)) * (0.25 / D))
-        mean_g.append(group_total(row_total(ghat_of(n))) * (0.25 / D))
-    merge_inv, slope = [], []
-    for n, rows in enumerate(spans):
-        cent = mixed_s[rows, :] - mean_m[n]
         ghat = ghat_of(n)
-        inv = lax.rsqrt(group_total(row_total(cent * cent)) * (0.25 / D) + norm_eps)
+        mu = group_total(row_total(mixed)) * (0.25 / D)
+        mg = group_total(row_total(ghat)) * (0.25 / D)
+        mm2 = group_total(row_total(mixed * mixed)) * (0.25 / D)
+        mgm = group_total(row_total(ghat * mixed)) * (0.25 / D)
+        inv = lax.rsqrt(jnp.maximum(mm2 - mu * mu, 0.0) + norm_eps)
+        mean_m.append(mu)
+        mean_g.append(mg)
         merge_inv.append(inv)
-        slope.append(group_total(row_total(ghat * cent)) * (0.25 / D) * inv * inv)
+        slope.append((mgm - mg * mu) * inv * inv)
     mean_e, mean_en = [], []
     for n, rows in enumerate(spans):
         cent = mixed_s[rows, :] - mean_m[n]
@@ -379,7 +383,7 @@
         proj_s[rows, kcols] = gk
     for n in range(8):
         cols = slice(128 * n, 128 * n + 128)
-        store_halves(n, unit_s[:, cols] * proj_s[:, cols])
+        store_terms(n, unit_s[:, cols] * proj_s[:, cols])
     along = mm(seg_s[...], seg)
     for n in range(8):
         cols = slice(128 * n, 128 * n + 128)
@@ -403,7 +407,7 @@
             pltpu.VMEM((128, 2 * ATT), f32),
             pltpu.VMEM((128, 2 * ATT), f32),
             pltpu.VMEM((128, 2 * ATT), bf16),
-            pltpu.VMEM((1024, 256), bf16),
+            pltpu.VMEM((1024, 128), bf16),
             pltpu.VMEM((2048, 128), bf16),
             pltpu.VMEM((128, HEADS * CELLS), f32),
             pltpu.VMEM((128, HEADS * CELLS), bf16),

time: 40.9 us -> 40.5 us (level)
  no operation moved by 1% of the time
where the time goes in v10:
time: 40.5 us; the launch traced here: 40.3 us
  starting transfers between devices  23.1 us (57%)
  waiting for transfers between devices  9.53 us (24%)
  Pallas kernels  6.66 us (16%)
  local copies, waits for them, and re-layouts  0.87 us (2%)
    ppermute x6, starting transfers between devices, shift_by(): return lax.ppermute(block, ('lon', 'lat'), route)  23.1 us
    ppermute x6, waiting for transfers between devices, shift_by(): return lax.ppermute(block, ('lon', 'lat'), route)  9.53 us
    pallas_call x1, Pallas kernels, main(): pl.pallas_call(main_kernel, out_shape=[jax.ShapeDtypeStruct((n, D), bf16)...  4.39 us
    pallas_call x1, Pallas kernels, final(): pl.pallas_call(final_kernel, out_shape=jax.ShapeDtypeStruct((16, 8, D), b...  0.93 us
    unnamed x20, local copies, waits for them, and re-layouts  0.87 us
    pallas_call x1, Pallas kernels, prep(): pl.pallas_call(prep_kernel, out_shape=[jax.ShapeDtypeStruct((CELLS, HEADS...  0.82 us
  transfers between devices with their start and end apart: 6, of which 2 were waited for; matrix products, arithmetic and copies ran while one was open for 0% of the time, Pallas kernels for 2%

profile of v10, /device:TPU:24, one launch (start us, length us, event | category | flops | bytes accessed | tf_op | source)
XLA Modules:
  0.0 40.3 jit_solution(18204728961927266020)
XLA Ops:
  0.0 0.0 copy-start.3
  0.0 0.0 copy-start.6
  0.0 0.0 copy-start.2
  0.0 0.2 places.1
  0.2 0.7 %copy-done.3 = bf16[8,4,4096]{2,1,0:T(4,128)(2,1)S(1)} copy-done((bf16[8,4,4096]{2,1,0:T(4,128)(2,1)S(1)}, bf16[8,4,4096]{2,1,0:T(4,128)(2,1)}, u32[]{:S(2)}) %copy-start.3) | copy-done | bytes 262168
  1.0 0.0 copy-done.6
  1.0 0.1 copy-done.2
  1.0 0.0 copy-start.4
  1.0 0.0 copy-start.9
  1.1 0.0 copy-start
  1.1 0.0 copy-start.1
  1.1 0.0 copy-start.5
  1.1 0.0 copy-start.7
  1.1 0.0 copy-start.8
  1.1 0.3 pack.1
  1.4 2.2 %collective-permute-start = (bf16[48,2176]{1,0:T(8,128)(2,1)S(1)}, bf16[48,2176]{1,0:T(8,128)(2,1)S(1)}, u32[]{:S(2)}, u32[]{:S(2)}) collective-permute-start(bf16[48,2176]{1,0:T(8,128)(2,1)S(1)} %get-tuple-element.24), channel_id=1, source_target_pairs={{0,8},{1,9},{2,10},{3,11},{4,12},{5,13},{6,14},{7,15},{8,16},{9,17... | collective-permute-start | bytes 626696 | tf_op jit(solution)/shard_map/ppermute | solution.py:453
  3.6 5.2 %collective-permute-start.1 = (bf16[16,2176]{1,0:T(8,128)(2,1)S(1)}, bf16[16,2176]{1,0:T(8,128)(2,1)S(1)}, u32[]{:S(2)}, u32[]{:S(2)}) collective-permute-start(bf16[16,2176]{1,0:T(8,128)(2,1)S(1)} %get-tuple-element.25), channel_id=1, source_target_pairs={{0,15},{1,8},{2,9},{3,10},{4,11},{5,12},{6,13},{7,14},{8,23},{9,16... | collective-permute-start | bytes 208904 | tf_op jit(solution)/shard_map/ppermute | solution.py:453
  8.8 2.4 %collective-permute-start.2 = (bf16[16,2176]{1,0:T(8,128)(2,1)S(1)}, bf16[16,2176]{1,0:T(8,128)(2,1)S(1)}, u32[]{:S(2)}, u32[]{:S(2)}) collective-permute-start(bf16[16,2176]{1,0:T(8,128)(2,1)S(1)} %get-tuple-element.26), channel_id=1, source_target_pairs={{0,7},{1,0},{2,1},{3,2},{4,3},{5,4},{6,5},{7,6},{8,15},{9,8},{10,9... | collective-permute-start | bytes 208904 | tf_op jit(solution)/shard_map/ppermute | solution.py:453
  11.3 0.0 copy-done.4
  11.3 0.0 copy-done.9
  11.3 0.8 %prep.1 = (f32[64,1024]{1,0:T(8,128)S(1)}, f32[1,512]{1,0:T(1,128)S(1)}) custom-call(f32[16,225]{1,0:T(8,128)S(1)} %copy-done.4, f32[1,16]{1,0:T(1,128)S(1)} %bitcast.9), custom_call_target="tpu_custom_call" | custom-call | flops 100000000 | bytes 400000 | tf_op jit(solution)/shard_map/prep/pallas_call | solution.py:172
  12.1 7.2 %collective-permute-done.1.dia = bf16[16,2176]{1,0:T(8,128)(2,1)S(1)} collective-permute-done((bf16[16,2176]{1,0:T(8,128)(2,1)S(1)}, bf16[16,2176]{1,0:T(8,128)(2,1)S(1)}, u32[]{:S(2)}, u32[]{:S(2)}) %collective-permute-start.1) | collective-permute-done | bytes 69664 | tf_op jit(solution)/shard_map/ppermute | solution.py:453
  19.3 0.0 collective-permute-done.2.lat
  19.3 0.0 collective-permute-done.lon
  19.3 0.0 copy-done
  19.3 0.0 copy-done.1
  19.3 0.0 copy-done.5
  19.3 0.0 copy-done.7
  19.3 0.0 copy-done.8
  19.4 4.4 %main.1 = (bf16[48,1024]{1,0:T(8,128)(2,1)S(1)}, bf16[48,1024]{1,0:T(8,128)(2,1)S(1)}, bf16[16,1024]{1,0:T(8,128)(2,1)S(1)}, bf16[16,1024]{1,0:T(8,128)(2,1)S(1)}) custom-call(bf16[48,2176]{1,0:T(8,128)(2,1)S(1)} %get-tuple-element.23.own, bf16[48,2176]{1,0:T(8,128)(2,1)S(1)} %collective-permute-done.lon, bf16[16,2176]{1,0:T(8,128)(2,1)S(1)} %collective-permute-done.1.dia, ...), custom_call_target="tpu_custom_call" | custom-call | flops 1500000000 | bytes 6000000 | tf_op jit(solution)/shard_map/main/pallas_call | solution.py:401
  23.8 4.9 %collective-permute-start.4 = (bf16[48,1024]{1,0:T(8,128)(2,1)S(1)}, bf16[48,1024]{1,0:T(8,128)(2,1)S(1)}, u32[]{:S(2)}, u32[]{:S(2)}) collective-permute-start(bf16[48,1024]{1,0:T(8,128)(2,1)S(1)} %get-tuple-element.31), channel_id=1, source_target_pairs={{0,504},{1,505},{2,506},{3,507},{4,508},{5,509},{6,510},{7,511},{8... | collective-permute-start | bytes 294920 | tf_op jit(solution)/shard_map/ppermute | solution.py:453
  28.7 4.6 %collective-permute-start.3 = (bf16[16,1024]{1,0:T(8,128)(2,1)S(1)}, bf16[16,1024]{1,0:T(8,128)(2,1)S(1)}, u32[]{:S(2)}, u32[]{:S(2)}) collective-permute-start(bf16[16,1024]{1,0:T(8,128)(2,1)S(1)} %get-tuple-element.30), channel_id=1, source_target_pairs={{0,1},{1,2},{2,3},{3,4},{4,5},{5,6},{6,7},{7,0},{8,9},{9,10},{10,1... | collective-permute-start | bytes 98312 | tf_op jit(solution)/shard_map/ppermute | solution.py:453
  33.2 3.8 %collective-permute-start.5 = (bf16[16,1024]{1,0:T(8,128)(2,1)S(1)}, bf16[16,1024]{1,0:T(8,128)(2,1)S(1)}, u32[]{:S(2)}, u32[]{:S(2)}) collective-permute-start(bf16[16,1024]{1,0:T(8,128)(2,1)S(1)} %get-tuple-element.32), channel_id=1, source_target_pairs={{0,505},{1,506},{2,507},{3,508},{4,509},{5,510},{6,511},{7,504},{8... | collective-permute-start | bytes 98312 | tf_op jit(solution)/shard_map/ppermute | solution.py:453
  37.0 0.0 collective-permute-done.3.lat
  37.0 2.3 %collective-permute-done.5.dia = bf16[16,1024]{1,0:T(8,128)(2,1)S(1)} collective-permute-done((bf16[16,1024]{1,0:T(8,128)(2,1)S(1)}, bf16[16,1024]{1,0:T(8,128)(2,1)S(1)}, u32[]{:S(2)}, u32[]{:S(2)}) %collective-permute-start.5) | collective-permute-done | bytes 32800 | tf_op jit(solution)/shard_map/ppermute | solution.py:453
  39.4 0.0 collective-permute-done.4.lon
  39.4 0.9 %final.1 = bf16[16,8,1024]{2,1,0:T(8,128)(2,1)} custom-call(bf16[48,1024]{1,0:T(8,128)(2,1)S(1)} %get-tuple-element.29.own, bf16[16,1024]{1,0:T(8,128)(2,1)S(1)} %collective-permute-done.3.lat, bf16[48,1024]{1,0:T(8,128)(2,1)S(1)} %collective-permute-done.4.lon, bf16[16,1024]{1,0:T(8,128)(2,1)S(1)} %collective-permute-done.5.dia), custom_call_target="tpu_custom_call" | custom-call | tf_op jit(solution)/shard_map/final/pallas_call | solution.py:438
Async XLA Ops:
  0.0 0.9 %copy-start.3 = (bf16[8,4,4096]{2,1,0:T(4,128)(2,1)S(1)}, bf16[8,4,4096]{2,1,0:T(4,128)(2,1)}, u32[]{:S(2)}) copy-start(bf16[8,4,4096]{2,1,0:T(4,128)(2,1)} %cot.1) | copy-start | bytes 786436
  0.0 1.0 %copy-start.6 = (s32[16,8]{0,1:T(8,128)S(1)}, s32[16,8]{0,1:T(8,128)}, u32[]{:S(2)}) copy-start(s32[16,8]{0,1:T(8,128)} %param.11) | copy-start | bytes 1540
  0.0 1.0 %copy-start.2 = (bf16[16,8,1024]{2,1,0:T(8,128)(2,1)S(1)}, bf16[16,8,1024]{2,1,0:T(8,128)(2,1)}, u32[]{:S(2)}) copy-start(bf16[16,8,1024]{2,1,0:T(8,128)(2,1)} %tokens.1) | copy-start | bytes 786436
  1.0 10.2 %copy-start.4 = (f32[16,225]{1,0:T(8,128)S(1)}, f32[16,225]{1,0:T(8,128)}, u32[]{:S(2)}) copy-start(f32[16,225]{1,0:T(8,128)} %table.1) | copy-start | bytes 43204
  1.0 10.2 %copy-start.9 = (f32[16]{0:T(128)S(1)}, f32[16]{0:T(128)}, u32[]{:S(2)}) copy-start(f32[16]{0:T(128)} %param.14) | copy-start | bytes 196
  1.1 18.3 %copy-start = (bf16[1024,1536]{1,0:T(8,128)(2,1)S(1)}, bf16[1024,1536]{1,0:T(8,128)(2,1)}, u32[]{:S(2)}) copy-start(bf16[1024,1536]{1,0:T(8,128)(2,1)} %w_qkv.1) | copy-start | bytes 9437188
  1.1 18.3 %copy-start.1 = (bf16[512,1024]{1,0:T(8,128)(2,1)S(1)}, bf16[512,1024]{1,0:T(8,128)(2,1)}, u32[]{:S(2)}) copy-start(bf16[512,1024]{1,0:T(8,128)(2,1)} %w_proj.1) | copy-start | bytes 3145732
  1.1 18.3 %copy-start.5 = (f32[4096]{0:T(1024)S(1)}, f32[4096]{0:T(1024)}, u32[]{:S(2)}) copy-start(f32[4096]{0:T(1024)} %param.18) | copy-start | bytes 49156
  1.1 18.3 %copy-start.7 = (f32[1024]{0:T(1024)S(1)}, f32[1024]{0:T(1024)}, u32[]{:S(2)}) copy-start(f32[1024]{0:T(1024)} %param.16) | copy-start | bytes 12292
  1.1 18.3 %copy-start.8 = (f32[1024]{0:T(1024)S(1)}, f32[1024]{0:T(1024)}, u32[]{:S(2)}) copy-start(f32[1024]{0:T(1024)} %param.17) | copy-start | bytes 12292
  1.4 17.9 %collective-permute-start = (bf16[48,2176]{1,0:T(8,128)(2,1)S(1)}, bf16[48,2176]{1,0:T(8,128)(2,1)S(1)}, u32[]{:S(2)}, u32[]{:S(2)}) collective-permute-start(bf16[48,2176]{1,0:T(8,128)(2,1)S(1)} %get-tuple-element.24), channel_id=1, source_target_pairs={{0,8},{1,9},{2,10},{3,11},{4,12},{5,13},{6,14},{7,15},{8,16},{9,17... | collective-permute-start | bytes 626696 | tf_op jit(solution)/shard_map/ppermute | solution.py:453
  3.6 15.7 %collective-permute-start.1 = (bf16[16,2176]{1,0:T(8,128)(2,1)S(1)}, bf16[16,2176]{1,0:T(8,128)(2,1)S(1)}, u32[]{:S(2)}, u32[]{:S(2)}) collective-permute-start(bf16[16,2176]{1,0:T(8,128)(2,1)S(1)} %get-tuple-element.25), channel_id=1, source_target_pairs={{0,15},{1,8},{2,9},{3,10},{4,11},{5,12},{6,13},{7,14},{8,23},{9,16... | collective-permute-start | bytes 208904 | tf_op jit(solution)/shard_map/ppermute | solution.py:453
  8.8 10.5 %collective-permute-start.2 = (bf16[16,2176]{1,0:T(8,128)(2,1)S(1)}, bf16[16,2176]{1,0:T(8,128)(2,1)S(1)}, u32[]{:S(2)}, u32[]{:S(2)}) collective-permute-start(bf16[16,2176]{1,0:T(8,128)(2,1)S(1)} %get-tuple-element.26), channel_id=1, source_target_pairs={{0,7},{1,0},{2,1},{3,2},{4,3},{5,4},{6,5},{7,6},{8,15},{9,8},{10,9... | collective-permute-start | bytes 208904 | tf_op jit(solution)/shard_map/ppermute | solution.py:453
  23.8 15.6 %collective-permute-start.4 = (bf16[48,1024]{1,0:T(8,128)(2,1)S(1)}, bf16[48,1024]{1,0:T(8,128)(2,1)S(1)}, u32[]{:S(2)}, u32[]{:S(2)}) collective-permute-start(bf16[48,1024]{1,0:T(8,128)(2,1)S(1)} %get-tuple-element.31), channel_id=1, source_target_pairs={{0,504},{1,505},{2,506},{3,507},{4,508},{5,509},{6,510},{7,511},{8... | collective-permute-start | bytes 294920 | tf_op jit(solution)/shard_map/ppermute | solution.py:453
  28.7 8.4 %collective-permute-start.3 = (bf16[16,1024]{1,0:T(8,128)(2,1)S(1)}, bf16[16,1024]{1,0:T(8,128)(2,1)S(1)}, u32[]{:S(2)}, u32[]{:S(2)}) collective-permute-start(bf16[16,1024]{1,0:T(8,128)(2,1)S(1)} %get-tuple-element.30), channel_id=1, source_target_pairs={{0,1},{1,2},{2,3},{3,4},{4,5},{5,6},{6,7},{7,0},{8,9},{9,10},{10,1... | collective-permute-start | bytes 98312 | tf_op jit(solution)/shard_map/ppermute | solution.py:453
  33.2 6.1 %collective-permute-start.5 = (bf16[16,1024]{1,0:T(8,128)(2,1)S(1)}, bf16[16,1024]{1,0:T(8,128)(2,1)S(1)}, u32[]{:S(2)}, u32[]{:S(2)}) collective-permute-start(bf16[16,1024]{1,0:T(8,128)(2,1)S(1)} %get-tuple-element.32), channel_id=1, source_target_pairs={{0,505},{1,506},{2,507},{3,508},{4,509},{5,510},{6,511},{7,504},{8... | collective-permute-start | bytes 98312 | tf_op jit(solution)/shard_map/ppermute | solution.py:453

commit v11 on v10

--- a/solution.py
+++ b/solution.py
@@ -28,7 +28,7 @@
     quad = n // 16
     s = (n // 4) % 4
     g = n % 4
-    row = jnp.where(quad < 6, 4 + 4 * (quad % 3), 0) + 2 * (g // 2) + s % 2
+    row = jnp.where(quad < 6, 4 * (quad % 3), 12) + 2 * (g // 2) + s % 2
     col = jnp.where((quad // 3 == 1) | (quad == 7), 4, 0) + 2 * (g % 2) + s // 2
     return row, col, s
 
@@ -232,14 +232,14 @@
     mgain,
 ):
     quads = (
+        (dia, out_dia, 0),
+        (lat, out_lat, 0),
         (lon, out_lon, 0),
         (own, out_own, 0),
         (lon, out_lon, 16),
         (own, out_own, 16),
         (lon, out_lon, 32),
         (own, out_own, 32),
-        (dia, out_dia, 0),
-        (lat, out_lat, 0),
     )
     pairs = [(w, b) for w in range(2) for b in range(BLOCKS)]
     for n, (ref, _, lo) in enumerate(quads):
@@ -467,8 +467,8 @@
 ):
     own, lon, lat, dia = pack(tokens, labels.T, cotangent, places())
     lon = shift_by(lon, 0, 1)
-    dia = shift_by(dia, -1, 1)
-    lat = shift_by(lat, -1, 0)
+    dia = shift_by(dia, 1, 1)
+    lat = shift_by(lat, 1, 0)
     ebias, temper = prep(bias_table, logit_scale.reshape(1, HEADS))
     own, lon, lat, dia = main(
         own,
@@ -484,8 +484,8 @@
         merge_gain.reshape(1, 4 * D),
     )
     lon = shift_by(lon, 0, -1)
-    dia = shift_by(dia, 1, -1)
-    lat = shift_by(lat, 1, 0)
+    dia = shift_by(dia, -1, -1)
+    lat = shift_by(lat, -1, 0)
     return final(own, lon, lat, dia)
 
 

time: 40.5 us -> 41.1 us (1.015)
  the two profiles are of different devices: /device:TPU:24 before, /device:TPU:1 now
where the time goes in v11:
time: 41.1 us; the launch traced here: 40.9 us
  starting transfers between devices  28.9 us (70%)
  Pallas kernels  6.64 us (16%)
  waiting for transfers between devices  4.33 us (11%)
  local copies, waits for them, and re-layouts  0.87 us (2%)
    ppermute x6, starting transfers between devices, shift_by(): return lax.ppermute(block, ('lon', 'lat'), route)  28.9 us
    pallas_call x1, Pallas kernels, main(): pl.pallas_call(main_kernel, out_shape=[jax.ShapeDtypeStruct((n, D), bf16)...  4.38 us
    ppermute x6, waiting for transfers between devices, shift_by(): return lax.ppermute(block, ('lon', 'lat'), route)  4.33 us
    pallas_call x1, Pallas kernels, final(): pl.pallas_call(final_kernel, out_shape=jax.ShapeDtypeStruct((16, 8, D), b...  0.93 us
    unnamed x20, local copies, waits for them, and re-layouts  0.87 us
  transfers between devices with their start and end apart: 6, of which 3 were waited for; matrix products, arithmetic and copies ran while one was open for 0% of the time, Pallas kernels for 2%

profile of v11, /device:TPU:1, one launch (start us, length us, event | category | flops | bytes accessed | tf_op | source)
XLA Modules:
  0.0 40.9 jit_solution(16793593286681126872)
XLA Ops:
  0.0 0.0 copy-start.3
  0.0 0.0 copy-start.6
  0.0 0.0 copy-start.2
  0.0 0.2 places.1
  0.2 0.7 %copy-done.3 = bf16[8,4,4096]{2,1,0:T(4,128)(2,1)S(1)} copy-done((bf16[8,4,4096]{2,1,0:T(4,128)(2,1)S(1)}, bf16[8,4,4096]{2,1,0:T(4,128)(2,1)}, u32[]{:S(2)}) %copy-start.3) | copy-done | bytes 262168
  1.0 0.0 copy-done.6
  1.0 0.1 copy-done.2
  1.0 0.0 copy-start.4
  1.0 0.0 copy-start.9
  1.1 0.0 copy-start
  1.1 0.0 copy-start.1
  1.1 0.0 copy-start.5
  1.1 0.0 copy-start.7
  1.1 0.0 copy-start.8
  1.1 0.3 pack.1
  1.4 5.2 %collective-permute-start = (bf16[48,2176]{1,0:T(8,128)(2,1)S(1)}, bf16[48,2176]{1,0:T(8,128)(2,1)S(1)}, u32[]{:S(2)}, u32[]{:S(2)}) collective-permute-start(bf16[48,2176]{1,0:T(8,128)(2,1)S(1)} %get-tuple-element.24), channel_id=1, source_target_pairs={{0,8},{1,9},{2,10},{3,11},{4,12},{5,13},{6,14},{7,15},{8,16},{9,17... | collective-permute-start | bytes 626696 | tf_op jit(solution)/shard_map/ppermute | solution.py:453
  6.6 2.9 %collective-permute-start.1 = (bf16[16,2176]{1,0:T(8,128)(2,1)S(1)}, bf16[16,2176]{1,0:T(8,128)(2,1)S(1)}, u32[]{:S(2)}, u32[]{:S(2)}) collective-permute-start(bf16[16,2176]{1,0:T(8,128)(2,1)S(1)} %get-tuple-element.25), channel_id=1, source_target_pairs={{0,9},{1,10},{2,11},{3,12},{4,13},{5,14},{6,15},{7,8},{8,17},{9,18... | collective-permute-start | bytes 208904 | tf_op jit(solution)/shard_map/ppermute | solution.py:453
  9.5 3.2 %collective-permute-start.2 = (bf16[16,2176]{1,0:T(8,128)(2,1)S(1)}, bf16[16,2176]{1,0:T(8,128)(2,1)S(1)}, u32[]{:S(2)}, u32[]{:S(2)}) collective-permute-start(bf16[16,2176]{1,0:T(8,128)(2,1)S(1)} %get-tuple-element.26), channel_id=1, source_target_pairs={{0,1},{1,2},{2,3},{3,4},{4,5},{5,6},{6,7},{7,0},{8,9},{9,10},{10,1... | collective-permute-start | bytes 208904 | tf_op jit(solution)/shard_map/ppermute | solution.py:453
  12.7 0.0 copy-done.4
  12.7 0.0 copy-done.9
  12.7 0.8 %prep.1 = (f32[64,1024]{1,0:T(8,128)S(1)}, f32[1,512]{1,0:T(1,128)S(1)}) custom-call(f32[16,225]{1,0:T(8,128)S(1)} %copy-done.4, f32[1,16]{1,0:T(1,128)S(1)} %bitcast.9), custom_call_target="tpu_custom_call" | custom-call | flops 100000000 | bytes 400000 | tf_op jit(solution)/shard_map/prep/pallas_call | solution.py:172
  13.5 0.8 %collective-permute-done.1.dia = bf16[16,2176]{1,0:T(8,128)(2,1)S(1)} collective-permute-done((bf16[16,2176]{1,0:T(8,128)(2,1)S(1)}, bf16[16,2176]{1,0:T(8,128)(2,1)S(1)}, u32[]{:S(2)}, u32[]{:S(2)}) %collective-permute-start.1) | collective-permute-done | bytes 69664 | tf_op jit(solution)/shard_map/ppermute | solution.py:453
  14.4 2.5 %collective-permute-done.2.lat = bf16[16,2176]{1,0:T(8,128)(2,1)S(1)} collective-permute-done((bf16[16,2176]{1,0:T(8,128)(2,1)S(1)}, bf16[16,2176]{1,0:T(8,128)(2,1)S(1)}, u32[]{:S(2)}, u32[]{:S(2)}) %collective-permute-start.2) | collective-permute-done | bytes 69664 | tf_op jit(solution)/shard_map/ppermute | solution.py:453
  16.8 0.0 collective-permute-done.lon
  16.8 0.0 copy-done
  16.8 0.0 copy-done.1
  16.9 0.0 copy-done.5
  16.9 0.0 copy-done.7
  16.9 0.0 copy-done.8
  16.9 4.4 %main.1 = (bf16[48,1024]{1,0:T(8,128)(2,1)S(1)}, bf16[48,1024]{1,0:T(8,128)(2,1)S(1)}, bf16[16,1024]{1,0:T(8,128)(2,1)S(1)}, bf16[16,1024]{1,0:T(8,128)(2,1)S(1)}) custom-call(bf16[48,2176]{1,0:T(8,128)(2,1)S(1)} %get-tuple-element.23.own, bf16[48,2176]{1,0:T(8,128)(2,1)S(1)} %collective-permute-done.lon, bf16[16,2176]{1,0:T(8,128)(2,1)S(1)} %collective-permute-done.1.dia, ...), custom_call_target="tpu_custom_call" | custom-call | flops 1500000000 | bytes 6000000 | tf_op jit(solution)/shard_map/main/pallas_call | solution.py:401
  21.3 8.2 %collective-permute-start.4 = (bf16[48,1024]{1,0:T(8,128)(2,1)S(1)}, bf16[48,1024]{1,0:T(8,128)(2,1)S(1)}, u32[]{:S(2)}, u32[]{:S(2)}) collective-permute-start(bf16[48,1024]{1,0:T(8,128)(2,1)S(1)} %get-tuple-element.31), channel_id=1, source_target_pairs={{0,504},{1,505},{2,506},{3,507},{4,508},{5,509},{6,510},{7,511},{8... | collective-permute-start | bytes 294920 | tf_op jit(solution)/shard_map/ppermute | solution.py:453
  29.5 2.2 %collective-permute-start.3 = (bf16[16,1024]{1,0:T(8,128)(2,1)S(1)}, bf16[16,1024]{1,0:T(8,128)(2,1)S(1)}, u32[]{:S(2)}, u32[]{:S(2)}) collective-permute-start(bf16[16,1024]{1,0:T(8,128)(2,1)S(1)} %get-tuple-element.30), channel_id=1, source_target_pairs={{0,7},{1,0},{2,1},{3,2},{4,3},{5,4},{6,5},{7,6},{8,15},{9,8},{10,9... | collective-permute-start | bytes 98312 | tf_op jit(solution)/shard_map/ppermute | solution.py:453
  31.8 7.2 %collective-permute-start.5 = (bf16[16,1024]{1,0:T(8,128)(2,1)S(1)}, bf16[16,1024]{1,0:T(8,128)(2,1)S(1)}, u32[]{:S(2)}, u32[]{:S(2)}) collective-permute-start(bf16[16,1024]{1,0:T(8,128)(2,1)S(1)} %get-tuple-element.32), channel_id=1, source_target_pairs={{0,511},{1,504},{2,505},{3,506},{4,507},{5,508},{6,509},{7,510},{8... | collective-permute-start | bytes 98312 | tf_op jit(solution)/shard_map/ppermute | solution.py:453
  38.9 0.0 collective-permute-done.3.lat
  38.9 1.0 %collective-permute-done.5.dia = bf16[16,1024]{1,0:T(8,128)(2,1)S(1)} collective-permute-done((bf16[16,1024]{1,0:T(8,128)(2,1)S(1)}, bf16[16,1024]{1,0:T(8,128)(2,1)S(1)}, u32[]{:S(2)}, u32[]{:S(2)}) %collective-permute-start.5) | collective-permute-done | bytes 32800 | tf_op jit(solution)/shard_map/ppermute | solution.py:453
  39.9 0.0 collective-permute-done.4.lon
  39.9 0.9 %final.1 = bf16[16,8,1024]{2,1,0:T(8,128)(2,1)} custom-call(bf16[48,1024]{1,0:T(8,128)(2,1)S(1)} %get-tuple-element.29.own, bf16[16,1024]{1,0:T(8,128)(2,1)S(1)} %collective-permute-done.3.lat, bf16[48,1024]{1,0:T(8,128)(2,1)S(1)} %collective-permute-done.4.lon, bf16[16,1024]{1,0:T(8,128)(2,1)S(1)} %collective-permute-done.5.dia), custom_call_target="tpu_custom_call" | custom-call | tf_op jit(solution)/shard_map/final/pallas_call | solution.py:438
Async XLA Ops:
  0.0 0.9 %copy-start.3 = (bf16[8,4,4096]{2,1,0:T(4,128)(2,1)S(1)}, bf16[8,4,4096]{2,1,0:T(4,128)(2,1)}, u32[]{:S(2)}) copy-start(bf16[8,4,4096]{2,1,0:T(4,128)(2,1)} %cot.1) | copy-start | bytes 786436
  0.0 1.0 %copy-start.6 = (s32[16,8]{0,1:T(8,128)S(1)}, s32[16,8]{0,1:T(8,128)}, u32[]{:S(2)}) copy-start(s32[16,8]{0,1:T(8,128)} %param.11) | copy-start | bytes 1540
  0.0 1.0 %copy-start.2 = (bf16[16,8,1024]{2,1,0:T(8,128)(2,1)S(1)}, bf16[16,8,1024]{2,1,0:T(8,128)(2,1)}, u32[]{:S(2)}) copy-start(bf16[16,8,1024]{2,1,0:T(8,128)(2,1)} %tokens.1) | copy-start | bytes 786436
  1.0 11.6 %copy-start.4 = (f32[16,225]{1,0:T(8,128)S(1)}, f32[16,225]{1,0:T(8,128)}, u32[]{:S(2)}) copy-start(f32[16,225]{1,0:T(8,128)} %table.1) | copy-start | bytes 43204
  1.0 11.6 %copy-start.9 = (f32[16]{0:T(128)S(1)}, f32[16]{0:T(128)}, u32[]{:S(2)}) copy-start(f32[16]{0:T(128)} %param.14) | copy-start | bytes 196
  1.1 15.8 %copy-start = (bf16[1024,1536]{1,0:T(8,128)(2,1)S(1)}, bf16[1024,1536]{1,0:T(8,128)(2,1)}, u32[]{:S(2)}) copy-start(bf16[1024,1536]{1,0:T(8,128)(2,1)} %w_qkv.1) | copy-start | bytes 9437188
  1.1 15.8 %copy-start.1 = (bf16[512,1024]{1,0:T(8,128)(2,1)S(1)}, bf16[512,1024]{1,0:T(8,128)(2,1)}, u32[]{:S(2)}) copy-start(bf16[512,1024]{1,0:T(8,128)(2,1)} %w_proj.1) | copy-start | bytes 3145732
  1.1 15.8 %copy-start.5 = (f32[4096]{0:T(1024)S(1)}, f32[4096]{0:T(1024)}, u32[]{:S(2)}) copy-start(f32[4096]{0:T(1024)} %param.18) | copy-start | bytes 49156
  1.1 15.8 %copy-start.7 = (f32[1024]{0:T(1024)S(1)}, f32[1024]{0:T(1024)}, u32[]{:S(2)}) copy-start(f32[1024]{0:T(1024)} %param.16) | copy-start | bytes 12292
  1.1 15.8 %copy-start.8 = (f32[1024]{0:T(1024)S(1)}, f32[1024]{0:T(1024)}, u32[]{:S(2)}) copy-start(f32[1024]{0:T(1024)} %param.17) | copy-start | bytes 12292
  1.4 15.4 %collective-permute-start = (bf16[48,2176]{1,0:T(8,128)(2,1)S(1)}, bf16[48,2176]{1,0:T(8,128)(2,1)S(1)}, u32[]{:S(2)}, u32[]{:S(2)}) collective-permute-start(bf16[48,2176]{1,0:T(8,128)(2,1)S(1)} %get-tuple-element.24), channel_id=1, source_target_pairs={{0,8},{1,9},{2,10},{3,11},{4,12},{5,13},{6,14},{7,15},{8,16},{9,17... | collective-permute-start | bytes 626696 | tf_op jit(solution)/shard_map/ppermute | solution.py:453
  6.6 7.7 %collective-permute-start.1 = (bf16[16,2176]{1,0:T(8,128)(2,1)S(1)}, bf16[16,2176]{1,0:T(8,128)(2,1)S(1)}, u32[]{:S(2)}, u32[]{:S(2)}) collective-permute-start(bf16[16,2176]{1,0:T(8,128)(2,1)S(1)} %get-tuple-element.25), channel_id=1, source_target_pairs={{0,9},{1,10},{2,11},{3,12},{4,13},{5,14},{6,15},{7,8},{8,17},{9,18... | collective-permute-start | bytes 208904 | tf_op jit(solution)/shard_map/ppermute | solution.py:453
  9.5 7.4 %collective-permute-start.2 = (bf16[16,2176]{1,0:T(8,128)(2,1)S(1)}, bf16[16,2176]{1,0:T(8,128)(2,1)S(1)}, u32[]{:S(2)}, u32[]{:S(2)}) collective-permute-start(bf16[16,2176]{1,0:T(8,128)(2,1)S(1)} %get-tuple-element.26), channel_id=1, source_target_pairs={{0,1},{1,2},{2,3},{3,4},{4,5},{5,6},{6,7},{7,0},{8,9},{9,10},{10,1... | collective-permute-start | bytes 208904 | tf_op jit(solution)/shard_map/ppermute | solution.py:453
  21.3 18.7 %collective-permute-start.4 = (bf16[48,1024]{1,0:T(8,128)(2,1)S(1)}, bf16[48,1024]{1,0:T(8,128)(2,1)S(1)}, u32[]{:S(2)}, u32[]{:S(2)}) collective-permute-start(bf16[48,1024]{1,0:T(8,128)(2,1)S(1)} %get-tuple-element.31), channel_id=1, source_target_pairs={{0,504},{1,505},{2,506},{3,507},{4,508},{5,509},{6,510},{7,511},{8... | collective-permute-start | bytes 294920 | tf_op jit(solution)/shard_map/ppermute | solution.py:453
  29.5 9.4 %collective-permute-start.3 = (bf16[16,1024]{1,0:T(8,128)(2,1)S(1)}, bf16[16,1024]{1,0:T(8,128)(2,1)S(1)}, u32[]{:S(2)}, u32[]{:S(2)}) collective-permute-start(bf16[16,1024]{1,0:T(8,128)(2,1)S(1)} %get-tuple-element.30), channel_id=1, source_target_pairs={{0,7},{1,0},{2,1},{3,2},{4,3},{5,4},{6,5},{7,6},{8,15},{9,8},{10,9... | collective-permute-start | bytes 98312 | tf_op jit(solution)/shard_map/ppermute | solution.py:453
  31.8 8.2 %collective-permute-start.5 = (bf16[16,1024]{1,0:T(8,128)(2,1)S(1)}, bf16[16,1024]{1,0:T(8,128)(2,1)S(1)}, u32[]{:S(2)}, u32[]{:S(2)}) collective-permute-start(bf16[16,1024]{1,0:T(8,128)(2,1)S(1)} %get-tuple-element.32), channel_id=1, source_target_pairs={{0,511},{1,504},{2,505},{3,506},{4,507},{5,508},{6,509},{7,510},{8... | collective-permute-start | bytes 98312 | tf_op jit(solution)/shard_map/ppermute | solution.py:453

commit v12 on v3

--- a/solution.py
+++ b/solution.py
@@ -242,15 +242,12 @@
         cols = slice(256 * n, 256 * n + 256)
         qkv_s[:, cols] = mm(x_s[...], w_qkv[:, cols]).astype(bf16)
 
-    line, lane = iota((256, 128), 0), iota((256, 128), 1)
-    seg = onehot((line % 128) // 32 == lane // 32)
+    seg = onehot(iota((128, 128), 0) // 32 == iota((128, 128), 1) // 32)
     head_lane = iota((64, 128), 1) // 32
     head_mask = [onehot(head_lane == h) for h in range(4)]
 
-    def store_halves(n, value):
-        high, low = halves(value)
-        seg_s[count * n : count * n + count, 0:128] = high
-        seg_s[count * n : count * n + count, 128:256] = low
+    def store_terms(n, value):
+        seg_s[count * n : count * n + count, :] = value.astype(bf16)
 
     def block_diagonal(value):
         return jnp.concatenate([value * head_mask[h] for h in range(4)], axis=0)
@@ -263,7 +260,7 @@
 
     for n in range(8):
         raw = qkv_s[:, 128 * n : 128 * n + 128].astype(f32)
-        store_halves(n, raw * raw)
+        store_terms(n, raw * raw)
     squares = mm(seg_s[...], seg)
     for n in range(8):
         cols = slice(128 * n, 128 * n + 128)
@@ -302,9 +299,15 @@
         att = diagonal(mm_tn(prob16_s[rows, 256 * b : 256 * b + 256], vals))
         att_s[rows, 128 * b : 128 * b + 128] = att.astype(bf16)
 
+    total = jnp.zeros((count, 128), f32)
+    square = jnp.zeros((count, 128), f32)
     for n in range(4):
         cols = slice(256 * n, 256 * n + 256)
-        proj_s[:, cols] = mm(att_s[...], w_proj[:, cols])
+        part = mm(att_s[...], w_proj[:, cols])
+        proj_s[:, cols] = part
+        left, right = part[:, 0:128], part[:, 128:256]
+        total = total + left + right
+        square = square + left * left + right * right
 
     spans = [slice(16 * n, 16 * n + 16) for n in range(len(quads))]
 
@@ -314,26 +317,27 @@
 
     for s in range(4):
         mgain[4 * s : 4 * s + 4, :] = jnp.broadcast_to(merge[:, s * D : (s + 1) * D], (4, D))
-    mean = [row_total(proj_s[rows, :]) * (1.0 / D) for rows in spans]
-    inv_std = []
-    for n, rows in enumerate(spans):
-        centered = proj_s[rows, :] - mean[n]
-        inv_std.append(lax.rsqrt(row_total(centered * centered) * (1.0 / D) + norm_eps))
-    mean_m, mean_g = [], []
+    mean_p = row_total(total) * (1.0 / D)
+    var_p = row_total(square) * (1.0 / D) - mean_p * mean_p
+    inv_p = lax.rsqrt(jnp.maximum(var_p, 0.0) + norm_eps)
+    mean = [mean_p[rows] for rows in spans]
+    inv_std = [inv_p[rows] for rows in spans]
+    mean_m, mean_g, merge_inv, slope = [], [], [], []
     for n, rows in enumerate(spans):
         normed = (proj_s[rows, :] - mean[n]) * inv_std[n]
         proj_s[rows, :] = normed
         mixed = x_s[rows, :].astype(f32) + normed * gain[...] + shift[...]
         mixed_s[rows, :] = mixed
-        mean_m.append(group_total(row_total(mixed)) * (0.25 / D))
-        mean_g.append(group_total(row_total(ghat_of(n))) * (0.25 / D))
-    merge_inv, slope = [], []
-    for n, rows in enumerate(spans):
-        cent = mixed_s[rows, :] - mean_m[n]
         ghat = ghat_of(n)
-        inv = lax.rsqrt(group_total(row_total(cent * cent)) * (0.25 / D) + norm_eps)
+        mu = group_total(row_total(mixed)) * (0.25 / D)
+        mg = group_total(row_total(ghat)) * (0.25 / D)
+        mm2 = group_total(row_total(mixed * mixed)) * (0.25 / D)
+        mgm = group_total(row_total(ghat * mixed)) * (0.25 / D)
+        inv = lax.rsqrt(jnp.maximum(mm2 - mu * mu, 0.0) + norm_eps)
+        mean_m.append(mu)
+        mean_g.append(mg)
         merge_inv.append(inv)
-        slope.append(group_total(row_total(ghat * cent)) * (0.25 / D) * inv * inv)
+        slope.append((mgm - mg * mu) * inv * inv)
     mean_e, mean_en = [], []
     for n, rows in enumerate(spans):
         cent = mixed_s[rows, :] - mean_m[n]
@@ -373,7 +377,7 @@
         proj_s[rows, kcols] = gk
     for n in range(8):
         cols = slice(128 * n, 128 * n + 128)
-        store_halves(n, unit_s[:, cols] * proj_s[:, cols])
+        store_terms(n, unit_s[:, cols] * proj_s[:, cols])
     along = mm(seg_s[...], seg)
     for n in range(8):
         cols = slice(128 * n, 128 * n + 128)
@@ -393,7 +397,7 @@
         pltpu.VMEM((count, 2 * ATT), f32),
         pltpu.VMEM((count, 2 * ATT), f32),
         pltpu.VMEM((count, 2 * ATT), bf16),
-        pltpu.VMEM((8 * count, 256), bf16),
+        pltpu.VMEM((8 * count, 128), bf16),
         pltpu.VMEM((16 * count, 128), bf16),
         pltpu.VMEM((count, HEADS * CELLS), f32),
         pltpu.VMEM((count, HEADS * CELLS), bf16),

time: 41.7 us -> 41 us (0.983)
  Pallas kernels: 11.1 us -> 10.4 us
  transfers between devices with their start and end apart: 4 -> 4, of which waited for: 2 -> 2; matrix products, arithmetic and copies ran while one was open for 0% -> 0% of each run, Pallas kernels for 12% -> 11%
where the time goes in v12:
time: 41 us; the launch traced here: 40.8 us
  starting transfers between devices  24.3 us (59%)
  Pallas kernels  10.4 us (25%)
  waiting for transfers between devices  5.02 us (12%)
  local copies, waits for them, and re-layouts  0.88 us (2%)
    ppermute x4, starting transfers between devices, passed_along(): return lax.ppermute(block, axis, route)  24.3 us
    ppermute x4, waiting for transfers between devices, passed_along(): return lax.ppermute(block, axis, route)  5.02 us
    pallas_call x1, Pallas kernels, outer(): pl.pallas_call(outer_kernel, out_shape=[jax.ShapeDtypeStruct((64, D), bf1...  4.28 us
    pallas_call x1, Pallas kernels, inner(): pl.pallas_call(inner_kernel, out_shape=[jax.ShapeDtypeStruct((32, D), bf1...  3.87 us
    pallas_call x1, Pallas kernels, final(): pl.pallas_call(final_kernel, out_shape=jax.ShapeDtypeStruct((16, 8, D), b...  0.93 us
    unnamed x20, local copies, waits for them, and re-layouts  0.88 us
    pallas_call x1, Pallas kernels, prep(): pl.pallas_call(prep_kernel, out_shape=[jax.ShapeDtypeStruct((CELLS, HEADS...  0.82 us
  transfers between devices with their start and end apart: 4, of which 2 were waited for; matrix products, arithmetic and copies ran while one was open for 0% of the time, Pallas kernels for 11%

profile of v12, /device:TPU:1, one launch (start us, length us, event | category | flops | bytes accessed | tf_op | source)
XLA Modules:
  0.0 40.8 jit_solution(6035649639082757448)
XLA Ops:
  0.0 0.0 copy-start.3
  0.0 0.0 copy-start.6
  0.0 0.0 copy-start.2
  0.0 0.2 places.1
  0.2 0.7 %copy-done.3 = bf16[8,4,4096]{2,1,0:T(4,128)(2,1)S(1)} copy-done((bf16[8,4,4096]{2,1,0:T(4,128)(2,1)S(1)}, bf16[8,4,4096]{2,1,0:T(4,128)(2,1)}, u32[]{:S(2)}) %copy-start.3) | copy-done | bytes 262168
  1.0 0.0 copy-done.6
  1.0 0.1 copy-done.2
  1.0 0.0 copy-start.4
  1.0 0.0 copy-start.9
  1.1 0.0 copy-start
  1.1 0.0 copy-start.1
  1.1 0.0 copy-start.5
  1.1 0.0 copy-start.7
  1.1 0.0 copy-start.8
  1.1 0.3 pack.1
  1.4 5.2 %collective-permute-start = (bf16[64,2176]{1,0:T(8,128)(2,1)S(1)}, bf16[64,2176]{1,0:T(8,128)(2,1)S(1)}, u32[]{:S(2)}, u32[]{:S(2)}) collective-permute-start(bf16[64,2176]{1,0:T(8,128)(2,1)S(1)} %get-tuple-element.24), channel_id=1, source_target_pairs={{0,8},{8,16},{16,24},{24,32},{32,40},{40,48},{48,56},{56,64},{64,7... | collective-permute-start | bytes 835592 | tf_op jit(solution)/shard_map/ppermute | solution.py:496
  6.6 0.0 copy-done.4
  6.6 0.0 copy-done.9
  6.6 0.8 %prep.1 = (f32[64,1024]{1,0:T(8,128)S(1)}, f32[1,512]{1,0:T(1,128)S(1)}) custom-call(f32[16,225]{1,0:T(8,128)S(1)} %copy-done.4, f32[1,16]{1,0:T(1,128)S(1)} %bitcast.12), custom_call_target="tpu_custom_call" | custom-call | flops 100000000 | bytes 400000 | tf_op jit(solution)/shard_map/prep/pallas_call | solution.py:188
  7.5 4.0 %collective-permute-done.lon = bf16[64,2176]{1,0:T(8,128)(2,1)S(1)} collective-permute-done((bf16[64,2176]{1,0:T(8,128)(2,1)S(1)}, bf16[64,2176]{1,0:T(8,128)(2,1)S(1)}, u32[]{:S(2)}, u32[]{:S(2)}) %collective-permute-start) | collective-permute-done | bytes 278560 | tf_op jit(solution)/shard_map/ppermute | solution.py:496
  11.5 1.9 %collective-permute-start.1 = (bf16[32,2176]{1,0:T(8,128)(2,1)S(1)}, bf16[32,2176]{1,0:T(8,128)(2,1)S(1)}, u32[]{:S(2)}, u32[]{:S(2)}) collective-permute-start(bf16[32,2176]{1,0:T(8,128)(2,1)S(1)} %get-tuple-element.25), channel_id=1, source_target_pairs={{0,1},{1,2},{2,3},{3,4},{4,5},{5,6},{6,7},{7,0},{8,9},{9,10},{10,1... | collective-permute-start | bytes 417800 | tf_op jit(solution)/shard_map/ppermute | solution.py:496
  13.5 5.5 %collective-permute-start.2 = (bf16[32,2176]{1,0:T(8,128)(2,1)S(1)}, bf16[32,2176]{1,0:T(8,128)(2,1)S(1)}, u32[]{:S(2)}, u32[]{:S(2)}) collective-permute-start(bf16[32,2176]{1,0:T(8,128)(2,1)S(1)} %get-tuple-element.26), channel_id=1, source_target_pairs={{0,7},{1,0},{2,1},{3,2},{4,3},{5,4},{6,5},{7,6},{8,15},{9,8},{10,9... | collective-permute-start | bytes 417800 | tf_op jit(solution)/shard_map/ppermute | solution.py:496
  18.9 0.0 copy-done
  19.0 0.0 copy-done.1
  19.0 0.0 copy-done.5
  19.0 0.0 copy-done.7
  19.0 0.0 copy-done.8
  19.0 3.9 %inner.1 = (bf16[32,1024]{1,0:T(8,128)(2,1)S(1)}, bf16[32,1024]{1,0:T(8,128)(2,1)S(1)}) custom-call(bf16[64,2176]{1,0:T(8,128)(2,1)S(1)} %get-tuple-element.23.own, bf16[64,2176]{1,0:T(8,128)(2,1)S(1)} %collective-permute-done.lon, f32[64,1024]{1,0:T(8,128)S(1)} %get-tuple-element.27.refs_0_, f32[1,512]{1,0:T(1,128)S(1)} %get-tuple-element.28.refs_1_, ...), custom_call_target="tpu_custom_call" | custom-call | flops 3000000000 | bytes 6000000 | tf_op jit(solution)/shard_map/inner/pallas_call | solution.py:428
  22.9 0.0 collective-permute-done.1.above
  22.9 0.0 collective-permute-done.2.below
  22.9 4.3 %outer.1 = (bf16[64,1024]{1,0:T(8,128)(2,1)S(1)}, bf16[64,1024]{1,0:T(8,128)(2,1)S(1)}) custom-call(bf16[64,2176]{1,0:T(8,128)(2,1)S(1)} %get-tuple-element.23.own, bf16[64,2176]{1,0:T(8,128)(2,1)S(1)} %collective-permute-done.lon, bf16[32,2176]{1,0:T(8,128)(2,1)S(1)} %collective-permute-done.1.above, bf16[32,2176]{1,0:T(8,128)(2,1)S(1)} %collective-permute-done.2.below, ...), custom_call_target="tpu_custom_call" | custom-call | flops 3000000000 | bytes 6000000 | tf_op jit(solution)/shard_map/outer/pallas_call | solution.py:465
  27.2 11.8 %collective-permute-start.3 = (bf16[64,1024]{1,0:T(8,128)(2,1)S(1)}, bf16[64,1024]{1,0:T(8,128)(2,1)S(1)}, u32[]{:S(2)}, u32[]{:S(2)}) collective-permute-start(bf16[64,1024]{1,0:T(8,128)(2,1)S(1)} %get-tuple-element.32), channel_id=1, source_target_pairs={{0,504},{8,0},{16,8},{24,16},{32,24},{40,32},{48,40},{56,48},{64,5... | collective-permute-start | bytes 393224 | tf_op jit(solution)/shard_map/ppermute | solution.py:496
  38.9 1.0 %collective-permute-done.3.lon = bf16[64,1024]{1,0:T(8,128)(2,1)S(1)} collective-permute-done((bf16[64,1024]{1,0:T(8,128)(2,1)S(1)}, bf16[64,1024]{1,0:T(8,128)(2,1)S(1)}, u32[]{:S(2)}, u32[]{:S(2)}) %collective-permute-start.3) | collective-permute-done | bytes 131104 | tf_op jit(solution)/shard_map/ppermute | solution.py:496
  39.9 0.9 %final.1 = bf16[16,8,1024]{2,1,0:T(8,128)(2,1)} custom-call(bf16[64,1024]{1,0:T(8,128)(2,1)S(1)} %get-tuple-element.31.own, bf16[64,1024]{1,0:T(8,128)(2,1)S(1)} %collective-permute-done.3.lon), custom_call_target="tpu_custom_call" | custom-call | tf_op jit(solution)/shard_map/final/pallas_call | solution.py:485
  (1 shorter events, 0.0 us)
Async XLA Ops:
  0.0 0.9 %copy-start.3 = (bf16[8,4,4096]{2,1,0:T(4,128)(2,1)S(1)}, bf16[8,4,4096]{2,1,0:T(4,128)(2,1)}, u32[]{:S(2)}) copy-start(bf16[8,4,4096]{2,1,0:T(4,128)(2,1)} %cot.1) | copy-start | bytes 786436
  0.0 1.0 %copy-start.6 = (s32[16,8]{0,1:T(8,128)S(1)}, s32[16,8]{0,1:T(8,128)}, u32[]{:S(2)}) copy-start(s32[16,8]{0,1:T(8,128)} %param.11) | copy-start | bytes 1540
  0.0 1.0 %copy-start.2 = (bf16[16,8,1024]{2,1,0:T(8,128)(2,1)S(1)}, bf16[16,8,1024]{2,1,0:T(8,128)(2,1)}, u32[]{:S(2)}) copy-start(bf16[16,8,1024]{2,1,0:T(8,128)(2,1)} %tokens.1) | copy-start | bytes 786436
  1.0 5.6 %copy-start.4 = (f32[16,225]{1,0:T(8,128)S(1)}, f32[16,225]{1,0:T(8,128)}, u32[]{:S(2)}) copy-start(f32[16,225]{1,0:T(8,128)} %table.1) | copy-start | bytes 43204
  1.0 5.6 %copy-start.9 = (f32[16]{0:T(128)S(1)}, f32[16]{0:T(128)}, u32[]{:S(2)}) copy-start(f32[16]{0:T(128)} %param.14) | copy-start | bytes 196
  1.1 17.9 %copy-start = (bf16[1024,1536]{1,0:T(8,128)(2,1)S(1)}, bf16[1024,1536]{1,0:T(8,128)(2,1)}, u32[]{:S(2)}) copy-start(bf16[1024,1536]{1,0:T(8,128)(2,1)} %refs_2_.3) | copy-start | bytes 9437188
  1.1 17.9 %copy-start.1 = (bf16[512,1024]{1,0:T(8,128)(2,1)S(1)}, bf16[512,1024]{1,0:T(8,128)(2,1)}, u32[]{:S(2)}) copy-start(bf16[512,1024]{1,0:T(8,128)(2,1)} %refs_3_.3) | copy-start | bytes 3145732
  1.1 17.9 %copy-start.5 = (f32[4096]{0:T(1024)S(1)}, f32[4096]{0:T(1024)}, u32[]{:S(2)}) copy-start(f32[4096]{0:T(1024)} %param.18) | copy-start | bytes 49156
  1.1 17.9 %copy-start.7 = (f32[1024]{0:T(1024)S(1)}, f32[1024]{0:T(1024)}, u32[]{:S(2)}) copy-start(f32[1024]{0:T(1024)} %param.16) | copy-start | bytes 12292
  1.1 17.9 %copy-start.8 = (f32[1024]{0:T(1024)S(1)}, f32[1024]{0:T(1024)}, u32[]{:S(2)}) copy-start(f32[1024]{0:T(1024)} %param.17) | copy-start | bytes 12292
  1.4 10.1 %collective-permute-start = (bf16[64,2176]{1,0:T(8,128)(2,1)S(1)}, bf16[64,2176]{1,0:T(8,128)(2,1)S(1)}, u32[]{:S(2)}, u32[]{:S(2)}) collective-permute-start(bf16[64,2176]{1,0:T(8,128)(2,1)S(1)} %get-tuple-element.24), channel_id=1, source_target_pairs={{0,8},{8,16},{16,24},{24,32},{32,40},{40,48},{48,56},{56,64},{64,7... | collective-permute-start | bytes 835592 | tf_op jit(solution)/shard_map/ppermute | solution.py:496
  11.5 11.3 %collective-permute-start.1 = (bf16[32,2176]{1,0:T(8,128)(2,1)S(1)}, bf16[32,2176]{1,0:T(8,128)(2,1)S(1)}, u32[]{:S(2)}, u32[]{:S(2)}) collective-permute-start(bf16[32,2176]{1,0:T(8,128)(2,1)S(1)} %get-tuple-element.25), channel_id=1, source_target_pairs={{0,1},{1,2},{2,3},{3,4},{4,5},{5,6},{6,7},{7,0},{8,9},{9,10},{10,1... | collective-permute-start | bytes 417800 | tf_op jit(solution)/shard_map/ppermute | solution.py:496
  13.5 9.4 %collective-permute-start.2 = (bf16[32,2176]{1,0:T(8,128)(2,1)S(1)}, bf16[32,2176]{1,0:T(8,128)(2,1)S(1)}, u32[]{:S(2)}, u32[]{:S(2)}) collective-permute-start(bf16[32,2176]{1,0:T(8,128)(2,1)S(1)} %get-tuple-element.26), channel_id=1, source_target_pairs={{0,7},{1,0},{2,1},{3,2},{4,3},{5,4},{6,5},{7,6},{8,15},{9,8},{10,9... | collective-permute-start | bytes 417800 | tf_op jit(solution)/shard_map/ppermute | solution.py:496
  27.2 12.7 %collective-permute-start.3 = (bf16[64,1024]{1,0:T(8,128)(2,1)S(1)}, bf16[64,1024]{1,0:T(8,128)(2,1)S(1)}, u32[]{:S(2)}, u32[]{:S(2)}) collective-permute-start(bf16[64,1024]{1,0:T(8,128)(2,1)S(1)} %get-tuple-element.32), channel_id=1, source_target_pairs={{0,504},{8,0},{16,8},{24,16},{32,24},{40,32},{48,40},{56,48},{64,5... | collective-permute-start | bytes 393224 | tf_op jit(solution)/shard_map/ppermute | solution.py:496
